TPU v7x, 128 devices: a whole 4x4x4 slice. The times are simulated.
128 devices in a mesh: band: 16 (over z, x), space: 8 (over y, core).
Axes of the slice: x: 4, y: 4, z: 4, core: 2. Of those that a mesh axis runs over, the one named last changes fastest.
Arguments:
- orbitals: bfloat16 [128, 128, 320, 128], P('band', None, 'space'), may hold values from -8.5 to 8.5
- occupations: float32 [128], P('band'), may hold values from 0.07 to 2.5
Outputs:
- potential: float32 [128, 320, 128], P('band', 'space')
All inputs are finite; a program needn't handle non-finite values.
Results may differ from a plain program's by a relative error of at most 0.0003.
Values sent between devices are 32-bit elements; how exact they have to be, the bound alone decides.
No kernel may reach another device: no remote copies, remote signals or barrier semaphores. Data moves between devices by JAX's collectives and lax.ppermute only.
A program may use at most 64 MiB of HBM per device.

v0:
```python
import functools
import math

import jax
import jax.numpy as jnp
from jax import lax
from jax.sharding import Mesh
from jax.sharding import PartitionSpec as P

ITERS = 3
BAND_SPACE = ("band_0", "band_1", "space_0", "space_1")
BAND = ("band_0", "band_1")
SPACE = ("space_0", "space_1")


four_pi = 4.0 * math.pi


def padded_2(shard, sides, width):
    edges = {}
    for axis, dim in sides:
        peers, length = (lax.axis_size(axis), shard.shape[dim])
        up = [(i, (i + 1) % peers) for i in range(peers - 1)]
        last = lax.slice_in_dim(shard, length - width, length, axis=dim)
        first = lax.slice_in_dim(shard, 0, width, axis=dim)
        edges[dim] = (
            lax.ppermute(last, axis, up),
            lax.ppermute(first, axis, [(b, a) for a, b in up]),
        )
    done = []
    for _, dim in sides:
        low, high = edges[dim]
        around = [(width, width) if d in done else (0, 0) for d in range(shard.ndim)]
        shard = jnp.concatenate([jnp.pad(low, around), shard, jnp.pad(high, around)], axis=dim)
        done.append(dim)
    return shard


def one_axis_at_a_time(shard, axes):
    return functools.reduce(lax.psum, axes, shard)


def cut_along(shard, dim, peers):
    before, after = (shard.shape[:dim], shard.shape[dim + 1 :])
    return jnp.moveaxis(shard.reshape(*before, peers, -1, *after), dim, 0)


def sum_at_owner(shard, axis, dim):
    blocks = cut_along(shard, dim, lax.axis_size(axis))
    arrived = lax.all_to_all(blocks, axis, split_axis=0, concat_axis=0, tiled=True)
    return arrived.sum(axis=0)


def stencil(padded):
    center = padded[2:-2, 2:-2, 2:-2]
    near = padded[3:-1, 2:-2, 2:-2] + padded[1:-3, 2:-2, 2:-2]
    near = near + padded[2:-2, 3:-1, 2:-2] + padded[2:-2, 1:-3, 2:-2]
    near = near + padded[2:-2, 2:-2, 3:-1] + padded[2:-2, 2:-2, 1:-3]
    distant = padded[4:, 2:-2, 2:-2] + padded[:-4, 2:-2, 2:-2]
    distant = distant + padded[2:-2, 4:, 2:-2] + padded[2:-2, :-4, 2:-2]
    distant = distant + padded[2:-2, 2:-2, 4:] + padded[2:-2, 2:-2, :-4]
    return 7.5 * center - 4.0 / 3.0 * near + 1.0 / 12.0 * distant


def operate(field):
    widened = padded_2(field, ((BAND, 0), (SPACE, 1)), 2)
    return stencil(jnp.pad(widened, ((0, 0), (0, 0), (2, 2))))


def paired_sums(residual, image):
    return (
        one_axis_at_a_time(jnp.sum(residual * residual), BAND_SPACE),
        one_axis_at_a_time(jnp.sum(residual * image), BAND_SPACE),
    )


def local(orbitals, occupations):

    def accumulate(index, total):
        wave = lax.dynamic_index_in_dim(orbitals, index, 0, keepdims=False).astype(jnp.float32)
        return total + occupations[index] * wave * wave

    start = jnp.zeros(orbitals.shape[1:], jnp.float32)
    partial_value = lax.fori_loop(0, orbitals.shape[0], accumulate, start)
    groups = lax.axis_size(BAND)
    mine = sum_at_owner(partial_value, BAND, 0)
    density = mine / (orbitals.shape[0] * groups)
    source = four_pi * density
    potential = jnp.zeros_like(source)
    residual = source
    image = operate(residual)
    norm_now, product = paired_sums(residual, image)
    alpha = norm_now / product
    direction, along = (residual, image)
    for step in range(ITERS):
        potential = potential + alpha * direction
        residual = residual - alpha * along
        if step + 1 < ITERS:
            image = operate(residual)
            norm_next, product = paired_sums(residual, image)
            ratio = norm_next / norm_now
            alpha = norm_next / (product - ratio * norm_next / alpha)
            direction = residual + ratio * direction
            along = image + ratio * along
            norm_now = norm_next
    return potential


def solution(mesh):
    split = Mesh(mesh.devices.reshape(4, 4, 4, 2), ("band_0", "band_1", "space_0", "space_1"))
    in_specs = (P(BAND, None, SPACE, None), P(BAND))
    out_specs = P(BAND, SPACE, None)
    return jax.shard_map(local, mesh=split, in_specs=in_specs, out_specs=out_specs, check_vma=False)
```

profile of v0, /device:TPU:1, one launch (start us, length us, event | category | flops | bytes accessed | tf_op | source)
XLA Modules:
  0.0 233.3 jit_solution(7428009627507512081)
XLA Ops:
  0.0 38.7 %while.14 = (s32[]{:T(128)}, f32[128,40,128]{2,1,0:T(8,128)S(1)}, f32[8]{0:T(128)}, bf16[8,128,40,128]{3,2,1,0:T(8,128)(2,1)}, s32[]{:T(128)}, /*index=5*/s32[]{:T(128)}) while((s32[]{:T(128)}, f32[128,40,128]{2,1,0:T(8,128)S(1)}, f32[8]{0:T(128)}, bf16[8,128,40,128]{3,2,1,0:T(8,128)(2,1)}, s32[]{:T(128)}, ...), condition=%wide.region_1.2_spmd.clone, body=%wide.region_0.1_spmd.clone.sunk | while | flops 3276803 | bytes 6553707 | solution.py:84
  1.3 3.5 %fusion.49 = f32[128,40,128]{2,1,0:T(8,128)S(1)} fusion(f32[128,40,128]{2,1,0:T(8,128)S(1)} %get-tuple-element.190, bf16[8,128,40,128]{3,2,1,0:T(8,128)(2,1)} %get-tuple-element.198, s32[]{:T(128)S(6)} %copy.5, f32[]{:T(128)} %bitcast.8, pred[]{:T(512)S(6)} %compare.60), kind=kLoop, calls=%fused_computation.1.clone.1 | loop fusion | flops 3276800 | bytes 6553609 | tf_op jit(solution)/shard_map/while/body/eval_jaxpr/add | solution.py:81
  6.2 3.5 %fusion.49 = f32[128,40,128]{2,1,0:T(8,128)S(1)} fusion(f32[128,40,128]{2,1,0:T(8,128)S(1)} %get-tuple-element.190, bf16[8,128,40,128]{3,2,1,0:T(8,128)(2,1)} %get-tuple-element.198, s32[]{:T(128)S(6)} %copy.5, f32[]{:T(128)} %bitcast.8, pred[]{:T(512)S(6)} %compare.60), kind=kLoop, calls=%fused_computation.1.clone.1 | loop fusion | flops 3276800 | bytes 6553609 | tf_op jit(solution)/shard_map/while/body/eval_jaxpr/add | solution.py:81
  11.0 3.5 %fusion.49 = f32[128,40,128]{2,1,0:T(8,128)S(1)} fusion(f32[128,40,128]{2,1,0:T(8,128)S(1)} %get-tuple-element.190, bf16[8,128,40,128]{3,2,1,0:T(8,128)(2,1)} %get-tuple-element.198, s32[]{:T(128)S(6)} %copy.5, f32[]{:T(128)} %bitcast.8, pred[]{:T(512)S(6)} %compare.60), kind=kLoop, calls=%fused_computation.1.clone.1 | loop fusion | flops 3276800 | bytes 6553609 | tf_op jit(solution)/shard_map/while/body/eval_jaxpr/add | solution.py:81
  15.8 3.5 %fusion.49 = f32[128,40,128]{2,1,0:T(8,128)S(1)} fusion(f32[128,40,128]{2,1,0:T(8,128)S(1)} %get-tuple-element.190, bf16[8,128,40,128]{3,2,1,0:T(8,128)(2,1)} %get-tuple-element.198, s32[]{:T(128)S(6)} %copy.5, f32[]{:T(128)} %bitcast.8, pred[]{:T(512)S(6)} %compare.60), kind=kLoop, calls=%fused_computation.1.clone.1 | loop fusion | flops 3276800 | bytes 6553609 | tf_op jit(solution)/shard_map/while/body/eval_jaxpr/add | solution.py:81
  20.7 3.5 %fusion.49 = f32[128,40,128]{2,1,0:T(8,128)S(1)} fusion(f32[128,40,128]{2,1,0:T(8,128)S(1)} %get-tuple-element.190, bf16[8,128,40,128]{3,2,1,0:T(8,128)(2,1)} %get-tuple-element.198, s32[]{:T(128)S(6)} %copy.5, f32[]{:T(128)} %bitcast.8, pred[]{:T(512)S(6)} %compare.60), kind=kLoop, calls=%fused_computation.1.clone.1 | loop fusion | flops 3276800 | bytes 6553609 | tf_op jit(solution)/shard_map/while/body/eval_jaxpr/add | solution.py:81
  25.5 3.5 %fusion.49 = f32[128,40,128]{2,1,0:T(8,128)S(1)} fusion(f32[128,40,128]{2,1,0:T(8,128)S(1)} %get-tuple-element.190, bf16[8,128,40,128]{3,2,1,0:T(8,128)(2,1)} %get-tuple-element.198, s32[]{:T(128)S(6)} %copy.5, f32[]{:T(128)} %bitcast.8, pred[]{:T(512)S(6)} %compare.60), kind=kLoop, calls=%fused_computation.1.clone.1 | loop fusion | flops 3276800 | bytes 6553609 | tf_op jit(solution)/shard_map/while/body/eval_jaxpr/add | solution.py:81
  30.3 3.5 %fusion.49 = f32[128,40,128]{2,1,0:T(8,128)S(1)} fusion(f32[128,40,128]{2,1,0:T(8,128)S(1)} %get-tuple-element.190, bf16[8,128,40,128]{3,2,1,0:T(8,128)(2,1)} %get-tuple-element.198, s32[]{:T(128)S(6)} %copy.5, f32[]{:T(128)} %bitcast.8, pred[]{:T(512)S(6)} %compare.60), kind=kLoop, calls=%fused_computation.1.clone.1 | loop fusion | flops 3276800 | bytes 6553609 | tf_op jit(solution)/shard_map/while/body/eval_jaxpr/add | solution.py:81
  35.2 3.5 %fusion.49 = f32[128,40,128]{2,1,0:T(8,128)S(1)} fusion(f32[128,40,128]{2,1,0:T(8,128)S(1)} %get-tuple-element.190, bf16[8,128,40,128]{3,2,1,0:T(8,128)(2,1)} %get-tuple-element.198, s32[]{:T(128)S(6)} %copy.5, f32[]{:T(128)} %bitcast.8, pred[]{:T(512)S(6)} %compare.60), kind=kLoop, calls=%fused_computation.1.clone.1 | loop fusion | flops 3276800 | bytes 6553609 | tf_op jit(solution)/shard_map/while/body/eval_jaxpr/add | solution.py:81
  38.7 41.3 %all_to_all.5 = f32[16,8,40,128]{3,2,1,0:T(8,128)} all-to-all(f32[16,8,40,128]{3,2,1,0:T(8,128)S(1)} %bitcast.9), channel_id=1, replica_groups=mesh['band_0'=4,'band_1'=4,'space_0'=4,'space_1'=2] {'band_0','band_1'}, dimensions={0} | all-to-all | bytes 5242880 | tf_op jit(solution)/shard_map/all_to_all | solution.py:50
  81.9 2.1 collective-permute-start.1
  85.4 5.4 %collective-permute-start.3 = (f32[8,2,128]{2,1,0:T(2,128)S(1)}, f32[8,2,128]{2,1,0:T(2,128)S(1)}, u32[]{:S(2)}, u32[]{:S(2)}) collective-permute-start(f32[8,2,128]{2,1,0:T(2,128)S(1)} %get-tuple-element.156), channel_id=1, source_target_pairs={{0,1},{1,2},{2,3},{3,4},{4,5},{5,6},{6,7},{8,9},{9,10},{10,11},{11... | collective-permute-start | bytes 24584 | tf_op jit(solution)/shard_map/ppermute | solution.py:27
  90.8 1.9 collective-permute-start.2
  92.8 3.0 %collective-permute-done.2 = f32[8,2,128]{2,1,0:T(2,128)S(1)} collective-permute-done((f32[8,2,128]{2,1,0:T(2,128)S(1)}, f32[8,2,128]{2,1,0:T(2,128)S(1)}, u32[]{:S(2)}, u32[]{:S(2)}) %collective-permute-start.2) | collective-permute-done | bytes 8224 | tf_op jit(solution)/shard_map/ppermute | solution.py:28
  97.0 11.4 %all-reduce.17 = (f32[]{:T(128)}, f32[]{:T(128)}) all-reduce(f32[]{:T(128)} %get-tuple-element.105, f32[]{:T(128)} %get-tuple-element.104), channel_id=1, replica_groups=mesh['band_0'=4,'band_1'=4,'space_0'=4,'space_1'=2] {'band_0'}, use_global_device_ids=true, to_apply=%region_4.5 | all-reduce | flops 2 | bytes 16 | tf_op jit(solution)/shard_map/psum | solution.py:40
  108.4 6.6 %all-reduce.14 = (f32[]{:T(128)}, f32[]{:T(128)}) all-reduce(f32[]{:T(128)} %get-tuple-element.130, f32[]{:T(128)} %get-tuple-element.131), channel_id=1, replica_groups=mesh['band_0'=4,'band_1'=4,'space_0'=4,'space_1'=2] {'band_1'}, use_global_device_ids=true, to_apply=%region_5.6 | all-reduce | flops 2 | bytes 16 | tf_op jit(solution)/shard_map/psum | solution.py:40
  115.0 7.9 %all-reduce.11 = (f32[]{:T(128)}, f32[]{:T(128)}) all-reduce(f32[]{:T(128)} %get-tuple-element.124, f32[]{:T(128)} %get-tuple-element.125), channel_id=1, replica_groups=mesh['band_0'=4,'band_1'=4,'space_0'=4,'space_1'=2] {'space_0'}, use_global_device_ids=true, to_apply=%region_6.7 | all-reduce | flops 2 | bytes 16 | tf_op jit(solution)/shard_map/psum | solution.py:40
  123.0 8.9 %all-reduce.20 = (f32[]{:T(128)}, f32[]{:T(128)}) all-reduce(f32[]{:T(128)} %get-tuple-element.118, f32[]{:T(128)} %get-tuple-element.119), channel_id=1, replica_groups=mesh['band_0'=4,'band_1'=4,'space_0'=4,'space_1'=2] {'space_1'}, use_global_device_ids=true, to_apply=%region_7.8 | all-reduce | flops 2 | bytes 16 | tf_op jit(solution)/shard_map/psum | solution.py:40
  133.3 3.6 %collective-permute-start.5 = (f32[2,40,128]{2,1,0:T(8,128)S(1)}, f32[2,40,128]{2,1,0:T(8,128)S(1)}, u32[]{:S(2)}, u32[]{:S(2)}) collective-permute-start(f32[2,40,128]{2,1,0:T(8,128)S(1)} %get-tuple-element.150), channel_id=1, source_target_pairs={{0,8},{8,16},{16,24},{24,32},{32,40},{40,48},{48,56},{56,64},{64,7... | collective-permute-start | bytes 122888 | tf_op jit(solution)/shard_map/ppermute | solution.py:27
  140.2 2.4 %collective-permute-start.6 = (f32[8,2,128]{2,1,0:T(2,128)S(1)}, f32[8,2,128]{2,1,0:T(2,128)S(1)}, u32[]{:S(2)}, u32[]{:S(2)}) collective-permute-start(f32[8,2,128]{2,1,0:T(2,128)S(1)} %get-tuple-element.153), channel_id=1, source_target_pairs={{1,0},{2,1},{3,2},{4,3},{5,4},{6,5},{7,6},{9,8},{10,9},{11,10},{12... | collective-permute-start | bytes 24584 | tf_op jit(solution)/shard_map/ppermute | solution.py:28
  142.6 2.5 %collective-permute-done.6 = f32[8,2,128]{2,1,0:T(2,128)S(1)} collective-permute-done((f32[8,2,128]{2,1,0:T(2,128)S(1)}, f32[8,2,128]{2,1,0:T(2,128)S(1)}, u32[]{:S(2)}, u32[]{:S(2)}) %collective-permute-start.6) | collective-permute-done | bytes 8224 | tf_op jit(solution)/shard_map/ppermute | solution.py:28
  146.4 8.8 %all-reduce.16 = (f32[]{:T(128)}, f32[]{:T(128)}) all-reduce(f32[]{:T(128)} %get-tuple-element.103, f32[]{:T(128)} %get-tuple-element.102), channel_id=1, replica_groups=mesh['band_0'=4,'band_1'=4,'space_0'=4,'space_1'=2] {'band_0'}, use_global_device_ids=true, to_apply=%region_14.15 | all-reduce | flops 2 | bytes 16 | tf_op jit(solution)/shard_map/psum | solution.py:40
  155.2 6.8 %all-reduce.13 = (f32[]{:T(128)}, f32[]{:T(128)}) all-reduce(f32[]{:T(128)} %get-tuple-element.128, f32[]{:T(128)} %get-tuple-element.129), channel_id=1, replica_groups=mesh['band_0'=4,'band_1'=4,'space_0'=4,'space_1'=2] {'band_1'}, use_global_device_ids=true, to_apply=%region_15.16 | all-reduce | flops 2 | bytes 16 | tf_op jit(solution)/shard_map/psum | solution.py:40
  162.0 7.5 %all-reduce.10 = (f32[]{:T(128)}, f32[]{:T(128)}) all-reduce(f32[]{:T(128)} %get-tuple-element.122, f32[]{:T(128)} %get-tuple-element.123), channel_id=1, replica_groups=mesh['band_0'=4,'band_1'=4,'space_0'=4,'space_1'=2] {'space_0'}, use_global_device_ids=true, to_apply=%region_16.17 | all-reduce | flops 2 | bytes 16 | tf_op jit(solution)/shard_map/psum | solution.py:40
  169.4 7.9 %all-reduce.19 = (f32[]{:T(128)}, f32[]{:T(128)}) all-reduce(f32[]{:T(128)} %get-tuple-element.116, f32[]{:T(128)} %get-tuple-element.117), channel_id=1, replica_groups=mesh['band_0'=4,'band_1'=4,'space_0'=4,'space_1'=2] {'space_1'}, use_global_device_ids=true, to_apply=%region_17.18 | all-reduce | flops 2 | bytes 16 | tf_op jit(solution)/shard_map/psum | solution.py:40
  181.9 3.5 %collective-permute-start.9 = (f32[2,40,128]{2,1,0:T(8,128)S(1)}, f32[2,40,128]{2,1,0:T(8,128)S(1)}, u32[]{:S(2)}, u32[]{:S(2)}) collective-permute-start(f32[2,40,128]{2,1,0:T(8,128)S(1)} %get-tuple-element.146), channel_id=1, source_target_pairs={{0,8},{8,16},{16,24},{24,32},{32,40},{40,48},{48,56},{56,64},{64,7... | collective-permute-start | bytes 122888 | tf_op jit(solution)/shard_map/ppermute | solution.py:27
  186.7 2.6 %collective-permute-start.11 = (f32[8,2,128]{2,1,0:T(2,128)S(1)}, f32[8,2,128]{2,1,0:T(2,128)S(1)}, u32[]{:S(2)}, u32[]{:S(2)}) collective-permute-start(f32[8,2,128]{2,1,0:T(2,128)S(1)} %get-tuple-element.148), channel_id=1, source_target_pairs={{0,1},{1,2},{2,3},{3,4},{4,5},{5,6},{6,7},{8,9},{9,10},{10,11},{11... | collective-permute-start | bytes 24584 | tf_op jit(solution)/shard_map/ppermute | solution.py:27
  191.2 3.0 %collective-permute-done.10 = f32[8,2,128]{2,1,0:T(2,128)S(1)} collective-permute-done((f32[8,2,128]{2,1,0:T(2,128)S(1)}, f32[8,2,128]{2,1,0:T(2,128)S(1)}, u32[]{:S(2)}, u32[]{:S(2)}) %collective-permute-start.10) | collective-permute-done | bytes 8224 | tf_op jit(solution)/shard_map/ppermute | solution.py:28
  195.5 11.3 %all-reduce.15 = (f32[]{:T(128)}, f32[]{:T(128)}) all-reduce(f32[]{:T(128)} %get-tuple-element.101, f32[]{:T(128)} %get-tuple-element.100), channel_id=1, replica_groups=mesh['band_0'=4,'band_1'=4,'space_0'=4,'space_1'=2] {'band_0'}, use_global_device_ids=true, to_apply=%region_24.25 | all-reduce | flops 2 | bytes 16 | tf_op jit(solution)/shard_map/psum | solution.py:40
  206.8 6.6 %all-reduce.12 = (f32[]{:T(128)}, f32[]{:T(128)}) all-reduce(f32[]{:T(128)} %get-tuple-element.126, f32[]{:T(128)} %get-tuple-element.127), channel_id=1, replica_groups=mesh['band_0'=4,'band_1'=4,'space_0'=4,'space_1'=2] {'band_1'}, use_global_device_ids=true, to_apply=%region_25.26 | all-reduce | flops 2 | bytes 16 | tf_op jit(solution)/shard_map/psum | solution.py:40
  213.4 6.8 %all-reduce.9 = (f32[]{:T(128)}, f32[]{:T(128)}) all-reduce(f32[]{:T(128)} %get-tuple-element.120, f32[]{:T(128)} %get-tuple-element.121), channel_id=1, replica_groups=mesh['band_0'=4,'band_1'=4,'space_0'=4,'space_1'=2] {'space_0'}, use_global_device_ids=true, to_apply=%region_26.27 | all-reduce | flops 2 | bytes 16 | tf_op jit(solution)/shard_map/psum | solution.py:40
  220.2 8.6 %all-reduce.18 = (f32[]{:T(128)}, f32[]{:T(128)}) all-reduce(f32[]{:T(128)} %get-tuple-element.114, f32[]{:T(128)} %get-tuple-element.115), channel_id=1, replica_groups=mesh['band_0'=4,'band_1'=4,'space_0'=4,'space_1'=2] {'space_1'}, use_global_device_ids=true, to_apply=%region_27.28 | all-reduce | flops 2 | bytes 16 | tf_op jit(solution)/shard_map/psum | solution.py:40
  (49 shorter events, 24.7 us)
Async XLA Ops:
  81.9 13.9 %collective-permute-start.1 = (f32[2,40,128]{2,1,0:T(8,128)S(1)}, f32[2,40,128]{2,1,0:T(8,128)S(1)}, u32[]{:S(2)}, u32[]{:S(2)}) collective-permute-start(f32[2,40,128]{2,1,0:T(8,128)S(1)} %get-tuple-element.154), channel_id=1, source_target_pairs={{0,8},{8,16},{16,24},{24,32},{32,40},{40,48},{48,56},{56,64},{64,7... | collective-permute-start | bytes 122888 | tf_op jit(solution)/shard_map/ppermute | solution.py:27
  84.1 11.7 %collective-permute-start = (f32[2,40,128]{2,1,0:T(8,128)S(1)}, f32[2,40,128]{2,1,0:T(8,128)S(1)}, u32[]{:S(2)}, u32[]{:S(2)}) collective-permute-start(f32[2,40,128]{2,1,0:T(8,128)S(1)} %get-tuple-element.155), channel_id=1, source_target_pairs={{8,0},{16,8},{24,16},{32,24},{40,32},{48,40},{56,48},{64,56},{72,6... | collective-permute-start | bytes 122888 | tf_op jit(solution)/shard_map/ppermute | solution.py:28
  85.4 7.3 %collective-permute-start.3 = (f32[8,2,128]{2,1,0:T(2,128)S(1)}, f32[8,2,128]{2,1,0:T(2,128)S(1)}, u32[]{:S(2)}, u32[]{:S(2)}) collective-permute-start(f32[8,2,128]{2,1,0:T(2,128)S(1)} %get-tuple-element.156), channel_id=1, source_target_pairs={{0,1},{1,2},{2,3},{3,4},{4,5},{5,6},{6,7},{8,9},{9,10},{10,11},{11... | collective-permute-start | bytes 24584 | tf_op jit(solution)/shard_map/ppermute | solution.py:27
  90.8 5.0 %collective-permute-start.2 = (f32[8,2,128]{2,1,0:T(2,128)S(1)}, f32[8,2,128]{2,1,0:T(2,128)S(1)}, u32[]{:S(2)}, u32[]{:S(2)}) collective-permute-start(f32[8,2,128]{2,1,0:T(2,128)S(1)} %get-tuple-element.157), channel_id=1, source_target_pairs={{1,0},{2,1},{3,2},{4,3},{5,4},{6,5},{7,6},{9,8},{10,9},{11,10},{12... | collective-permute-start | bytes 24584 | tf_op jit(solution)/shard_map/ppermute | solution.py:28
  133.3 11.9 %collective-permute-start.5 = (f32[2,40,128]{2,1,0:T(8,128)S(1)}, f32[2,40,128]{2,1,0:T(8,128)S(1)}, u32[]{:S(2)}, u32[]{:S(2)}) collective-permute-start(f32[2,40,128]{2,1,0:T(8,128)S(1)} %get-tuple-element.150), channel_id=1, source_target_pairs={{0,8},{8,16},{16,24},{24,32},{32,40},{40,48},{48,56},{56,64},{64,7... | collective-permute-start | bytes 122888 | tf_op jit(solution)/shard_map/ppermute | solution.py:27
  136.9 8.2 %collective-permute-start.4 = (f32[2,40,128]{2,1,0:T(8,128)S(1)}, f32[2,40,128]{2,1,0:T(8,128)S(1)}, u32[]{:S(2)}, u32[]{:S(2)}) collective-permute-start(f32[2,40,128]{2,1,0:T(8,128)S(1)} %get-tuple-element.151), channel_id=1, source_target_pairs={{8,0},{16,8},{24,16},{32,24},{40,32},{48,40},{56,48},{64,56},{72,6... | collective-permute-start | bytes 122888 | tf_op jit(solution)/shard_map/ppermute | solution.py:28
  138.2 4.3 %collective-permute-start.7 = (f32[8,2,128]{2,1,0:T(2,128)S(1)}, f32[8,2,128]{2,1,0:T(2,128)S(1)}, u32[]{:S(2)}, u32[]{:S(2)}) collective-permute-start(f32[8,2,128]{2,1,0:T(2,128)S(1)} %get-tuple-element.152), channel_id=1, source_target_pairs={{0,1},{1,2},{2,3},{3,4},{4,5},{5,6},{6,7},{8,9},{9,10},{10,11},{11... | collective-permute-start | bytes 24584 | tf_op jit(solution)/shard_map/ppermute | solution.py:27
  140.2 5.0 %collective-permute-start.6 = (f32[8,2,128]{2,1,0:T(2,128)S(1)}, f32[8,2,128]{2,1,0:T(2,128)S(1)}, u32[]{:S(2)}, u32[]{:S(2)}) collective-permute-start(f32[8,2,128]{2,1,0:T(2,128)S(1)} %get-tuple-element.153), channel_id=1, source_target_pairs={{1,0},{2,1},{3,2},{4,3},{5,4},{6,5},{7,6},{9,8},{10,9},{11,10},{12... | collective-permute-start | bytes 24584 | tf_op jit(solution)/shard_map/ppermute | solution.py:28
  181.9 12.4 %collective-permute-start.9 = (f32[2,40,128]{2,1,0:T(8,128)S(1)}, f32[2,40,128]{2,1,0:T(8,128)S(1)}, u32[]{:S(2)}, u32[]{:S(2)}) collective-permute-start(f32[2,40,128]{2,1,0:T(8,128)S(1)} %get-tuple-element.146), channel_id=1, source_target_pairs={{0,8},{8,16},{16,24},{24,32},{32,40},{40,48},{48,56},{56,64},{64,7... | collective-permute-start | bytes 122888 | tf_op jit(solution)/shard_map/ppermute | solution.py:27
  185.3 8.9 %collective-permute-start.8 = (f32[2,40,128]{2,1,0:T(8,128)S(1)}, f32[2,40,128]{2,1,0:T(8,128)S(1)}, u32[]{:S(2)}, u32[]{:S(2)}) collective-permute-start(f32[2,40,128]{2,1,0:T(8,128)S(1)} %get-tuple-element.147), channel_id=1, source_target_pairs={{8,0},{16,8},{24,16},{32,24},{40,32},{48,40},{56,48},{64,56},{72,6... | collective-permute-start | bytes 122888 | tf_op jit(solution)/shard_map/ppermute | solution.py:28
  186.7 4.5 %collective-permute-start.11 = (f32[8,2,128]{2,1,0:T(2,128)S(1)}, f32[8,2,128]{2,1,0:T(2,128)S(1)}, u32[]{:S(2)}, u32[]{:S(2)}) collective-permute-start(f32[8,2,128]{2,1,0:T(2,128)S(1)} %get-tuple-element.148), channel_id=1, source_target_pairs={{0,1},{1,2},{2,3},{3,4},{4,5},{5,6},{6,7},{8,9},{9,10},{10,11},{11... | collective-permute-start | bytes 24584 | tf_op jit(solution)/shard_map/ppermute | solution.py:27
  189.3 5.0 %collective-permute-start.10 = (f32[8,2,128]{2,1,0:T(2,128)S(1)}, f32[8,2,128]{2,1,0:T(2,128)S(1)}, u32[]{:S(2)}, u32[]{:S(2)}) collective-permute-start(f32[8,2,128]{2,1,0:T(2,128)S(1)} %get-tuple-element.149), channel_id=1, source_target_pairs={{1,0},{2,1},{3,2},{4,3},{5,4},{6,5},{7,6},{9,8},{10,9},{11,10},{12... | collective-permute-start | bytes 24584 | tf_op jit(solution)/shard_map/ppermute | solution.py:28
where the time goes:
time: 235 us; the launch traced here: 233 us
  blocking collectives  140 us (60%)
  other arithmetic  34.2 us (15%)
  starting transfers between devices  29.3 us (12%)
  local copies, waits for them, and re-layouts  10.7 us (5%)
  between operations  9.88 us (4%)
  waiting for transfers between devices  8.59 us (4%)
    psum x12, blocking collectives, one_axis_at_a_time(): return functools.reduce(lax.psum, axes, shard)  99.1 us
    all_to_all x1, blocking collectives, sum_at_owner(): lax.all_to_all(blocks, axis, split_axis=0, concat_axis=0, tiled=True)  41.3 us
    add x8, other arithmetic, accumulate(): return total + occupations[index] * wave * wave  28 us
    ppermute x6, starting transfers between devices, padded_2(): lax.ppermute(last, axis, up)  19.2 us
    dynamic_slice x8, local copies, waits for them, and re-layouts, accumulate(): return total + occupations[index] * wave * wave  10.6 us
    ppermute x6, starting transfers between devices, padded_2(): lax.ppermute(first, axis, [(b, a) for a, b in up])  10.1 us
    ppermute x6, waiting for transfers between devices, padded_2(): lax.ppermute(first, axis, [(b, a) for a, b in up])  8.57 us
  transfers between devices with their start and end apart: 12, of which 3 were waited for; matrix products, arithmetic and copies ran while one was open for 0% of the time, Pallas kernels for 0%

commit v1 on v0

v1 whole, which is shorter than its diff:
```python
import functools
import math

import jax
import jax.numpy as jnp
from jax import lax
from jax.experimental import pallas as pl
from jax.experimental.pallas import tpu as pltpu
from jax.sharding import Mesh
from jax.sharding import PartitionSpec as P


ITERS = 3
REACH = 2 * ITERS
BAND = ("band_0", "band_1")
SPACE = ("space_0", "space_1")
EVERY = BAND + SPACE
SIDE = 4
F32 = jnp.float32


def device(z, x, y, core):
    return ((z * SIDE + x) * SIDE + y) * 2 + core


def moves(target):
    places = [(z, x, y, c) for z in range(SIDE) for x in range(SIDE) for y in range(SIDE) for c in range(2)]
    return [(device(*p), device(*target(*p))) for p in places]


def ring(phase, distance):
    def target(z, x, y, c):
        if (c == 0) == (phase == 0):
            return z, (x + distance) % SIDE, y, c
        return (z + distance) % SIDE, x, y, c

    return moves(target)


def send(value, pairs):
    return lax.ppermute(value, EVERY, pairs)


def density_body(order, occ, orb, out):
    total = None
    for b in range(orb.shape[0]):
        wave = orb[b].astype(F32)
        term = occ[b] * wave * wave
        total = term if total is None else total + term
    out[0] = total


def density_part(orbitals, weights, order, first):
    bands, rows, cols, lanes = orbitals.shape
    deep = rows // 16
    return pl.pallas_call(
        density_body,
        out_shape=jax.ShapeDtypeStruct((SIDE, deep, cols, lanes), F32),
        grid_spec=pltpu.PrefetchScalarGridSpec(
            num_scalar_prefetch=1,
            grid=(SIDE,),
            in_specs=[
                pl.BlockSpec(memory_space=pltpu.SMEM),
                pl.BlockSpec((bands, deep, cols, lanes), lambda g, o: (0, o[first + g], 0, 0)),
            ],
            out_specs=pl.BlockSpec((1, deep, cols, lanes), lambda g, o: (g, 0, 0, 0)),
        ),
        compiler_params=pltpu.CompilerParams(vmem_limit_bytes=16 * 2**20),
        cost_estimate=pl.CostEstimate(flops=0, bytes_accessed=orbitals.size // 2, transcendentals=0),
        name="density",
    )(order, weights, orbitals)


def own_density(orbitals, weights):
    z, x, c = lax.axis_index("band_0"), lax.axis_index("band_1"), lax.axis_index("space_1")
    slot = jnp.arange(16, dtype=jnp.int32)
    first, second = slot // SIDE, slot % SIDE
    to_z = (z + jnp.where(c == 0, second, first)) % SIDE
    to_x = (x + jnp.where(c == 0, first, second)) % SIDE
    order = to_z * SIDE + to_x
    part = [None] * SIDE
    arrived = []
    for k in (2, 1, 3):
        part[k] = density_part(orbitals, weights, order, k * SIDE)
        arrived.append(send(part[k], ring(0, k)))
    mine = density_part(orbitals, weights, order, 0)
    for other in arrived:
        mine = mine + other
    total = mine[0]
    for other in [send(mine[k], ring(1, k)) for k in (2, 1, 3)]:
        total = total + other
    return total


def with_halo(field):
    band = [(i, i + 1) for i in range(15)]
    low = lax.ppermute(field[-REACH:], BAND, band)
    high = lax.ppermute(field[:REACH], BAND, [(b, a) for a, b in band])
    field = jnp.concatenate([low, field, high], 0)
    first = lax.axis_index("space_1") == 0
    left, right = field[:, :REACH], field[:, -REACH:]
    inside = [(i, i ^ 1) for i in range(8)]
    across = [(1, 2), (2, 1), (3, 4), (4, 3), (5, 6), (6, 5)]
    near = lax.ppermute(jnp.where(first, right, left), SPACE, inside)
    far = lax.ppermute(jnp.where(first, left, right), SPACE, across)
    left, right = jnp.where(first, far, near), jnp.where(first, near, far)
    return jnp.concatenate([left, field, right], 1)


def stencil(padded):
    center = padded[2:-2, 2:-2, 2:-2]
    near = padded[3:-1, 2:-2, 2:-2] + padded[1:-3, 2:-2, 2:-2]
    near = near + padded[2:-2, 3:-1, 2:-2] + padded[2:-2, 1:-3, 2:-2]
    near = near + padded[2:-2, 2:-2, 3:-1] + padded[2:-2, 2:-2, 1:-3]
    distant = padded[4:, 2:-2, 2:-2] + padded[:-4, 2:-2, 2:-2]
    distant = distant + padded[2:-2, 4:, 2:-2] + padded[2:-2, :-4, 2:-2]
    distant = distant + padded[2:-2, 2:-2, 4:] + padded[2:-2, 2:-2, :-4]
    return 7.5 * center - 4.0 / 3.0 * near + 1.0 / 12.0 * distant


def weights_of(moments):
    unit = [m / moments[0] * 0.125**k for k, m in enumerate(moments)]

    def inner(a, b, shift):
        terms = [x * y * unit[i + j + shift] for i, x in enumerate(a) for j, y in enumerate(b)]
        return functools.reduce(lambda p, q: p + q, terms)

    residual, direction, answer = [1.0], [1.0], []
    norm = unit[0]
    for step in range(ITERS):
        alpha = norm / inner(direction, direction, 1)
        old = answer + [0.0] * (len(direction) - len(answer))
        answer = [a + alpha * d for a, d in zip(old, direction)]
        if step + 1 < ITERS:
            residual = [r - alpha * d for r, d in zip(residual + [0.0], [0.0] + direction)]
            fresh = inner(residual, residual, 0)
            ratio = fresh / norm
            direction = [r + ratio * d for r, d in zip(residual, direction + [0.0])]
            norm = fresh
    return [a * 0.125 ** (k + 1) for k, a in enumerate(answer)]


def local(orbitals, occupations):
    rows, cols, lanes = orbitals.shape[1] // 16, orbitals.shape[2], orbitals.shape[3]
    scale = 4.0 * math.pi / (orbitals.shape[0] * 16)
    source = own_density(orbitals, occupations * scale)
    wide = with_halo(source)
    band = lax.axis_index(BAND)
    space = lax.axis_index(SPACE)
    row = band * rows - REACH + jnp.arange(wide.shape[0])[:, None, None]
    col = space * cols - REACH + jnp.arange(wide.shape[1])[None, :, None]
    inside = (row >= 0) & (row < 16 * rows) & (col >= 0) & (col < 8 * cols)
    fields = [wide]
    for step in range(ITERS):
        image = stencil(jnp.pad(fields[-1], ((0, 0), (0, 0), (2, 2))))
        edge = 2 * (step + 1)
        fields.append(jnp.where(inside[edge:-edge, edge:-edge], image, 0.0))
    own = []
    for step, field in enumerate(fields):
        edge = REACH - 2 * step
        own.append(field[edge : edge + rows, edge : edge + cols])
    sums = [jnp.sum(own[(k) // 2] * own[(k + 1) // 2]) for k in range(2 * ITERS)]
    lane = jnp.arange(lanes)
    line = functools.reduce(lambda p, q: p + q, [jnp.where(lane == k, m, 0.0) for k, m in enumerate(sums)])
    lines = jnp.broadcast_to(line[None, None], (128, 1, lanes))
    lines = lax.all_to_all(lines, EVERY, split_axis=0, concat_axis=0, tiled=True)
    total = jnp.sum(lines, (0, 1))
    factors = weights_of([total[k] for k in range(2 * ITERS)])
    return factors[0] * own[0] + factors[1] * own[1] + factors[2] * own[2]


def solution(mesh):
    split = Mesh(mesh.devices.reshape(SIDE, SIDE, SIDE, 2), EVERY)
    in_specs = (P(BAND, None, SPACE, None), P(BAND))
    out_specs = P(BAND, SPACE, None)
    return jax.shard_map(local, mesh=split, in_specs=in_specs, out_specs=out_specs, check_vma=False)
```

time: 235 us -> 94.2 us (0.40)
  blocking collectives: 140 us -> 20.5 us
  other arithmetic: 34.2 us -> 8.87 us
  Pallas kernels: 0 us -> 8.05 us
  waiting for transfers between devices: 8.59 us -> 16.4 us
  local copies, waits for them, and re-layouts: 10.7 us -> 4.96 us
  starting transfers between devices: 29.3 us -> 24.5 us
    psum x12 -> x0, blocking collectives: 99.1 us -> none  [one_axis_at_a_time(): return functools.reduce(lax.psum, axes, shard)]
    add x9 -> x5, other arithmetic: 28.7 us -> 5.99 us  [the longest x1 3.77 us: local(): p + q]
    all_to_all x1, blocking collectives: 41.3 us -> 20.5 us  [local(): lax.all_to_all(lines, EVERY, split_axis=0, concat_axis=0, tiled=True)]
    dynamic_slice x8 -> x0, local copies, waits for them, and re-layouts: 10.6 us -> none  [accumulate(): return total + occupations[index] * wave * wave]
    pallas_call x0 -> x4, Pallas kernels: none -> 8.05 us  [density_part(): pl.pallas_call(density_body, out_shape=jax.ShapeDtypeStruct((SIDE, deep,...]
    ppermute x12 -> x10, waiting for transfers between devices: 8.59 us -> 16.4 us  [the longest x6 9.62 us: send(): return lax.ppermute(value, EVERY, pairs)]
    ppermute x12 -> x10, starting transfers between devices: 29.3 us -> 24.5 us  [the longest x6 12.7 us: send(): return lax.ppermute(value, EVERY, pairs)]
    unnamed x0 -> x2, local copies, waits for them, and re-layouts: none -> 3.97 us
  transfers between devices with their start and end apart: 12 -> 10, of which waited for: 3 -> 7; matrix products, arithmetic and copies ran while one was open for 0% -> 0% of each run, Pallas kernels for 0% -> 6%
where the time goes in v1:
time: 94.2 us; the launch traced here: 93.8 us
  starting transfers between devices  24.5 us (26%)
  blocking collectives  20.5 us (22%)
  waiting for transfers between devices  16.4 us (17%)
  between operations  10.5 us (11%)
  other arithmetic  8.87 us (9%)
  Pallas kernels  8.05 us (9%)
  local copies, waits for them, and re-layouts  4.96 us (5%)
    all_to_all x1, blocking collectives, local(): lax.all_to_all(lines, EVERY, split_axis=0, concat_axis=0, tiled=True)  20.5 us
    ppermute x6, starting transfers between devices, send(): return lax.ppermute(value, EVERY, pairs)  12.7 us
    ppermute x6, waiting for transfers between devices, send(): return lax.ppermute(value, EVERY, pairs)  9.62 us
    pallas_call x4, Pallas kernels, density_part(): pl.pallas_call(density_body, out_shape=jax.ShapeDtypeStruct((SIDE, deep,...  8.05 us
    ppermute x1, starting transfers between devices, with_halo(): near = lax.ppermute(jnp.where(first, right, left), SPACE, inside)  4.88 us
    unnamed x2, local copies, waits for them, and re-layouts  3.97 us
    ppermute x1, waiting for transfers between devices, with_halo(): high = lax.ppermute(field[:REACH], BAND, [(b, a) for a, b in band])  3.78 us
    add x1, other arithmetic, local(): p + q  3.77 us
  transfers between devices with their start and end apart: 10, of which 7 were waited for; matrix products, arithmetic and copies ran while one was open for 0% of the time, Pallas kernels for 6%

profile of v1, /device:TPU:1, one launch (start us, length us, event | category | flops | bytes accessed | tf_op | source)
XLA Modules:
  0.0 93.8 jit_solution(8966623498921109650)
XLA Ops:
  0.0 0.7 broadcast_multiply_fusion.occ
  0.7 4.0 %copy-done = bf16[8,128,40,128]{3,2,1,0:T(8,128)(2,1)S(1)} copy-done((bf16[8,128,40,128]{3,2,1,0:T(8,128)(2,1)S(1)}, bf16[8,128,40,128]{3,2,1,0:T(8,128)(2,1)}, u32[]{:S(2)}) %copy-start) | copy-done | bytes 10485784
  4.7 2.0 %density.5 = f32[4,8,40,128]{3,2,1,0:T(8,128)S(1)} custom-call(s32[16]{0:T(128)S(1)} %fusion.32.order, f32[8]{0:T(128)S(1)} %broadcast_multiply_fusion.occ, bf16[8,128,40,128]{3,2,1,0:T(8,128)(2,1)S(1)} %copy-done), custom_call_target="tpu_custom_call" | custom-call | bytes 2621440 | tf_op jit(solution)/shard_map/density/pallas_call | solution.py:56
  6.7 4.5 %collective-permute-start = (f32[4,8,40,128]{3,2,1,0:T(8,128)S(1)}, f32[4,8,40,128]{3,2,1,0:T(8,128)S(1)}, u32[]{:S(2)}, u32[]{:S(2)}) collective-permute-start(f32[4,8,40,128]{3,2,1,0:T(8,128)S(1)} %density.5), channel_id=1, source_target_pairs={{0,16},{1,65},{2,18},{3,67},{4,20},{5,69},{6,22},{7,71},{8,24},{9,... | collective-permute-start | bytes 1966088 | tf_op jit(solution)/shard_map/ppermute | solution.py:41
  11.2 2.0 %density.6 = f32[4,8,40,128]{3,2,1,0:T(8,128)S(1)} custom-call(s32[16]{0:T(128)S(1)} %fusion.32.order, f32[8]{0:T(128)S(1)} %broadcast_multiply_fusion.occ, bf16[8,128,40,128]{3,2,1,0:T(8,128)(2,1)S(1)} %copy-done), custom_call_target="tpu_custom_call" | custom-call | bytes 2621440 | tf_op jit(solution)/shard_map/density/pallas_call | solution.py:56
  13.2 0.8 collective-permute-start.1
  14.0 2.0 %density.7 = f32[4,8,40,128]{3,2,1,0:T(8,128)S(1)} custom-call(s32[16]{0:T(128)S(1)} %fusion.32.order, f32[8]{0:T(128)S(1)} %broadcast_multiply_fusion.occ, bf16[8,128,40,128]{3,2,1,0:T(8,128)(2,1)S(1)} %copy-done), custom_call_target="tpu_custom_call" | custom-call | bytes 2621440 | tf_op jit(solution)/shard_map/density/pallas_call | solution.py:56
  16.0 2.0 %collective-permute-start.2 = (f32[4,8,40,128]{3,2,1,0:T(8,128)S(1)}, f32[4,8,40,128]{3,2,1,0:T(8,128)}, u32[]{:S(2)}, u32[]{:S(2)}) collective-permute-start(f32[4,8,40,128]{3,2,1,0:T(8,128)S(1)} %density.7), channel_id=1, source_target_pairs={{0,24},{1,97},{2,26},{3,99},{4,28},{5,101},{6,30},{7,103},{8,0},{9... | collective-permute-start | bytes 1966088 | tf_op jit(solution)/shard_map/ppermute | solution.py:41
  18.0 2.0 %density.4 = f32[4,8,40,128]{3,2,1,0:T(8,128)S(1)} custom-call(s32[16]{0:T(128)S(1)} %fusion.32.order, f32[8]{0:T(128)S(1)} %broadcast_multiply_fusion.occ, bf16[8,128,40,128]{3,2,1,0:T(8,128)(2,1)S(1)} %copy-done), custom_call_target="tpu_custom_call" | custom-call | bytes 2621440 | tf_op jit(solution)/shard_map/density/pallas_call | solution.py:56
  20.1 0.1 and_and_fusion
  20.2 6.4 %collective-permute-done.1 = f32[4,8,40,128]{3,2,1,0:T(8,128)} collective-permute-done((f32[4,8,40,128]{3,2,1,0:T(8,128)S(1)}, f32[4,8,40,128]{3,2,1,0:T(8,128)}, u32[]{:S(2)}, u32[]{:S(2)}) %collective-permute-start.1) | collective-permute-done | bytes 655392 | tf_op jit(solution)/shard_map/ppermute | solution.py:41
  26.6 0.6 collective-permute-done.2
  27.2 1.4 %add_add_fusion = f32[4,8,40,128]{3,2,1,0:T(8,128)S(1)} fusion(f32[4,8,40,128]{3,2,1,0:T(8,128)} %collective-permute-done.2, f32[4,8,40,128]{3,2,1,0:T(8,128)} %collective-permute-done.1, f32[4,8,40,128]{3,2,1,0:T(8,128)S(1)} %density.4, f32[4,8,40,128]{3,2,1,0:T(8,128)S(1)} %collective-permute-done), kind=kLoop, calls=%fused_computation.12 | loop fusion | flops 491520 | bytes 3276800 | tf_op jit(solution)/shard_map/add | solution.py:88
  28.6 2.7 %collective-permute-start.3 = (f32[8,40,128]{2,1,0:T(8,128)S(1)}, f32[8,40,128]{2,1,0:T(8,128)S(1)}, u32[]{:S(2)}, u32[]{:S(2)}) collective-permute-start(f32[8,40,128]{2,1,0:T(8,128)S(1)} %get-tuple-element.14), channel_id=1, source_target_pairs={{0,64},{1,17},{2,66},{3,19},{4,68},{5,21},{6,70},{7,23},{8,72},{9,... | collective-permute-start | bytes 491528 | tf_op jit(solution)/shard_map/ppermute | solution.py:41
  31.4 0.5 collective-permute-start.4
  31.9 2.1 %collective-permute-start.5 = (f32[8,40,128]{2,1,0:T(8,128)S(1)}, f32[8,40,128]{2,1,0:T(8,128)S(1)}, u32[]{:S(2)}, u32[]{:S(2)}) collective-permute-start(f32[8,40,128]{2,1,0:T(8,128)S(1)} %get-tuple-element.15), channel_id=1, source_target_pairs={{0,96},{1,25},{2,98},{3,27},{4,100},{5,29},{6,102},{7,31},{8,104},... | collective-permute-start | bytes 491528 | tf_op jit(solution)/shard_map/ppermute | solution.py:41
  34.1 0.6 collective-permute-done.3
  34.7 2.1 %collective-permute-done.4 = f32[8,40,128]{2,1,0:T(8,128)S(1)} collective-permute-done((f32[8,40,128]{2,1,0:T(8,128)S(1)}, f32[8,40,128]{2,1,0:T(8,128)S(1)}, u32[]{:S(2)}, u32[]{:S(2)}) %collective-permute-start.4) | collective-permute-done | bytes 163872 | tf_op jit(solution)/shard_map/ppermute | solution.py:41
  36.8 2.5 %collective-permute-start.6 = (f32[6,40,128]{2,1,0:T(8,128)S(1)}, f32[6,40,128]{2,1,0:T(8,128)S(1)}, u32[]{:S(2)}, u32[]{:S(2)}) collective-permute-start(f32[6,40,128]{2,1,0:T(8,128)S(1)} %get-tuple-element.19), channel_id=1, source_target_pairs={{0,8},{8,16},{16,24},{24,32},{32,40},{40,48},{48,56},{56,64},{64,7... | collective-permute-start | bytes 368648 | tf_op jit(solution)/shard_map/ppermute | solution.py:97
  39.4 1.3 %collective-permute-start.7 = (f32[6,40,128]{2,1,0:T(8,128)S(1)}, f32[6,40,128]{2,1,0:T(8,128)S(1)}, u32[]{:S(2)}, u32[]{:S(2)}) collective-permute-start(f32[6,40,128]{2,1,0:T(8,128)S(1)} %get-tuple-element.20), channel_id=1, source_target_pairs={{8,0},{16,8},{24,16},{32,24},{40,32},{48,40},{56,48},{64,56},{72,6... | collective-permute-start | bytes 368648 | tf_op jit(solution)/shard_map/ppermute | solution.py:98
  40.7 0.5 collective-permute-done.6
  41.2 3.8 %collective-permute-done.7 = f32[6,40,128]{2,1,0:T(8,128)S(1)} collective-permute-done((f32[6,40,128]{2,1,0:T(8,128)S(1)}, f32[6,40,128]{2,1,0:T(8,128)S(1)}, u32[]{:S(2)}, u32[]{:S(2)}) %collective-permute-start.7) | collective-permute-done | bytes 122912 | tf_op jit(solution)/shard_map/ppermute | solution.py:98
  45.0 4.9 %collective-permute-start.9 = (f32[20,6,128]{2,1,0:T(8,128)S(1)}, f32[20,6,128]{2,1,0:T(8,128)S(1)}, u32[]{:S(2)}, u32[]{:S(2)}) collective-permute-start(f32[20,6,128]{2,1,0:T(8,128)S(1)} %broadcast_select_fusion.2), channel_id=1, source_target_pairs={{0,1},{1,0},{2,3},{3,2},{4,5},{5,4},{6,7},{7,6},{8,9},{9,8},{10,11... | collective-permute-start | bytes 184328 | tf_op jit(solution)/shard_map/ppermute | solution.py:104
  49.9 3.1 %collective-permute-start.8 = (f32[20,6,128]{2,1,0:T(8,128)S(1)}, f32[20,6,128]{2,1,0:T(8,128)S(1)}, u32[]{:S(2)}, u32[]{:S(2)}) collective-permute-start(f32[20,6,128]{2,1,0:T(8,128)S(1)} %get-tuple-element.11), channel_id=1, source_target_pairs={{1,2},{2,1},{3,4},{4,3},{5,6},{6,5},{9,10},{10,9},{11,12},{12,11},... | collective-permute-start | bytes 184328 | tf_op jit(solution)/shard_map/ppermute | solution.py:105
  53.1 2.6 %collective-permute-done.8 = f32[20,6,128]{2,1,0:T(8,128)S(1)} collective-permute-done((f32[20,6,128]{2,1,0:T(8,128)S(1)}, f32[20,6,128]{2,1,0:T(8,128)S(1)}, u32[]{:S(2)}, u32[]{:S(2)}) %collective-permute-start.8) | collective-permute-done | bytes 61472 | tf_op jit(solution)/shard_map/ppermute | solution.py:105
  55.7 0.6 fusion.5
  56.3 0.4 fusion.14
  56.8 1.0 %multiply_reduce_fusion.3 = (f32[]{:T(128)}, f32[]{:T(128)}, f32[]{:T(128)}, f32[]{:T(128)}, f32[]{:T(128)}, /*index=5*/f32[]{:T(128)}) fusion(f32[8,40,128]{2,1,0:T(8,128)S(1)} %fusion.30, f32[16,48,128]{2,1,0:T(8,128)S(1)} %fusion.5, f32[12,44,128]{2,1,0:T(8,128)S(1)} %fusion.14, pred[8,40]{1,0:T(8,128)(4,1)S(1)} %slice_bitcast_fusion.6), kind=kLoop, calls=%fused_computation.73 | loop fusion | flops 1146874 | bytes 2098200 | tf_op jit(solution)/shard_map/reduce_sum | solution.py:162
  57.7 3.8 %fusion.40 = f32[128]{0:T(128)S(1)} fusion(f32[]{:T(128)} %get-tuple-element.9, f32[]{:T(128)} %get-tuple-element.8, f32[]{:T(128)} %get-tuple-element.7, f32[]{:T(128)} %get-tuple-element.6, f32[]{:T(128)} %get-tuple-element.5, f32[]{:T(128)} %get-tuple-element.10), kind=kLoop, calls=%fused_computation.114 | loop fusion | flops 2176 | bytes 536 | tf_op jit(solution)/shard_map/add | solution.py:164
  61.6 20.5 %all_to_all.5 = f32[128,1,128]{2,1,0:T(1,128)S(1)} all-to-all(f32[128,1,128]{2,1,0:T(1,128)S(1)} %broadcast_in_dim.94), channel_id=1, replica_groups=mesh['band_0'=4,'band_1'=4,'space_0'=4,'space_1'=2] {'band_0','band_1','..., dimensions={0} | all-to-all | bytes 131072 | tf_op jit(solution)/shard_map/all_to_all | solution.py:166
  82.1 0.7 fusion.46
  93.0 0.7 multiply_add_fusion
  (19 shorter events, 0.5 us)
Async XLA Ops:
  0.7 4.0 %copy-start = (bf16[8,128,40,128]{3,2,1,0:T(8,128)(2,1)S(1)}, bf16[8,128,40,128]{3,2,1,0:T(8,128)(2,1)}, u32[]{:S(2)}) copy-start(bf16[8,128,40,128]{3,2,1,0:T(8,128)(2,1)} %orb.7) | copy-start | bytes 31457284
  6.7 13.5 %collective-permute-start = (f32[4,8,40,128]{3,2,1,0:T(8,128)S(1)}, f32[4,8,40,128]{3,2,1,0:T(8,128)S(1)}, u32[]{:S(2)}, u32[]{:S(2)}) collective-permute-start(f32[4,8,40,128]{3,2,1,0:T(8,128)S(1)} %density.5), channel_id=1, source_target_pairs={{0,16},{1,65},{2,18},{3,67},{4,20},{5,69},{6,22},{7,71},{8,24},{9,... | collective-permute-start | bytes 1966088 | tf_op jit(solution)/shard_map/ppermute | solution.py:41
  13.2 13.4 %collective-permute-start.1 = (f32[4,8,40,128]{3,2,1,0:T(8,128)S(1)}, f32[4,8,40,128]{3,2,1,0:T(8,128)}, u32[]{:S(2)}, u32[]{:S(2)}) collective-permute-start(f32[4,8,40,128]{3,2,1,0:T(8,128)S(1)} %density.6), channel_id=1, source_target_pairs={{0,8},{1,33},{2,10},{3,35},{4,12},{5,37},{6,14},{7,39},{8,16},{9,4... | collective-permute-start | bytes 1966088 | tf_op jit(solution)/shard_map/ppermute | solution.py:41
  16.0 11.1 %collective-permute-start.2 = (f32[4,8,40,128]{3,2,1,0:T(8,128)S(1)}, f32[4,8,40,128]{3,2,1,0:T(8,128)}, u32[]{:S(2)}, u32[]{:S(2)}) collective-permute-start(f32[4,8,40,128]{3,2,1,0:T(8,128)S(1)} %density.7), channel_id=1, source_target_pairs={{0,24},{1,97},{2,26},{3,99},{4,28},{5,101},{6,30},{7,103},{8,0},{9... | collective-permute-start | bytes 1966088 | tf_op jit(solution)/shard_map/ppermute | solution.py:41
  28.6 6.0 %collective-permute-start.3 = (f32[8,40,128]{2,1,0:T(8,128)S(1)}, f32[8,40,128]{2,1,0:T(8,128)S(1)}, u32[]{:S(2)}, u32[]{:S(2)}) collective-permute-start(f32[8,40,128]{2,1,0:T(8,128)S(1)} %get-tuple-element.14), channel_id=1, source_target_pairs={{0,64},{1,17},{2,66},{3,19},{4,68},{5,21},{6,70},{7,23},{8,72},{9,... | collective-permute-start | bytes 491528 | tf_op jit(solution)/shard_map/ppermute | solution.py:41
  31.4 5.4 %collective-permute-start.4 = (f32[8,40,128]{2,1,0:T(8,128)S(1)}, f32[8,40,128]{2,1,0:T(8,128)S(1)}, u32[]{:S(2)}, u32[]{:S(2)}) collective-permute-start(f32[8,40,128]{2,1,0:T(8,128)S(1)} %get-tuple-element.16), channel_id=1, source_target_pairs={{0,32},{1,9},{2,34},{3,11},{4,36},{5,13},{6,38},{7,15},{8,40},{9,1... | collective-permute-start | bytes 491528 | tf_op jit(solution)/shard_map/ppermute | solution.py:41
  31.9 4.8 %collective-permute-start.5 = (f32[8,40,128]{2,1,0:T(8,128)S(1)}, f32[8,40,128]{2,1,0:T(8,128)S(1)}, u32[]{:S(2)}, u32[]{:S(2)}) collective-permute-start(f32[8,40,128]{2,1,0:T(8,128)S(1)} %get-tuple-element.15), channel_id=1, source_target_pairs={{0,96},{1,25},{2,98},{3,27},{4,100},{5,29},{6,102},{7,31},{8,104},... | collective-permute-start | bytes 491528 | tf_op jit(solution)/shard_map/ppermute | solution.py:41
  36.8 4.4 %collective-permute-start.6 = (f32[6,40,128]{2,1,0:T(8,128)S(1)}, f32[6,40,128]{2,1,0:T(8,128)S(1)}, u32[]{:S(2)}, u32[]{:S(2)}) collective-permute-start(f32[6,40,128]{2,1,0:T(8,128)S(1)} %get-tuple-element.19), channel_id=1, source_target_pairs={{0,8},{8,16},{16,24},{24,32},{32,40},{40,48},{48,56},{56,64},{64,7... | collective-permute-start | bytes 368648 | tf_op jit(solution)/shard_map/ppermute | solution.py:97
  39.4 5.6 %collective-permute-start.7 = (f32[6,40,128]{2,1,0:T(8,128)S(1)}, f32[6,40,128]{2,1,0:T(8,128)S(1)}, u32[]{:S(2)}, u32[]{:S(2)}) collective-permute-start(f32[6,40,128]{2,1,0:T(8,128)S(1)} %get-tuple-element.20), channel_id=1, source_target_pairs={{8,0},{16,8},{24,16},{32,24},{40,32},{48,40},{56,48},{64,56},{72,6... | collective-permute-start | bytes 368648 | tf_op jit(solution)/shard_map/ppermute | solution.py:98
  45.0 8.1 %collective-permute-start.9 = (f32[20,6,128]{2,1,0:T(8,128)S(1)}, f32[20,6,128]{2,1,0:T(8,128)S(1)}, u32[]{:S(2)}, u32[]{:S(2)}) collective-permute-start(f32[20,6,128]{2,1,0:T(8,128)S(1)} %broadcast_select_fusion.2), channel_id=1, source_target_pairs={{0,1},{1,0},{2,3},{3,2},{4,5},{5,4},{6,7},{7,6},{8,9},{9,8},{10,11... | collective-permute-start | bytes 184328 | tf_op jit(solution)/shard_map/ppermute | solution.py:104
  49.9 5.7 %collective-permute-start.8 = (f32[20,6,128]{2,1,0:T(8,128)S(1)}, f32[20,6,128]{2,1,0:T(8,128)S(1)}, u32[]{:S(2)}, u32[]{:S(2)}) collective-permute-start(f32[20,6,128]{2,1,0:T(8,128)S(1)} %get-tuple-element.11), channel_id=1, source_target_pairs={{1,2},{2,1},{3,4},{4,3},{5,6},{6,5},{9,10},{10,9},{11,12},{12,11},... | collective-permute-start | bytes 184328 | tf_op jit(solution)/shard_map/ppermute | solution.py:105

commit v2 on v1

--- a/solution.py
+++ b/solution.py
@@ -65,7 +65,7 @@
             ],
             out_specs=pl.BlockSpec((1, deep, cols, lanes), lambda g, o: (g, 0, 0, 0)),
         ),
-        compiler_params=pltpu.CompilerParams(vmem_limit_bytes=16 * 2**20),
+        compiler_params=pltpu.CompilerParams(vmem_limit_bytes=52 * 2**20),
         cost_estimate=pl.CostEstimate(flops=0, bytes_accessed=orbitals.size // 2, transcendentals=0),
         name="density",
     )(order, weights, orbitals)
@@ -92,7 +92,7 @@
     return total
 
 
-def with_halo(field):
+def halo(field):
     band = [(i, i + 1) for i in range(15)]
     low = lax.ppermute(field[-REACH:], BAND, band)
     high = lax.ppermute(field[:REACH], BAND, [(b, a) for a, b in band])
@@ -103,19 +103,104 @@
     across = [(1, 2), (2, 1), (3, 4), (4, 3), (5, 6), (6, 5)]
     near = lax.ppermute(jnp.where(first, right, left), SPACE, inside)
     far = lax.ppermute(jnp.where(first, left, right), SPACE, across)
-    left, right = jnp.where(first, far, near), jnp.where(first, near, far)
-    return jnp.concatenate([left, field, right], 1)
-
-
-def stencil(padded):
-    center = padded[2:-2, 2:-2, 2:-2]
-    near = padded[3:-1, 2:-2, 2:-2] + padded[1:-3, 2:-2, 2:-2]
-    near = near + padded[2:-2, 3:-1, 2:-2] + padded[2:-2, 1:-3, 2:-2]
-    near = near + padded[2:-2, 2:-2, 3:-1] + padded[2:-2, 2:-2, 1:-3]
-    distant = padded[4:, 2:-2, 2:-2] + padded[:-4, 2:-2, 2:-2]
-    distant = distant + padded[2:-2, 4:, 2:-2] + padded[2:-2, :-4, 2:-2]
-    distant = distant + padded[2:-2, 2:-2, 4:] + padded[2:-2, 2:-2, :-4]
+    return low, high, near, far
+
+
+def laplacian(ref, r, lane):
+    center = ref[r]
+    wide = center.shape[0]
+
+    def across(k):
+        return pltpu.roll(center, k % wide, 0)
+
+    def along(k):
+        moved = pltpu.roll(center, k % center.shape[1], 1)
+        inside = lane >= k if k > 0 else lane < center.shape[1] + k
+        return jnp.where(inside, moved, 0.0)
+
+    near = ref[r + 1] + ref[r - 1] + across(-1) + across(1) + along(-1) + along(1)
+    distant = ref[r + 2] + ref[r - 2] + across(-2) + across(2) + along(-2) + along(2)
     return 7.5 * center - 4.0 / 3.0 * near + 1.0 / 12.0 * distant
+
+
+PAD = 8
+
+
+def krylov_body(place, own, low, high, near, far, first_out, second_out, lines, zero, one, two):
+    rows, cols, lanes = own.shape
+    deep = rows + 2 * REACH
+    band, space, core = place[0], place[1], place[2]
+    zero[:, 0:PAD] = jnp.zeros((deep, PAD, lanes), F32)
+    zero[:, PAD + cols : 2 * PAD + cols] = jnp.zeros((deep, PAD, lanes), F32)
+    zero[0:REACH, PAD : PAD + cols] = low[...]
+    zero[REACH : REACH + rows, PAD : PAD + cols] = own[...]
+    zero[REACH + rows : deep, PAD : PAD + cols] = high[...]
+
+    @pl.when(core == 0)
+    def _():
+        zero[:, PAD - REACH : PAD] = far[...]
+        zero[:, PAD + cols : PAD + cols + REACH] = near[...]
+
+    @pl.when(core == 1)
+    def _():
+        zero[:, PAD - REACH : PAD] = near[...]
+        zero[:, PAD + cols : PAD + cols + REACH] = far[...]
+
+    shape = (cols + 2 * PAD, lanes)
+    lane = lax.broadcasted_iota(jnp.int32, shape, 1)
+    col = lax.broadcasted_iota(jnp.int32, shape, 0) + (space * cols - PAD)
+    col_in = (col >= 0) & (col < 8 * cols)
+
+    def advance(source, target, edge):
+        def step(r, carry):
+            row = band * rows + (r - REACH)
+            row_in = (row >= 0) & (row < 16 * rows)
+            target[r] = jnp.where(col_in & row_in, laplacian(source, r, lane), 0.0)
+            return carry
+
+        lax.fori_loop(edge, deep - edge, step, 0)
+
+    advance(zero, one, 2)
+    advance(one, two, 4)
+
+    def fold(p, q):
+        product = p * q
+        return functools.reduce(lambda a, b: a + b, [product[i : i + 8] for i in range(0, cols, 8)])
+
+    def gather(r, sums):
+        at = r + REACH
+        s0 = zero[at, PAD : PAD + cols]
+        s1 = one[at, PAD : PAD + cols]
+        s2 = two[at, PAD : PAD + cols]
+        s3 = laplacian(two, at, lane)[PAD : PAD + cols]
+        first_out[r] = s1
+        second_out[r] = s2
+        pairs = ((s0, s0), (s0, s1), (s1, s1), (s1, s2), (s2, s2), (s2, s3))
+        return tuple(t + fold(p, q) for t, (p, q) in zip(sums, pairs))
+
+    sums = lax.fori_loop(0, rows, gather, tuple(jnp.zeros((8, lanes), F32) for _ in range(2 * ITERS)))
+    spot = lax.broadcasted_iota(jnp.int32, (1, lanes), 1)
+    line = jnp.zeros((1, lanes), F32)
+    for k, part in enumerate(sums):
+        whole = jnp.sum(jnp.sum(part, axis=0, keepdims=True), axis=1, keepdims=True)
+        line = line + jnp.where(spot == k, whole, 0.0)
+    lines[...] = jnp.broadcast_to(line[None], lines.shape)
+
+
+def krylov(place, own, low, high, near, far):
+    rows, cols, lanes = own.shape
+    scratch = pltpu.VMEM((rows + 2 * REACH, cols + 2 * PAD, lanes), F32)
+    vmem = pl.BlockSpec(memory_space=pltpu.VMEM)
+    field = jax.ShapeDtypeStruct(own.shape, F32)
+    return pl.pallas_call(
+        krylov_body,
+        out_shape=(field, field, jax.ShapeDtypeStruct((128, 1, lanes), F32)),
+        in_specs=[pl.BlockSpec(memory_space=pltpu.SMEM)] + [vmem] * 5,
+        out_specs=(vmem, vmem, vmem),
+        scratch_shapes=[scratch, scratch, scratch],
+        compiler_params=pltpu.CompilerParams(vmem_limit_bytes=8 * 2**20),
+        name="krylov",
+    )(place, own, low, high, near, far)
 
 
 def weights_of(moments):
@@ -140,33 +225,34 @@
     return [a * 0.125 ** (k + 1) for k, a in enumerate(answer)]
 
 
+def combine_body(lines, own, first, second, out):
+    line = jnp.sum(lines[...], axis=0)
+    spot = lax.broadcasted_iota(jnp.int32, line.shape, 1)
+    moments = [jnp.sum(jnp.where(spot == k, line, 0.0), axis=1, keepdims=True) for k in range(2 * ITERS)]
+    factors = [jnp.broadcast_to(f, own.shape[1:]) for f in weights_of(moments)]
+    for r in range(own.shape[0]):
+        out[r] = factors[0] * own[r] + factors[1] * first[r] + factors[2] * second[r]
+
+
+def combine(lines, own, first, second):
+    vmem = pl.BlockSpec(memory_space=pltpu.VMEM)
+    return pl.pallas_call(
+        combine_body,
+        out_shape=jax.ShapeDtypeStruct(own.shape, F32),
+        in_specs=[vmem] * 4,
+        out_specs=vmem,
+        compiler_params=pltpu.CompilerParams(vmem_limit_bytes=8 * 2**20),
+        name="combine",
+    )(lines, own, first, second)
+
+
 def local(orbitals, occupations):
-    rows, cols, lanes = orbitals.shape[1] // 16, orbitals.shape[2], orbitals.shape[3]
     scale = 4.0 * math.pi / (orbitals.shape[0] * 16)
     source = own_density(orbitals, occupations * scale)
-    wide = with_halo(source)
-    band = lax.axis_index(BAND)
-    space = lax.axis_index(SPACE)
-    row = band * rows - REACH + jnp.arange(wide.shape[0])[:, None, None]
-    col = space * cols - REACH + jnp.arange(wide.shape[1])[None, :, None]
-    inside = (row >= 0) & (row < 16 * rows) & (col >= 0) & (col < 8 * cols)
-    fields = [wide]
-    for step in range(ITERS):
-        image = stencil(jnp.pad(fields[-1], ((0, 0), (0, 0), (2, 2))))
-        edge = 2 * (step + 1)
-        fields.append(jnp.where(inside[edge:-edge, edge:-edge], image, 0.0))
-    own = []
-    for step, field in enumerate(fields):
-        edge = REACH - 2 * step
-        own.append(field[edge : edge + rows, edge : edge + cols])
-    sums = [jnp.sum(own[(k) // 2] * own[(k + 1) // 2]) for k in range(2 * ITERS)]
-    lane = jnp.arange(lanes)
-    line = functools.reduce(lambda p, q: p + q, [jnp.where(lane == k, m, 0.0) for k, m in enumerate(sums)])
-    lines = jnp.broadcast_to(line[None, None], (128, 1, lanes))
+    place = jnp.stack([lax.axis_index(BAND), lax.axis_index(SPACE), lax.axis_index("space_1")])
+    first, second, lines = krylov(place.astype(jnp.int32), source, *halo(source))
     lines = lax.all_to_all(lines, EVERY, split_axis=0, concat_axis=0, tiled=True)
-    total = jnp.sum(lines, (0, 1))
-    factors = weights_of([total[k] for k in range(2 * ITERS)])
-    return factors[0] * own[0] + factors[1] * own[1] + factors[2] * own[2]
+    return combine(lines, source, first, second)
 
 
 def solution(mesh):

time: 94.2 us -> 80 us (0.85)
  Pallas kernels: 8.05 us -> 18.9 us
  between operations: 10.5 us -> 0.13 us
  other arithmetic: 8.87 us -> 0.97 us
  local copies, waits for them, and re-layouts: 4.96 us -> 0.05 us
  waiting for transfers between devices: 16.4 us -> 14 us
  blocking collectives: 20.5 us -> 22.1 us
  starting transfers between devices: 24.5 us -> 23.5 us
    pallas_call x4, Pallas kernels: 8.05 us -> 13.5 us  [density_part(): pl.pallas_call(density_body, out_shape=jax.ShapeDtypeStruct((SIDE, deep,...]
    pallas_call x0 -> x2, Pallas kernels: none -> 5.42 us  [the longest x1 4.43 us: krylov(): pl.pallas_call(krylov_body, out_shape=(field, field, jax.ShapeDtypeStruct...]
    add x2 -> x0, other arithmetic: 4.49 us -> none  [the longest x1 3.77 us: local(): p + q]
    unnamed x2 -> x0, local copies, waits for them, and re-layouts: 3.97 us -> none
    ppermute x6, waiting for transfers between devices: 9.62 us -> 7.1 us  [send(): return lax.ppermute(value, EVERY, pairs)]
    all_to_all x1, blocking collectives: 20.5 us -> 22.1 us  [local(): lax.all_to_all(lines, EVERY, split_axis=0, concat_axis=0, tiled=True)]
    add x1, other arithmetic: 1.44 us -> 0.16 us  [own_density(): mine = mine + other]
    select_n x5 -> x2, other arithmetic: 1.07 us -> 0.03 us  [the longest x1 0.02 us: halo(): far = lax.ppermute(jnp.where(first, left, right), SPACE, across)]
  transfers between devices with their start and end apart: 10 -> 10, of which waited for: 7 -> 7; matrix products, arithmetic and copies ran while one was open for 0% -> 0% of each run, Pallas kernels for 6% -> 13%
where the time goes in v2:
time: 80 us; the launch traced here: 79.6 us
  starting transfers between devices  23.5 us (29%)
  blocking collectives  22.1 us (28%)
  Pallas kernels  18.9 us (24%)
  waiting for transfers between devices  14 us (18%)
  other arithmetic  0.97 us (1%)
    all_to_all x1, blocking collectives, local(): lax.all_to_all(lines, EVERY, split_axis=0, concat_axis=0, tiled=True)  22.1 us
    pallas_call x4, Pallas kernels, density_part(): pl.pallas_call(density_body, out_shape=jax.ShapeDtypeStruct((SIDE, deep,...  13.5 us
    ppermute x6, starting transfers between devices, send(): return lax.ppermute(value, EVERY, pairs)  12.6 us
    ppermute x6, waiting for transfers between devices, send(): return lax.ppermute(value, EVERY, pairs)  7.1 us
    pallas_call x1, Pallas kernels, krylov(): pl.pallas_call(krylov_body, out_shape=(field, field, jax.ShapeDtypeStruct...  4.43 us
    ppermute x1, waiting for transfers between devices, halo(): high = lax.ppermute(field[:REACH], BAND, [(b, a) for a, b in band])  3.78 us
    ppermute x1, starting transfers between devices, halo(): near = lax.ppermute(jnp.where(first, right, left), SPACE, inside)  3.73 us
    ppermute x1, starting transfers between devices, halo(): far = lax.ppermute(jnp.where(first, left, right), SPACE, across)  3.1 us
  transfers between devices with their start and end apart: 10, of which 7 were waited for; matrix products, arithmetic and copies ran while one was open for 0% of the time, Pallas kernels for 13%

profile of v2, /device:TPU:1, one launch (start us, length us, event | category | flops | bytes accessed | tf_op | source)
XLA Modules:
  0.0 79.6 jit_solution(822090041542773638)
XLA Ops:
  0.0 0.7 broadcast_multiply_fusion.occ
  0.7 3.4 %density.5 = f32[4,8,40,128]{3,2,1,0:T(8,128)S(1)} custom-call(s32[16]{0:T(128)S(1)} %fusion.3.order, f32[8]{0:T(128)S(1)} %broadcast_multiply_fusion.occ, bf16[8,128,40,128]{3,2,1,0:T(8,128)(2,1)} %orb.7), custom_call_target="tpu_custom_call" | custom-call | bytes 2621440 | tf_op jit(solution)/shard_map/density/pallas_call | solution.py:56
  4.1 4.5 %collective-permute-start = (f32[4,8,40,128]{3,2,1,0:T(8,128)S(1)}, f32[4,8,40,128]{3,2,1,0:T(8,128)S(1)}, u32[]{:S(2)}, u32[]{:S(2)}) collective-permute-start(f32[4,8,40,128]{3,2,1,0:T(8,128)S(1)} %density.5), channel_id=1, source_target_pairs={{0,16},{1,65},{2,18},{3,67},{4,20},{5,69},{6,22},{7,71},{8,24},{9,... | collective-permute-start | bytes 1966088 | tf_op jit(solution)/shard_map/ppermute | solution.py:41
  8.6 3.4 %density.6 = f32[4,8,40,128]{3,2,1,0:T(8,128)S(1)} custom-call(s32[16]{0:T(128)S(1)} %fusion.3.order, f32[8]{0:T(128)S(1)} %broadcast_multiply_fusion.occ, bf16[8,128,40,128]{3,2,1,0:T(8,128)(2,1)} %orb.7), custom_call_target="tpu_custom_call" | custom-call | bytes 2621440 | tf_op jit(solution)/shard_map/density/pallas_call | solution.py:56
  12.0 0.8 %collective-permute-start.1 = (f32[4,8,40,128]{3,2,1,0:T(8,128)S(1)}, f32[4,8,40,128]{3,2,1,0:T(8,128)S(1)}, u32[]{:S(2)}, u32[]{:S(2)}) collective-permute-start(f32[4,8,40,128]{3,2,1,0:T(8,128)S(1)} %density.6), channel_id=1, source_target_pairs={{0,8},{1,33},{2,10},{3,35},{4,12},{5,37},{6,14},{7,39},{8,16},{9,4... | collective-permute-start | bytes 1966088 | tf_op jit(solution)/shard_map/ppermute | solution.py:41
  12.8 3.4 %density.7 = f32[4,8,40,128]{3,2,1,0:T(8,128)S(1)} custom-call(s32[16]{0:T(128)S(1)} %fusion.3.order, f32[8]{0:T(128)S(1)} %broadcast_multiply_fusion.occ, bf16[8,128,40,128]{3,2,1,0:T(8,128)(2,1)} %orb.7), custom_call_target="tpu_custom_call" | custom-call | bytes 2621440 | tf_op jit(solution)/shard_map/density/pallas_call | solution.py:56
  16.1 2.0 %collective-permute-start.2 = (f32[4,8,40,128]{3,2,1,0:T(8,128)S(1)}, f32[4,8,40,128]{3,2,1,0:T(8,128)S(1)}, u32[]{:S(2)}, u32[]{:S(2)}) collective-permute-start(f32[4,8,40,128]{3,2,1,0:T(8,128)S(1)} %density.7), channel_id=1, source_target_pairs={{0,24},{1,97},{2,26},{3,99},{4,28},{5,101},{6,30},{7,103},{8,0},{9... | collective-permute-start | bytes 1966088 | tf_op jit(solution)/shard_map/ppermute | solution.py:41
  18.2 3.4 %density.4 = f32[4,8,40,128]{3,2,1,0:T(8,128)S(1)} custom-call(s32[16]{0:T(128)S(1)} %fusion.3.order, f32[8]{0:T(128)S(1)} %broadcast_multiply_fusion.occ, bf16[8,128,40,128]{3,2,1,0:T(8,128)(2,1)} %orb.7), custom_call_target="tpu_custom_call" | custom-call | bytes 2621440 | tf_op jit(solution)/shard_map/density/pallas_call | solution.py:56
  21.5 0.0 collective-permute-done
  21.6 2.3 %collective-permute-done.1 = f32[4,8,40,128]{3,2,1,0:T(8,128)S(1)} collective-permute-done((f32[4,8,40,128]{3,2,1,0:T(8,128)S(1)}, f32[4,8,40,128]{3,2,1,0:T(8,128)S(1)}, u32[]{:S(2)}, u32[]{:S(2)}) %collective-permute-start.1) | collective-permute-done | bytes 655392 | tf_op jit(solution)/shard_map/ppermute | solution.py:41
  23.9 2.1 %collective-permute-done.2 = f32[4,8,40,128]{3,2,1,0:T(8,128)S(1)} collective-permute-done((f32[4,8,40,128]{3,2,1,0:T(8,128)S(1)}, f32[4,8,40,128]{3,2,1,0:T(8,128)S(1)}, u32[]{:S(2)}, u32[]{:S(2)}) %collective-permute-start.2) | collective-permute-done | bytes 655392 | tf_op jit(solution)/shard_map/ppermute | solution.py:41
  25.9 0.2 add_add_fusion
  26.2 2.6 %collective-permute-start.3 = (f32[8,40,128]{2,1,0:T(8,128)S(1)}, f32[8,40,128]{2,1,0:T(8,128)S(1)}, u32[]{:S(2)}, u32[]{:S(2)}) collective-permute-start(f32[8,40,128]{2,1,0:T(8,128)S(1)} %get-tuple-element.14), channel_id=1, source_target_pairs={{0,64},{1,17},{2,66},{3,19},{4,68},{5,21},{6,70},{7,23},{8,72},{9,... | collective-permute-start | bytes 491528 | tf_op jit(solution)/shard_map/ppermute | solution.py:41
  28.7 0.6 collective-permute-start.4
  29.3 2.1 %collective-permute-start.5 = (f32[8,40,128]{2,1,0:T(8,128)S(1)}, f32[8,40,128]{2,1,0:T(8,128)S(1)}, u32[]{:S(2)}, u32[]{:S(2)}) collective-permute-start(f32[8,40,128]{2,1,0:T(8,128)S(1)} %get-tuple-element.15), channel_id=1, source_target_pairs={{0,96},{1,25},{2,98},{3,27},{4,100},{5,29},{6,102},{7,31},{8,104},... | collective-permute-start | bytes 491528 | tf_op jit(solution)/shard_map/ppermute | solution.py:41
  31.4 0.5 collective-permute-done.3
  31.9 2.2 %collective-permute-done.4 = f32[8,40,128]{2,1,0:T(8,128)S(1)} collective-permute-done((f32[8,40,128]{2,1,0:T(8,128)S(1)}, f32[8,40,128]{2,1,0:T(8,128)S(1)}, u32[]{:S(2)}, u32[]{:S(2)}) %collective-permute-start.4) | collective-permute-done | bytes 163872 | tf_op jit(solution)/shard_map/ppermute | solution.py:41
  34.1 0.0 collective-permute-done.5
  34.2 2.8 %collective-permute-start.6 = (f32[6,40,128]{2,1,0:T(8,128)S(1)}, f32[6,40,128]{2,1,0:T(8,128)S(1)}, u32[]{:S(2)}, u32[]{:S(2)}) collective-permute-start(f32[6,40,128]{2,1,0:T(8,128)S(1)} %get-tuple-element.18), channel_id=1, source_target_pairs={{0,8},{8,16},{16,24},{24,32},{32,40},{40,48},{48,56},{56,64},{64,7... | collective-permute-start | bytes 368648 | tf_op jit(solution)/shard_map/ppermute | solution.py:97
  37.0 1.3 %collective-permute-start.7 = (f32[6,40,128]{2,1,0:T(8,128)S(1)}, f32[6,40,128]{2,1,0:T(8,128)S(1)}, u32[]{:S(2)}, u32[]{:S(2)}) collective-permute-start(f32[6,40,128]{2,1,0:T(8,128)S(1)} %get-tuple-element.17), channel_id=1, source_target_pairs={{8,0},{16,8},{24,16},{32,24},{40,32},{48,40},{56,48},{64,56},{72,6... | collective-permute-start | bytes 368648 | tf_op jit(solution)/shard_map/ppermute | solution.py:98
  38.3 0.5 collective-permute-done.6.low
  38.8 3.8 %collective-permute-done.7.high = f32[6,40,128]{2,1,0:T(8,128)S(1)} collective-permute-done((f32[6,40,128]{2,1,0:T(8,128)S(1)}, f32[6,40,128]{2,1,0:T(8,128)S(1)}, u32[]{:S(2)}, u32[]{:S(2)}) %collective-permute-start.7) | collective-permute-done | bytes 122912 | tf_op jit(solution)/shard_map/ppermute | solution.py:98
  42.6 3.7 %collective-permute-start.8 = (f32[20,6,128]{2,1,0:T(8,128)S(1)}, f32[20,6,128]{2,1,0:T(8,128)S(1)}, u32[]{:S(2)}, u32[]{:S(2)}) collective-permute-start(f32[20,6,128]{2,1,0:T(8,128)S(1)} %broadcast_select_fusion.1), channel_id=1, source_target_pairs={{0,1},{1,0},{2,3},{3,2},{4,5},{5,4},{6,7},{7,6},{8,9},{9,8},{10,11... | collective-permute-start | bytes 184328 | tf_op jit(solution)/shard_map/ppermute | solution.py:104
  46.4 3.1 %collective-permute-start.9 = (f32[20,6,128]{2,1,0:T(8,128)S(1)}, f32[20,6,128]{2,1,0:T(8,128)S(1)}, u32[]{:S(2)}, u32[]{:S(2)}) collective-permute-start(f32[20,6,128]{2,1,0:T(8,128)S(1)} %get-tuple-element.11), channel_id=1, source_target_pairs={{1,2},{2,1},{3,4},{4,3},{5,6},{6,5},{9,10},{10,9},{11,12},{12,11},... | collective-permute-start | bytes 184328 | tf_op jit(solution)/shard_map/ppermute | solution.py:105
  49.5 0.1 pad_add_fusion.place
  49.6 0.0 collective-permute-done.8.near
  49.6 2.6 %collective-permute-done.9.far = f32[20,6,128]{2,1,0:T(8,128)S(1)} collective-permute-done((f32[20,6,128]{2,1,0:T(8,128)S(1)}, f32[20,6,128]{2,1,0:T(8,128)S(1)}, u32[]{:S(2)}, u32[]{:S(2)}) %collective-permute-start.9) | collective-permute-done | bytes 61472 | tf_op jit(solution)/shard_map/ppermute | solution.py:105
  52.1 4.4 %krylov.1 = (f32[8,40,128]{2,1,0:T(8,128)S(1)}, f32[8,40,128]{2,1,0:T(8,128)S(1)}, f32[128,1,128]{2,1,0:T(1,128)S(1)}) custom-call(s32[3]{0:T(128)S(1)} %pad_add_fusion.place, f32[8,40,128]{2,1,0:T(8,128)S(1)} %fusion.2.own, f32[6,40,128]{2,1,0:T(8,128)S(1)} %collective-permute-done.6.low, f32[6,40,128]{2,1,0:T(8,128)S(1)} %collective-permute-done.7.high, ...), custom_call_target="tpu_custom_call" | custom-call | tf_op jit(solution)/shard_map/krylov/pallas_call | solution.py:195
  56.6 22.1 %all_to_all.5.lines = f32[128,1,128]{2,1,0:T(1,128)S(1)} all-to-all(f32[128,1,128]{2,1,0:T(1,128)S(1)} %get-tuple-element.8), channel_id=1, replica_groups=mesh['band_0'=4,'band_1'=4,'space_0'=4,'space_1'=2] {'band_0','band_1','..., dimensions={0} | all-to-all | bytes 131072 | tf_op jit(solution)/shard_map/all_to_all | solution.py:254
  78.6 1.0 %combine.1 = f32[8,40,128]{2,1,0:T(8,128)} custom-call(f32[128,1,128]{2,1,0:T(1,128)S(1)} %all_to_all.5.lines, f32[8,40,128]{2,1,0:T(8,128)S(1)} %fusion.2.own, f32[8,40,128]{2,1,0:T(8,128)S(1)} %get-tuple-element.9.first, f32[8,40,128]{2,1,0:T(8,128)S(1)} %get-tuple-element.10.second), custom_call_target="tpu_custom_call" | custom-call | tf_op jit(solution)/shard_map/combine/pallas_call | solution.py:239
  (6 shorter events, 0.1 us)
Async XLA Ops:
  4.1 17.5 %collective-permute-start = (f32[4,8,40,128]{3,2,1,0:T(8,128)S(1)}, f32[4,8,40,128]{3,2,1,0:T(8,128)S(1)}, u32[]{:S(2)}, u32[]{:S(2)}) collective-permute-start(f32[4,8,40,128]{3,2,1,0:T(8,128)S(1)} %density.5), channel_id=1, source_target_pairs={{0,16},{1,65},{2,18},{3,67},{4,20},{5,69},{6,22},{7,71},{8,24},{9,... | collective-permute-start | bytes 1966088 | tf_op jit(solution)/shard_map/ppermute | solution.py:41
  12.0 11.9 %collective-permute-start.1 = (f32[4,8,40,128]{3,2,1,0:T(8,128)S(1)}, f32[4,8,40,128]{3,2,1,0:T(8,128)S(1)}, u32[]{:S(2)}, u32[]{:S(2)}) collective-permute-start(f32[4,8,40,128]{3,2,1,0:T(8,128)S(1)} %density.6), channel_id=1, source_target_pairs={{0,8},{1,33},{2,10},{3,35},{4,12},{5,37},{6,14},{7,39},{8,16},{9,4... | collective-permute-start | bytes 1966088 | tf_op jit(solution)/shard_map/ppermute | solution.py:41
  16.1 9.8 %collective-permute-start.2 = (f32[4,8,40,128]{3,2,1,0:T(8,128)S(1)}, f32[4,8,40,128]{3,2,1,0:T(8,128)S(1)}, u32[]{:S(2)}, u32[]{:S(2)}) collective-permute-start(f32[4,8,40,128]{3,2,1,0:T(8,128)S(1)} %density.7), channel_id=1, source_target_pairs={{0,24},{1,97},{2,26},{3,99},{4,28},{5,101},{6,30},{7,103},{8,0},{9... | collective-permute-start | bytes 1966088 | tf_op jit(solution)/shard_map/ppermute | solution.py:41
  26.2 5.8 %collective-permute-start.3 = (f32[8,40,128]{2,1,0:T(8,128)S(1)}, f32[8,40,128]{2,1,0:T(8,128)S(1)}, u32[]{:S(2)}, u32[]{:S(2)}) collective-permute-start(f32[8,40,128]{2,1,0:T(8,128)S(1)} %get-tuple-element.14), channel_id=1, source_target_pairs={{0,64},{1,17},{2,66},{3,19},{4,68},{5,21},{6,70},{7,23},{8,72},{9,... | collective-permute-start | bytes 491528 | tf_op jit(solution)/shard_map/ppermute | solution.py:41
  28.7 5.4 %collective-permute-start.4 = (f32[8,40,128]{2,1,0:T(8,128)S(1)}, f32[8,40,128]{2,1,0:T(8,128)S(1)}, u32[]{:S(2)}, u32[]{:S(2)}) collective-permute-start(f32[8,40,128]{2,1,0:T(8,128)S(1)} %get-tuple-element.16), channel_id=1, source_target_pairs={{0,32},{1,9},{2,34},{3,11},{4,36},{5,13},{6,38},{7,15},{8,40},{9,1... | collective-permute-start | bytes 491528 | tf_op jit(solution)/shard_map/ppermute | solution.py:41
  29.3 4.8 %collective-permute-start.5 = (f32[8,40,128]{2,1,0:T(8,128)S(1)}, f32[8,40,128]{2,1,0:T(8,128)S(1)}, u32[]{:S(2)}, u32[]{:S(2)}) collective-permute-start(f32[8,40,128]{2,1,0:T(8,128)S(1)} %get-tuple-element.15), channel_id=1, source_target_pairs={{0,96},{1,25},{2,98},{3,27},{4,100},{5,29},{6,102},{7,31},{8,104},... | collective-permute-start | bytes 491528 | tf_op jit(solution)/shard_map/ppermute | solution.py:41
  34.2 4.7 %collective-permute-start.6 = (f32[6,40,128]{2,1,0:T(8,128)S(1)}, f32[6,40,128]{2,1,0:T(8,128)S(1)}, u32[]{:S(2)}, u32[]{:S(2)}) collective-permute-start(f32[6,40,128]{2,1,0:T(8,128)S(1)} %get-tuple-element.18), channel_id=1, source_target_pairs={{0,8},{8,16},{16,24},{24,32},{32,40},{40,48},{48,56},{56,64},{64,7... | collective-permute-start | bytes 368648 | tf_op jit(solution)/shard_map/ppermute | solution.py:97
  37.0 5.6 %collective-permute-start.7 = (f32[6,40,128]{2,1,0:T(8,128)S(1)}, f32[6,40,128]{2,1,0:T(8,128)S(1)}, u32[]{:S(2)}, u32[]{:S(2)}) collective-permute-start(f32[6,40,128]{2,1,0:T(8,128)S(1)} %get-tuple-element.17), channel_id=1, source_target_pairs={{8,0},{16,8},{24,16},{32,24},{40,32},{48,40},{56,48},{64,56},{72,6... | collective-permute-start | bytes 368648 | tf_op jit(solution)/shard_map/ppermute | solution.py:98
  42.6 6.9 %collective-permute-start.8 = (f32[20,6,128]{2,1,0:T(8,128)S(1)}, f32[20,6,128]{2,1,0:T(8,128)S(1)}, u32[]{:S(2)}, u32[]{:S(2)}) collective-permute-start(f32[20,6,128]{2,1,0:T(8,128)S(1)} %broadcast_select_fusion.1), channel_id=1, source_target_pairs={{0,1},{1,0},{2,3},{3,2},{4,5},{5,4},{6,7},{7,6},{8,9},{9,8},{10,11... | collective-permute-start | bytes 184328 | tf_op jit(solution)/shard_map/ppermute | solution.py:104
  46.4 5.7 %collective-permute-start.9 = (f32[20,6,128]{2,1,0:T(8,128)S(1)}, f32[20,6,128]{2,1,0:T(8,128)S(1)}, u32[]{:S(2)}, u32[]{:S(2)}) collective-permute-start(f32[20,6,128]{2,1,0:T(8,128)S(1)} %get-tuple-element.11), channel_id=1, source_target_pairs={{1,2},{2,1},{3,4},{4,3},{5,6},{6,5},{9,10},{10,9},{11,12},{12,11},... | collective-permute-start | bytes 184328 | tf_op jit(solution)/shard_map/ppermute | solution.py:105

commit v3 on v2

v3 whole, which is shorter than its diff:
```python
import functools
import math

import jax
import jax.numpy as jnp
from jax import lax
from jax.experimental import pallas as pl
from jax.experimental.pallas import tpu as pltpu
from jax.sharding import Mesh
from jax.sharding import PartitionSpec as P


ITERS = 3
REACH = 2 * ITERS
BAND = ("band_0", "band_1")
SPACE = ("space_0", "space_1")
EVERY = BAND + SPACE
SIDE = 4
F32 = jnp.float32


def device(z, x, y, core):
    return ((z * SIDE + x) * SIDE + y) * 2 + core


def moves(target):
    places = [(z, x, y, c) for z in range(SIDE) for x in range(SIDE) for y in range(SIDE) for c in range(2)]
    return [(device(*p), device(*target(*p))) for p in places]


def partner(phase, k):
    def target(z, x, y, c):
        if (c == 0) == (phase == 0):
            return z, x ^ k, y, c
        return z ^ k, x, y, c

    return moves(target)


def send(value, pairs):
    return lax.ppermute(value, EVERY, pairs)


def density_body(first, scale, orb, occ, out, held, level, arrive, ready):
    z, x, core = lax.axis_index("band_0"), lax.axis_index("band_1"), lax.axis_index("space_1")
    bands, deep = held.shape[1], held.shape[2]
    weights = pltpu.make_async_copy(occ, level, ready)
    weights.start()
    copies = []
    for second in range(SIDE):
        to_z = z ^ jnp.where(core == 0, second, first)
        to_x = x ^ jnp.where(core == 0, first, second)
        row = (to_z * SIDE + to_x) * deep
        copies.append(pltpu.make_async_copy(orb.at[:, pl.ds(row, deep)], held.at[second], arrive.at[second]))
        copies[-1].start()
    weights.wait()
    factor = [level[b] * scale for b in range(bands)]
    for second in range(SIDE):
        copies[second].wait()

        def row(r, carry):
            total = None
            for b in range(bands):
                wave = held[second, b, r].astype(F32)
                term = factor[b] * wave * wave
                total = term if total is None else total + term
            out[second, r] = total
            return carry

        lax.fori_loop(0, deep, row, 0)


def density_part(orbitals, occupations, scale, first):
    bands, rows, cols, lanes = orbitals.shape
    deep = rows // 16
    return pl.pallas_call(
        functools.partial(density_body, first, scale),
        out_shape=jax.ShapeDtypeStruct((SIDE, deep, cols, lanes), F32),
        in_specs=[pl.BlockSpec(memory_space=pl.ANY), pl.BlockSpec(memory_space=pltpu.HBM)],
        out_specs=pl.BlockSpec(memory_space=pltpu.VMEM),
        scratch_shapes=[
            pltpu.VMEM((SIDE, bands, deep, cols, lanes), orbitals.dtype),
            pltpu.SMEM((bands,), F32),
            pltpu.SemaphoreType.DMA((SIDE,)),
            pltpu.SemaphoreType.DMA,
        ],
        compiler_params=pltpu.CompilerParams(vmem_limit_bytes=52 * 2**20),
        cost_estimate=pl.CostEstimate(flops=0, bytes_accessed=orbitals.size // 2, transcendentals=0),
        name="density",
    )(orbitals, occupations)


def own_density(orbitals, occupations, scale):
    part = [None] * SIDE
    arrived = []
    for k in (2, 1, 3):
        part[k] = density_part(orbitals, occupations, scale, k)
        arrived.append(send(part[k], partner(0, k)))
    mine = density_part(orbitals, occupations, scale, 0)
    for other in arrived:
        mine = mine + other
    total = mine[0]
    for other in [send(mine[k], partner(1, k)) for k in (2, 1, 3)]:
        total = total + other
    return total


def across(y, core):
    space = 2 * y + core
    space = space + 1 if core else space - 1
    return (space // 2, space % 2) if 0 <= space < 8 else None


def beside():
    pairs = []
    for z in range(SIDE):
        for x in range(SIDE):
            for y in range(SIDE):
                for c in range(2):
                    if across(y, c) is not None:
                        pairs.append((device(z, x, y, c), device(z, x, *across(y, c))))
    return pairs


def halo(field):
    first = lax.axis_index("space_1") == 0
    left, right = field[:, :REACH], field[:, -REACH:]
    far = send(jnp.where(first, left, right), beside())
    near = lax.ppermute(jnp.where(first, right, left), "space_1", [(0, 1), (1, 0)])
    left, right = jnp.where(first, far, near), jnp.where(first, near, far)
    wide = jnp.concatenate([left, field, right], 1)
    even = lax.axis_index("band_1") % 2 == 0
    inner, outer = [(i, i ^ 1) for i in range(16)], []
    for i in range(1, 15, 2):
        outer += [(i, i + 1), (i + 1, i)]
    first_rows, last_rows = wide[:REACH], wide[-REACH:]
    inner = lax.ppermute(jnp.where(even, last_rows, first_rows), BAND, inner)
    outer = lax.ppermute(jnp.where(even, first_rows, last_rows), BAND, outer)
    return left, right, inner, outer


def laplacian(ref, r, start, size, masks):
    def at(row, shift):
        return ref[row, start + shift : start + shift + size]

    center = at(r, 0)
    lanes = center.shape[1]

    def along(k):
        return jnp.where(masks[k], pltpu.roll(center, -k % lanes, 1), 0.0)

    near = at(r + 1, 0) + at(r - 1, 0) + at(r, 1) + at(r, -1) + along(1) + along(-1)
    distant = at(r + 2, 0) + at(r - 2, 0) + at(r, 2) + at(r, -2) + along(2) + along(-2)
    return 7.5 * center - 4.0 / 3.0 * near + 1.0 / 12.0 * distant


PAD = 8


def krylov_body(own, left, right, inner, outer, first_out, second_out, lines, zero, one, two):
    rows, cols, lanes = own.shape
    deep = rows + 2 * REACH
    band, space = lax.axis_index(BAND), lax.axis_index(SPACE)
    wide = slice(PAD - REACH, PAD + cols + REACH)
    zero[REACH : REACH + rows, PAD : PAD + cols] = own[...]
    zero[REACH : REACH + rows, PAD - REACH : PAD] = left[...]
    zero[REACH : REACH + rows, PAD + cols : PAD + cols + REACH] = right[...]

    @pl.when(band % 2 == 0)
    def _():
        zero[0:REACH, wide] = outer[...]
        zero[REACH + rows : deep, wide] = inner[...]

    @pl.when(band % 2 == 1)
    def _():
        zero[0:REACH, wide] = inner[...]
        zero[REACH + rows : deep, wide] = outer[...]

    def masks(size):
        lane = lax.broadcasted_iota(jnp.int32, (size, lanes), 1)
        return {1: lane < lanes - 1, -1: lane >= 1, 2: lane < lanes - 2, -2: lane >= 2}

    def advance(source, target, edge):
        start = PAD - REACH + edge
        size = cols + 2 * (REACH - edge)
        inside = masks(size)
        col = lax.broadcasted_iota(jnp.int32, (size, lanes), 0) + (space * cols + start - PAD)
        col_in = (col >= 0) & (col < 8 * cols)

        def step(i, carry):
            for j in range(4):
                r = edge + 4 * i + j
                row = band * rows + (r - REACH)
                row_in = (row >= 0) & (row < 16 * rows)
                image = laplacian(source, r, start, size, inside)
                target[r, start : start + size] = jnp.where(col_in & row_in, image, 0.0)
            return carry

        lax.fori_loop(0, (deep - 2 * edge) // 4, step, 0)

    advance(zero, one, 2)
    advance(one, two, 4)
    inside = masks(cols)

    def fold(p, q):
        product = p * q
        return functools.reduce(lambda a, b: a + b, [product[i : i + 8] for i in range(0, cols, 8)])

    def gather(i, sums):
        for j in range(4):
            r = 4 * i + j
            at = r + REACH
            s0 = zero[at, PAD : PAD + cols]
            s1 = one[at, PAD : PAD + cols]
            s2 = two[at, PAD : PAD + cols]
            s3 = laplacian(two, at, PAD, cols, inside)
            first_out[r] = s1
            second_out[r] = s2
            pairs = ((s0, s0), (s0, s1), (s1, s1), (s1, s2), (s2, s2), (s2, s3))
            sums = tuple(t + fold(p, q) for t, (p, q) in zip(sums, pairs))
        return sums

    sums = lax.fori_loop(0, rows // 4, gather, tuple(jnp.zeros((8, lanes), F32) for _ in range(2 * ITERS)))
    spot = lax.broadcasted_iota(jnp.int32, (1, lanes), 1)
    line = jnp.zeros((1, lanes), F32)
    for k, part in enumerate(sums):
        whole = jnp.sum(jnp.sum(part, axis=0, keepdims=True), axis=1, keepdims=True)
        line = line + jnp.where(spot == k, whole, 0.0)
    lines[...] = jnp.broadcast_to(line[None], lines.shape)


def krylov(own, pieces):
    rows, cols, lanes = own.shape
    scratch = pltpu.VMEM((rows + 2 * REACH, cols + 2 * PAD, lanes), F32)
    vmem = pl.BlockSpec(memory_space=pltpu.VMEM)
    field = jax.ShapeDtypeStruct(own.shape, F32)
    return pl.pallas_call(
        krylov_body,
        out_shape=(field, field, jax.ShapeDtypeStruct((128, 1, lanes), F32)),
        in_specs=[vmem] * (1 + len(pieces)),
        out_specs=(vmem, vmem, vmem),
        scratch_shapes=[scratch, scratch, scratch],
        compiler_params=pltpu.CompilerParams(vmem_limit_bytes=8 * 2**20),
        name="krylov",
    )(own, *pieces)


def weights_of(moments):
    unit = [m / moments[0] * 0.125**k for k, m in enumerate(moments)]

    def inner(a, b, shift):
        terms = [x * y * unit[i + j + shift] for i, x in enumerate(a) for j, y in enumerate(b)]
        return functools.reduce(lambda p, q: p + q, terms)

    residual, direction, answer = [1.0], [1.0], []
    norm = unit[0]
    for step in range(ITERS):
        alpha = norm / inner(direction, direction, 1)
        old = answer + [0.0] * (len(direction) - len(answer))
        answer = [a + alpha * d for a, d in zip(old, direction)]
        if step + 1 < ITERS:
            residual = [r - alpha * d for r, d in zip(residual + [0.0], [0.0] + direction)]
            fresh = inner(residual, residual, 0)
            ratio = fresh / norm
            direction = [r + ratio * d for r, d in zip(residual, direction + [0.0])]
            norm = fresh
    return [a * 0.125 ** (k + 1) for k, a in enumerate(answer)]


def combine_body(lines, own, first, second, out):
    line = jnp.sum(lines[...], axis=0)
    spot = lax.broadcasted_iota(jnp.int32, line.shape, 1)
    moments = [jnp.sum(jnp.where(spot == k, line, 0.0), axis=1, keepdims=True) for k in range(2 * ITERS)]
    factors = [jnp.broadcast_to(f, own.shape[1:]) for f in weights_of(moments)]
    for r in range(own.shape[0]):
        out[r] = factors[0] * own[r] + factors[1] * first[r] + factors[2] * second[r]


def combine(lines, own, first, second):
    vmem = pl.BlockSpec(memory_space=pltpu.VMEM)
    return pl.pallas_call(
        combine_body,
        out_shape=jax.ShapeDtypeStruct(own.shape, F32),
        in_specs=[vmem] * 4,
        out_specs=vmem,
        compiler_params=pltpu.CompilerParams(vmem_limit_bytes=8 * 2**20),
        name="combine",
    )(lines, own, first, second)


def local(orbitals, occupations):
    scale = 4.0 * math.pi / (orbitals.shape[0] * 16)
    source = own_density(orbitals, occupations, scale)
    first, second, lines = krylov(source, halo(source))
    lines = lax.all_to_all(lines, EVERY, split_axis=0, concat_axis=0, tiled=True)
    return combine(lines, source, first, second)


def solution(mesh):
    split = Mesh(mesh.devices.reshape(SIDE, SIDE, SIDE, 2), EVERY)
    in_specs = (P(BAND, None, SPACE, None), P(BAND))
    out_specs = P(BAND, SPACE, None)
    return jax.shard_map(local, mesh=split, in_specs=in_specs, out_specs=out_specs, check_vma=False)
```

time: 80 us -> 70.4 us (0.88)
  Pallas kernels: 18.9 us -> 10.7 us
  starting transfers between devices: 23.5 us -> 17.4 us
  waiting for transfers between devices: 14 us -> 20 us
  blocking collectives: 22.1 us -> 20.9 us
    ppermute x4 -> x3, starting transfers between devices: 10.9 us -> 1.6 us  [the longest x1 0.85 us: halo(): inner = lax.ppermute(jnp.where(even, last_rows, first_rows), BAND, inner)]
    ppermute x6 -> x7, waiting for transfers between devices: 7.1 us -> 15.3 us  [send(): return lax.ppermute(value, EVERY, pairs)]
    pallas_call x4, Pallas kernels: 13.5 us -> 8.05 us  [density_part(): pl.pallas_call(functools.partial(density_body, first, scale), out_shape=j...]
    ppermute x6 -> x7, starting transfers between devices: 12.6 us -> 15.8 us  [send(): return lax.ppermute(value, EVERY, pairs)]
    pallas_call x1, Pallas kernels: 4.43 us -> 1.71 us  [krylov(): pl.pallas_call(krylov_body, out_shape=(field, field, jax.ShapeDtypeStruct...]
    ppermute x4 -> x3, waiting for transfers between devices: 6.86 us -> 4.64 us  [the longest x1 4.63 us: halo(): inner = lax.ppermute(jnp.where(even, last_rows, first_rows), BAND, inner)]
    all_to_all x1, blocking collectives: 22.1 us -> 20.9 us  [local(): lax.all_to_all(lines, EVERY, split_axis=0, concat_axis=0, tiled=True)]
  transfers between devices with their start and end apart: 10 -> 10, of which waited for: 7 -> 7; matrix products, arithmetic and copies ran while one was open for 0% -> 0% of each run, Pallas kernels for 13% -> 9%
where the time goes in v3:
time: 70.4 us; the launch traced here: 70.1 us
  blocking collectives  20.9 us (30%)
  waiting for transfers between devices  20 us (28%)
  starting transfers between devices  17.4 us (25%)
  Pallas kernels  10.7 us (15%)
    all_to_all x1, blocking collectives, local(): lax.all_to_all(lines, EVERY, split_axis=0, concat_axis=0, tiled=True)  20.9 us
    ppermute x7, starting transfers between devices, send(): return lax.ppermute(value, EVERY, pairs)  15.8 us
    ppermute x7, waiting for transfers between devices, send(): return lax.ppermute(value, EVERY, pairs)  15.3 us
    pallas_call x4, Pallas kernels, density_part(): pl.pallas_call(functools.partial(density_body, first, scale), out_shape=j...  8.05 us
    ppermute x1, waiting for transfers between devices, halo(): inner = lax.ppermute(jnp.where(even, last_rows, first_rows), BAND, inner)  4.63 us
    pallas_call x1, Pallas kernels, krylov(): pl.pallas_call(krylov_body, out_shape=(field, field, jax.ShapeDtypeStruct...  1.71 us
  transfers between devices with their start and end apart: 10, of which 7 were waited for; matrix products, arithmetic and copies ran while one was open for 0% of the time, Pallas kernels for 9%

profile of v3, /device:TPU:1, one launch (start us, length us, event | category | flops | bytes accessed | tf_op | source)
XLA Modules:
  0.0 70.1 jit_solution(6772431038986966874)
XLA Ops:
  0.0 0.0 copy-start
  0.0 0.7 copy-done
  0.7 2.0 %density.5 = f32[4,8,40,128]{3,2,1,0:T(8,128)S(1)} custom-call(bf16[8,128,40,128]{3,2,1,0:T(8,128)(2,1)} %orb.7, f32[8]{0:T(128)S(1)} %copy-done), custom_call_target="tpu_custom_call" | custom-call | bytes 2621440 | tf_op jit(solution)/shard_map/density/pallas_call | solution.py:76
  2.7 4.5 %collective-permute-start = (f32[4,8,40,128]{3,2,1,0:T(8,128)S(1)}, f32[4,8,40,128]{3,2,1,0:T(8,128)S(1)}, u32[]{:S(2)}, u32[]{:S(2)}) collective-permute-start(f32[4,8,40,128]{3,2,1,0:T(8,128)S(1)} %density.5), channel_id=1, source_target_pairs={{0,16},{1,65},{2,18},{3,67},{4,20},{5,69},{6,22},{7,71},{8,24},{9,... | collective-permute-start | bytes 1966088 | tf_op jit(solution)/shard_map/ppermute | solution.py:41
  7.2 2.0 %density.6 = f32[4,8,40,128]{3,2,1,0:T(8,128)S(1)} custom-call(bf16[8,128,40,128]{3,2,1,0:T(8,128)(2,1)} %orb.7, f32[8]{0:T(128)S(1)} %copy-done), custom_call_target="tpu_custom_call" | custom-call | bytes 2621440 | tf_op jit(solution)/shard_map/density/pallas_call | solution.py:76
  9.2 0.8 %collective-permute-start.1 = (f32[4,8,40,128]{3,2,1,0:T(8,128)S(1)}, f32[4,8,40,128]{3,2,1,0:T(8,128)S(1)}, u32[]{:S(2)}, u32[]{:S(2)}) collective-permute-start(f32[4,8,40,128]{3,2,1,0:T(8,128)S(1)} %density.6), channel_id=1, source_target_pairs={{0,8},{1,33},{2,10},{3,35},{4,12},{5,37},{6,14},{7,39},{8,0},{9,41... | collective-permute-start | bytes 1966088 | tf_op jit(solution)/shard_map/ppermute | solution.py:41
  10.0 2.0 %density.7 = f32[4,8,40,128]{3,2,1,0:T(8,128)S(1)} custom-call(bf16[8,128,40,128]{3,2,1,0:T(8,128)(2,1)} %orb.7, f32[8]{0:T(128)S(1)} %copy-done), custom_call_target="tpu_custom_call" | custom-call | bytes 2621440 | tf_op jit(solution)/shard_map/density/pallas_call | solution.py:76
  12.0 0.1 collective-permute-start.2
  12.1 2.0 %density.4 = f32[4,8,40,128]{3,2,1,0:T(8,128)S(1)} custom-call(bf16[8,128,40,128]{3,2,1,0:T(8,128)(2,1)} %orb.7, f32[8]{0:T(128)S(1)} %copy-done), custom_call_target="tpu_custom_call" | custom-call | bytes 2621440 | tf_op jit(solution)/shard_map/density/pallas_call | solution.py:76
  14.2 1.3 %collective-permute-done = f32[4,8,40,128]{3,2,1,0:T(8,128)S(1)} collective-permute-done((f32[4,8,40,128]{3,2,1,0:T(8,128)S(1)}, f32[4,8,40,128]{3,2,1,0:T(8,128)S(1)}, u32[]{:S(2)}, u32[]{:S(2)}) %collective-permute-start) | collective-permute-done | bytes 655392 | tf_op jit(solution)/shard_map/ppermute | solution.py:41
  15.5 7.8 %collective-permute-done.1 = f32[4,8,40,128]{3,2,1,0:T(8,128)S(1)} collective-permute-done((f32[4,8,40,128]{3,2,1,0:T(8,128)S(1)}, f32[4,8,40,128]{3,2,1,0:T(8,128)S(1)}, u32[]{:S(2)}, u32[]{:S(2)}) %collective-permute-start.1) | collective-permute-done | bytes 655392 | tf_op jit(solution)/shard_map/ppermute | solution.py:41
  23.2 0.0 collective-permute-done.2
  23.3 0.1 add_add_fusion
  23.4 2.6 %collective-permute-start.3 = (f32[8,40,128]{2,1,0:T(8,128)S(1)}, f32[8,40,128]{2,1,0:T(8,128)S(1)}, u32[]{:S(2)}, u32[]{:S(2)}) collective-permute-start(f32[8,40,128]{2,1,0:T(8,128)S(1)} %get-tuple-element.11), channel_id=1, source_target_pairs={{0,64},{1,17},{2,66},{3,19},{4,68},{5,21},{6,70},{7,23},{8,72},{9,... | collective-permute-start | bytes 491528 | tf_op jit(solution)/shard_map/ppermute | solution.py:41
  26.0 0.3 collective-permute-start.4
  26.3 0.6 collective-permute-start.5
  26.9 2.6 %collective-permute-done.3 = f32[8,40,128]{2,1,0:T(8,128)S(1)} collective-permute-done((f32[8,40,128]{2,1,0:T(8,128)S(1)}, f32[8,40,128]{2,1,0:T(8,128)S(1)}, u32[]{:S(2)}, u32[]{:S(2)}) %collective-permute-start.3) | collective-permute-done | bytes 163872 | tf_op jit(solution)/shard_map/ppermute | solution.py:41
  29.5 1.4 %collective-permute-done.4 = f32[8,40,128]{2,1,0:T(8,128)S(1)} collective-permute-done((f32[8,40,128]{2,1,0:T(8,128)S(1)}, f32[8,40,128]{2,1,0:T(8,128)S(1)}, u32[]{:S(2)}, u32[]{:S(2)}) %collective-permute-start.4) | collective-permute-done | bytes 163872 | tf_op jit(solution)/shard_map/ppermute | solution.py:41
  30.9 0.8 %collective-permute-done.5 = f32[8,40,128]{2,1,0:T(8,128)S(1)} collective-permute-done((f32[8,40,128]{2,1,0:T(8,128)S(1)}, f32[8,40,128]{2,1,0:T(8,128)S(1)}, u32[]{:S(2)}, u32[]{:S(2)}) %collective-permute-start.5) | collective-permute-done | bytes 163872 | tf_op jit(solution)/shard_map/ppermute | solution.py:41
  31.7 7.0 %collective-permute-start.6 = (f32[8,6,128]{2,1,0:T(8,128)S(1)}, f32[8,6,128]{2,1,0:T(8,128)S(1)}, u32[]{:S(2)}, u32[]{:S(2)}) collective-permute-start(f32[8,6,128]{2,1,0:T(8,128)S(1)} %get-tuple-element.17), channel_id=1, source_target_pairs={{1,2},{2,1},{3,4},{4,3},{5,6},{6,5},{9,10},{10,9},{11,12},{12,11},... | collective-permute-start | bytes 73736 | tf_op jit(solution)/shard_map/ppermute | solution.py:41
  38.7 0.1 collective-permute-start.7
  38.8 1.5 %collective-permute-done.6 = f32[8,6,128]{2,1,0:T(8,128)S(1)} collective-permute-done((f32[8,6,128]{2,1,0:T(8,128)S(1)}, f32[8,6,128]{2,1,0:T(8,128)S(1)}, u32[]{:S(2)}, u32[]{:S(2)}) %collective-permute-start.6) | collective-permute-done | bytes 24608 | tf_op jit(solution)/shard_map/ppermute | solution.py:41
  40.3 0.0 collective-permute-done.7
  40.4 0.9 %collective-permute-start.8 = (f32[6,52,128]{2,1,0:T(8,128)S(1)}, f32[6,52,128]{2,1,0:T(8,128)S(1)}, u32[]{:S(2)}, u32[]{:S(2)}) collective-permute-start(f32[6,52,128]{2,1,0:T(8,128)S(1)} %get-tuple-element.15), channel_id=1, source_target_pairs={{0,8},{8,0},{16,24},{24,16},{32,40},{40,32},{48,56},{56,48},{64,72... | collective-permute-start | bytes 479240 | tf_op jit(solution)/shard_map/ppermute | solution.py:137
  41.2 0.7 collective-permute-start.9
  41.9 4.6 %collective-permute-done.8.inner = f32[6,52,128]{2,1,0:T(8,128)S(1)} collective-permute-done((f32[6,52,128]{2,1,0:T(8,128)S(1)}, f32[6,52,128]{2,1,0:T(8,128)S(1)}, u32[]{:S(2)}, u32[]{:S(2)}) %collective-permute-start.8) | collective-permute-done | bytes 159776 | tf_op jit(solution)/shard_map/ppermute | solution.py:137
  46.5 0.0 collective-permute-done.9.outer
  46.5 1.7 %krylov.1 = (f32[8,40,128]{2,1,0:T(8,128)S(1)}, f32[8,40,128]{2,1,0:T(8,128)S(1)}, f32[128,1,128]{2,1,0:T(1,128)S(1)}) custom-call(f32[8,40,128]{2,1,0:T(8,128)S(1)} %fusion.2.own, f32[8,6,128]{2,1,0:T(8,128)S(1)} %get-tuple-element.19.left, f32[8,6,128]{2,1,0:T(8,128)S(1)} %get-tuple-element.18.right, f32[6,52,128]{2,1,0:T(8,128)S(1)} %collective-permute-done.8.inner, ...), custom_call_target="tpu_custom_call" | custom-call | tf_op jit(solution)/shard_map/krylov/pallas_call | solution.py:237
  48.2 20.9 %all_to_all.5.lines = f32[128,1,128]{2,1,0:T(1,128)S(1)} all-to-all(f32[128,1,128]{2,1,0:T(1,128)S(1)} %get-tuple-element.8), channel_id=1, replica_groups=mesh['band_0'=4,'band_1'=4,'space_0'=4,'space_1'=2] {'band_0','band_1','..., dimensions={0} | all-to-all | bytes 131072 | tf_op jit(solution)/shard_map/all_to_all | solution.py:295
  69.1 1.0 %combine.1 = f32[8,40,128]{2,1,0:T(8,128)} custom-call(f32[128,1,128]{2,1,0:T(1,128)S(1)} %all_to_all.5.lines, f32[8,40,128]{2,1,0:T(8,128)S(1)} %fusion.2.own, f32[8,40,128]{2,1,0:T(8,128)S(1)} %get-tuple-element.9.first, f32[8,40,128]{2,1,0:T(8,128)S(1)} %get-tuple-element.10.second), custom_call_target="tpu_custom_call" | custom-call | tf_op jit(solution)/shard_map/combine/pallas_call | solution.py:281
  (6 shorter events, 0.1 us)
Async XLA Ops:
  0.0 0.7 copy-start
  2.7 12.8 %collective-permute-start = (f32[4,8,40,128]{3,2,1,0:T(8,128)S(1)}, f32[4,8,40,128]{3,2,1,0:T(8,128)S(1)}, u32[]{:S(2)}, u32[]{:S(2)}) collective-permute-start(f32[4,8,40,128]{3,2,1,0:T(8,128)S(1)} %density.5), channel_id=1, source_target_pairs={{0,16},{1,65},{2,18},{3,67},{4,20},{5,69},{6,22},{7,71},{8,24},{9,... | collective-permute-start | bytes 1966088 | tf_op jit(solution)/shard_map/ppermute | solution.py:41
  9.2 14.1 %collective-permute-start.1 = (f32[4,8,40,128]{3,2,1,0:T(8,128)S(1)}, f32[4,8,40,128]{3,2,1,0:T(8,128)S(1)}, u32[]{:S(2)}, u32[]{:S(2)}) collective-permute-start(f32[4,8,40,128]{3,2,1,0:T(8,128)S(1)} %density.6), channel_id=1, source_target_pairs={{0,8},{1,33},{2,10},{3,35},{4,12},{5,37},{6,14},{7,39},{8,0},{9,41... | collective-permute-start | bytes 1966088 | tf_op jit(solution)/shard_map/ppermute | solution.py:41
  12.0 11.2 %collective-permute-start.2 = (f32[4,8,40,128]{3,2,1,0:T(8,128)S(1)}, f32[4,8,40,128]{3,2,1,0:T(8,128)S(1)}, u32[]{:S(2)}, u32[]{:S(2)}) collective-permute-start(f32[4,8,40,128]{3,2,1,0:T(8,128)S(1)} %density.7), channel_id=1, source_target_pairs={{0,24},{1,97},{2,26},{3,99},{4,28},{5,101},{6,30},{7,103},{8,16},{... | collective-permute-start | bytes 1966088 | tf_op jit(solution)/shard_map/ppermute | solution.py:41
  23.4 6.0 %collective-permute-start.3 = (f32[8,40,128]{2,1,0:T(8,128)S(1)}, f32[8,40,128]{2,1,0:T(8,128)S(1)}, u32[]{:S(2)}, u32[]{:S(2)}) collective-permute-start(f32[8,40,128]{2,1,0:T(8,128)S(1)} %get-tuple-element.11), channel_id=1, source_target_pairs={{0,64},{1,17},{2,66},{3,19},{4,68},{5,21},{6,70},{7,23},{8,72},{9,... | collective-permute-start | bytes 491528 | tf_op jit(solution)/shard_map/ppermute | solution.py:41
  26.0 4.9 %collective-permute-start.4 = (f32[8,40,128]{2,1,0:T(8,128)S(1)}, f32[8,40,128]{2,1,0:T(8,128)S(1)}, u32[]{:S(2)}, u32[]{:S(2)}) collective-permute-start(f32[8,40,128]{2,1,0:T(8,128)S(1)} %get-tuple-element.13), channel_id=1, source_target_pairs={{0,32},{1,9},{2,34},{3,11},{4,36},{5,13},{6,38},{7,15},{8,40},{9,1... | collective-permute-start | bytes 491528 | tf_op jit(solution)/shard_map/ppermute | solution.py:41
  26.3 5.4 %collective-permute-start.5 = (f32[8,40,128]{2,1,0:T(8,128)S(1)}, f32[8,40,128]{2,1,0:T(8,128)S(1)}, u32[]{:S(2)}, u32[]{:S(2)}) collective-permute-start(f32[8,40,128]{2,1,0:T(8,128)S(1)} %get-tuple-element.12), channel_id=1, source_target_pairs={{0,96},{1,25},{2,98},{3,27},{4,100},{5,29},{6,102},{7,31},{8,104},... | collective-permute-start | bytes 491528 | tf_op jit(solution)/shard_map/ppermute | solution.py:41
  31.7 8.6 %collective-permute-start.6 = (f32[8,6,128]{2,1,0:T(8,128)S(1)}, f32[8,6,128]{2,1,0:T(8,128)S(1)}, u32[]{:S(2)}, u32[]{:S(2)}) collective-permute-start(f32[8,6,128]{2,1,0:T(8,128)S(1)} %get-tuple-element.17), channel_id=1, source_target_pairs={{1,2},{2,1},{3,4},{4,3},{5,6},{6,5},{9,10},{10,9},{11,12},{12,11},... | collective-permute-start | bytes 73736 | tf_op jit(solution)/shard_map/ppermute | solution.py:41
  38.7 1.6 %collective-permute-start.7 = (f32[8,6,128]{2,1,0:T(8,128)S(1)}, f32[8,6,128]{2,1,0:T(8,128)S(1)}, u32[]{:S(2)}, u32[]{:S(2)}) collective-permute-start(f32[8,6,128]{2,1,0:T(8,128)S(1)} %get-tuple-element.16), channel_id=1, source_target_pairs={{0,1},{1,0},{2,3},{3,2},{4,5},{5,4},{6,7},{7,6},{8,9},{9,8},{10,11... | collective-permute-start | bytes 73736 | tf_op jit(solution)/shard_map/ppermute | solution.py:129
  40.4 6.2 %collective-permute-start.8 = (f32[6,52,128]{2,1,0:T(8,128)S(1)}, f32[6,52,128]{2,1,0:T(8,128)S(1)}, u32[]{:S(2)}, u32[]{:S(2)}) collective-permute-start(f32[6,52,128]{2,1,0:T(8,128)S(1)} %get-tuple-element.15), channel_id=1, source_target_pairs={{0,8},{8,0},{16,24},{24,16},{32,40},{40,32},{48,56},{56,48},{64,72... | collective-permute-start | bytes 479240 | tf_op jit(solution)/shard_map/ppermute | solution.py:137
  41.2 5.3 %collective-permute-start.9 = (f32[6,52,128]{2,1,0:T(8,128)S(1)}, f32[6,52,128]{2,1,0:T(8,128)S(1)}, u32[]{:S(2)}, u32[]{:S(2)}) collective-permute-start(f32[6,52,128]{2,1,0:T(8,128)S(1)} %get-tuple-element.14), channel_id=1, source_target_pairs={{8,16},{16,8},{24,32},{32,24},{40,48},{48,40},{56,64},{64,56},{72,... | collective-permute-start | bytes 479240 | tf_op jit(solution)/shard_map/ppermute | solution.py:138

commit v4 on v3

--- a/solution.py
+++ b/solution.py
@@ -107,8 +107,8 @@
 
 def across(y, core):
     space = 2 * y + core
-    space = space + 1 if core else space - 1
-    return (space // 2, space % 2) if 0 <= space < 8 else None
+    space = (space + 1 if core else space - 1) % 8
+    return space // 2, space % 2
 
 
 def beside():
@@ -117,8 +117,7 @@
         for x in range(SIDE):
             for y in range(SIDE):
                 for c in range(2):
-                    if across(y, c) is not None:
-                        pairs.append((device(z, x, y, c), device(z, x, *across(y, c))))
+                    pairs.append((device(z, x, y, c), device(z, x, *across(y, c))))
     return pairs
 
 
@@ -127,12 +126,13 @@
     left, right = field[:, :REACH], field[:, -REACH:]
     far = send(jnp.where(first, left, right), beside())
     near = lax.ppermute(jnp.where(first, right, left), "space_1", [(0, 1), (1, 0)])
+    space = lax.axis_index(SPACE)
+    far = jnp.where((space > 0) & (space < 7), far, 0.0)
     left, right = jnp.where(first, far, near), jnp.where(first, near, far)
     wide = jnp.concatenate([left, field, right], 1)
     even = lax.axis_index("band_1") % 2 == 0
-    inner, outer = [(i, i ^ 1) for i in range(16)], []
-    for i in range(1, 15, 2):
-        outer += [(i, i + 1), (i + 1, i)]
+    inner = [(i, i ^ 1) for i in range(16)]
+    outer = [(i, (i + 1 if i % 2 else i - 1) % 16) for i in range(16)]
     first_rows, last_rows = wide[:REACH], wide[-REACH:]
     inner = lax.ppermute(jnp.where(even, last_rows, first_rows), BAND, inner)
     outer = lax.ppermute(jnp.where(even, first_rows, last_rows), BAND, outer)
@@ -168,13 +168,13 @@
 
     @pl.when(band % 2 == 0)
     def _():
-        zero[0:REACH, wide] = outer[...]
+        zero[0:REACH, wide] = jnp.where(band > 0, outer[...], 0.0)
         zero[REACH + rows : deep, wide] = inner[...]
 
     @pl.when(band % 2 == 1)
     def _():
         zero[0:REACH, wide] = inner[...]
-        zero[REACH + rows : deep, wide] = outer[...]
+        zero[REACH + rows : deep, wide] = jnp.where(band < 15, outer[...], 0.0)
 
     def masks(size):
         lane = lax.broadcasted_iota(jnp.int32, (size, lanes), 1)
@@ -226,7 +226,7 @@
     for k, part in enumerate(sums):
         whole = jnp.sum(jnp.sum(part, axis=0, keepdims=True), axis=1, keepdims=True)
         line = line + jnp.where(spot == k, whole, 0.0)
-    lines[...] = jnp.broadcast_to(line[None], lines.shape)
+    lines[...] = jnp.broadcast_to(line, lines.shape)
 
 
 def krylov(own, pieces):
@@ -236,7 +236,7 @@
     field = jax.ShapeDtypeStruct(own.shape, F32)
     return pl.pallas_call(
         krylov_body,
-        out_shape=(field, field, jax.ShapeDtypeStruct((128, 1, lanes), F32)),
+        out_shape=(field, field, jax.ShapeDtypeStruct((128, lanes), F32)),
         in_specs=[vmem] * (1 + len(pieces)),
         out_specs=(vmem, vmem, vmem),
         scratch_shapes=[scratch, scratch, scratch],
@@ -268,7 +268,7 @@
 
 
 def combine_body(lines, own, first, second, out):
-    line = jnp.sum(lines[...], axis=0)
+    line = jnp.sum(lines[...], axis=0, keepdims=True)
     spot = lax.broadcasted_iota(jnp.int32, line.shape, 1)
     moments = [jnp.sum(jnp.where(spot == k, line, 0.0), axis=1, keepdims=True) for k in range(2 * ITERS)]
     factors = [jnp.broadcast_to(f, own.shape[1:]) for f in weights_of(moments)]
@@ -292,7 +292,7 @@
     scale = 4.0 * math.pi / (orbitals.shape[0] * 16)
     source = own_density(orbitals, occupations, scale)
     first, second, lines = krylov(source, halo(source))
-    lines = lax.all_to_all(lines, EVERY, split_axis=0, concat_axis=0, tiled=True)
+    lines = lax.all_to_all(lines[:, None], EVERY, split_axis=0, concat_axis=0, tiled=True)[:, 0]
     return combine(lines, source, first, second)
 
 

time: 70.4 us -> 67.9 us (0.964)
  blocking collectives: 20.9 us -> 18.1 us
    ppermute x1, waiting for transfers between devices: 0.01 us -> 4.09 us  [halo(): outer = lax.ppermute(jnp.where(even, first_rows, last_rows), BAND, outer)]
    ppermute x1, waiting for transfers between devices: 4.63 us -> 1.1 us  [halo(): inner = lax.ppermute(jnp.where(even, last_rows, first_rows), BAND, inner)]
    all_to_all x1, blocking collectives: 20.9 us -> 18.1 us  [local(): lax.all_to_all(lines[:, None], EVERY, split_axis=0, concat_axis=0, tiled=...]
    ppermute x7, starting transfers between devices: 15.8 us -> 14 us  [send(): return lax.ppermute(value, EVERY, pairs)]
    ppermute x1, starting transfers between devices: 0.66 us -> 2.38 us  [halo(): outer = lax.ppermute(jnp.where(even, first_rows, last_rows), BAND, outer)]
  transfers between devices with their start and end apart: 10 -> 10, of which waited for: 7 -> 8; matrix products, arithmetic and copies ran while one was open for 0% -> 0% of each run, Pallas kernels for 9% -> 9%
where the time goes in v4:
time: 67.9 us; the launch traced here: 67.6 us
  waiting for transfers between devices  20.7 us (30%)
  blocking collectives  18.1 us (27%)
  starting transfers between devices  17.3 us (25%)
  Pallas kernels  10.6 us (16%)
  local copies, waits for them, and re-layouts  0.69 us (1%)
    all_to_all x1, blocking collectives, local(): lax.all_to_all(lines[:, None], EVERY, split_axis=0, concat_axis=0, tiled=...  18.1 us
    ppermute x7, waiting for transfers between devices, send(): return lax.ppermute(value, EVERY, pairs)  15.5 us
    ppermute x7, starting transfers between devices, send(): return lax.ppermute(value, EVERY, pairs)  14 us
    pallas_call x4, Pallas kernels, density_part(): pl.pallas_call(functools.partial(density_body, first, scale), out_shape=j...  8.05 us
    ppermute x1, waiting for transfers between devices, halo(): outer = lax.ppermute(jnp.where(even, first_rows, last_rows), BAND, outer)  4.09 us
    ppermute x1, starting transfers between devices, halo(): outer = lax.ppermute(jnp.where(even, first_rows, last_rows), BAND, outer)  2.38 us
    pallas_call x1, Pallas kernels, krylov(): pl.pallas_call(krylov_body, out_shape=(field, field, jax.ShapeDtypeStruct...  1.68 us
  transfers between devices with their start and end apart: 10, of which 8 were waited for; matrix products, arithmetic and copies ran while one was open for 0% of the time, Pallas kernels for 9%

profile of v4, /device:TPU:1, one launch (start us, length us, event | category | flops | bytes accessed | tf_op | source)
XLA Modules:
  0.0 67.6 jit_solution(198935162664225997)
XLA Ops:
  0.0 0.0 copy-start
  0.0 0.7 copy-done
  0.7 2.0 %density.5 = f32[4,8,40,128]{3,2,1,0:T(8,128)S(1)} custom-call(bf16[8,128,40,128]{3,2,1,0:T(8,128)(2,1)} %orb.7, f32[8]{0:T(128)S(1)} %copy-done), custom_call_target="tpu_custom_call" | custom-call | bytes 2621440 | tf_op jit(solution)/shard_map/density/pallas_call | solution.py:76
  2.7 4.5 %collective-permute-start = (f32[4,8,40,128]{3,2,1,0:T(8,128)S(1)}, f32[4,8,40,128]{3,2,1,0:T(8,128)S(1)}, u32[]{:S(2)}, u32[]{:S(2)}) collective-permute-start(f32[4,8,40,128]{3,2,1,0:T(8,128)S(1)} %density.5), channel_id=1, source_target_pairs={{0,16},{1,65},{2,18},{3,67},{4,20},{5,69},{6,22},{7,71},{8,24},{9,... | collective-permute-start | bytes 1966088 | tf_op jit(solution)/shard_map/ppermute | solution.py:41
  7.2 2.0 %density.6 = f32[4,8,40,128]{3,2,1,0:T(8,128)S(1)} custom-call(bf16[8,128,40,128]{3,2,1,0:T(8,128)(2,1)} %orb.7, f32[8]{0:T(128)S(1)} %copy-done), custom_call_target="tpu_custom_call" | custom-call | bytes 2621440 | tf_op jit(solution)/shard_map/density/pallas_call | solution.py:76
  9.2 0.8 %collective-permute-start.1 = (f32[4,8,40,128]{3,2,1,0:T(8,128)S(1)}, f32[4,8,40,128]{3,2,1,0:T(8,128)S(1)}, u32[]{:S(2)}, u32[]{:S(2)}) collective-permute-start(f32[4,8,40,128]{3,2,1,0:T(8,128)S(1)} %density.6), channel_id=1, source_target_pairs={{0,8},{1,33},{2,10},{3,35},{4,12},{5,37},{6,14},{7,39},{8,0},{9,41... | collective-permute-start | bytes 1966088 | tf_op jit(solution)/shard_map/ppermute | solution.py:41
  10.0 2.0 %density.7 = f32[4,8,40,128]{3,2,1,0:T(8,128)S(1)} custom-call(bf16[8,128,40,128]{3,2,1,0:T(8,128)(2,1)} %orb.7, f32[8]{0:T(128)S(1)} %copy-done), custom_call_target="tpu_custom_call" | custom-call | bytes 2621440 | tf_op jit(solution)/shard_map/density/pallas_call | solution.py:76
  12.0 0.1 collective-permute-start.2
  12.1 2.0 %density.4 = f32[4,8,40,128]{3,2,1,0:T(8,128)S(1)} custom-call(bf16[8,128,40,128]{3,2,1,0:T(8,128)(2,1)} %orb.7, f32[8]{0:T(128)S(1)} %copy-done), custom_call_target="tpu_custom_call" | custom-call | bytes 2621440 | tf_op jit(solution)/shard_map/density/pallas_call | solution.py:76
  14.2 1.3 %collective-permute-done = f32[4,8,40,128]{3,2,1,0:T(8,128)S(1)} collective-permute-done((f32[4,8,40,128]{3,2,1,0:T(8,128)S(1)}, f32[4,8,40,128]{3,2,1,0:T(8,128)S(1)}, u32[]{:S(2)}, u32[]{:S(2)}) %collective-permute-start) | collective-permute-done | bytes 655392 | tf_op jit(solution)/shard_map/ppermute | solution.py:41
  15.5 7.8 %collective-permute-done.1 = f32[4,8,40,128]{3,2,1,0:T(8,128)S(1)} collective-permute-done((f32[4,8,40,128]{3,2,1,0:T(8,128)S(1)}, f32[4,8,40,128]{3,2,1,0:T(8,128)S(1)}, u32[]{:S(2)}, u32[]{:S(2)}) %collective-permute-start.1) | collective-permute-done | bytes 655392 | tf_op jit(solution)/shard_map/ppermute | solution.py:41
  23.2 0.0 collective-permute-done.2
  23.3 0.1 add_add_fusion
  23.4 2.6 %collective-permute-start.3 = (f32[8,40,128]{2,1,0:T(8,128)S(1)}, f32[8,40,128]{2,1,0:T(8,128)S(1)}, u32[]{:S(2)}, u32[]{:S(2)}) collective-permute-start(f32[8,40,128]{2,1,0:T(8,128)S(1)} %get-tuple-element.11), channel_id=1, source_target_pairs={{0,64},{1,17},{2,66},{3,19},{4,68},{5,21},{6,70},{7,23},{8,72},{9,... | collective-permute-start | bytes 491528 | tf_op jit(solution)/shard_map/ppermute | solution.py:41
  26.0 0.3 collective-permute-start.4
  26.3 0.6 collective-permute-start.5
  26.9 2.6 %collective-permute-done.3 = f32[8,40,128]{2,1,0:T(8,128)S(1)} collective-permute-done((f32[8,40,128]{2,1,0:T(8,128)S(1)}, f32[8,40,128]{2,1,0:T(8,128)S(1)}, u32[]{:S(2)}, u32[]{:S(2)}) %collective-permute-start.3) | collective-permute-done | bytes 163872 | tf_op jit(solution)/shard_map/ppermute | solution.py:41
  29.5 1.4 %collective-permute-done.4 = f32[8,40,128]{2,1,0:T(8,128)S(1)} collective-permute-done((f32[8,40,128]{2,1,0:T(8,128)S(1)}, f32[8,40,128]{2,1,0:T(8,128)S(1)}, u32[]{:S(2)}, u32[]{:S(2)}) %collective-permute-start.4) | collective-permute-done | bytes 163872 | tf_op jit(solution)/shard_map/ppermute | solution.py:41
  30.9 0.8 %collective-permute-done.5 = f32[8,40,128]{2,1,0:T(8,128)S(1)} collective-permute-done((f32[8,40,128]{2,1,0:T(8,128)S(1)}, f32[8,40,128]{2,1,0:T(8,128)S(1)}, u32[]{:S(2)}, u32[]{:S(2)}) %collective-permute-start.5) | collective-permute-done | bytes 163872 | tf_op jit(solution)/shard_map/ppermute | solution.py:41
  31.7 5.1 %collective-permute-start.6 = (f32[8,6,128]{2,1,0:T(8,128)S(1)}, f32[8,6,128]{2,1,0:T(8,128)S(1)}, u32[]{:S(2)}, u32[]{:S(2)}) collective-permute-start(f32[8,6,128]{2,1,0:T(8,128)S(1)} %get-tuple-element.16), channel_id=1, source_target_pairs={{0,7},{1,2},{2,1},{3,4},{4,3},{5,6},{6,5},{7,0},{8,15},{9,10},{10,... | collective-permute-start | bytes 73736 | tf_op jit(solution)/shard_map/ppermute | solution.py:41
  36.9 0.0 collective-permute-start.7
  36.9 1.6 %collective-permute-done.6 = f32[8,6,128]{2,1,0:T(8,128)S(1)} collective-permute-done((f32[8,6,128]{2,1,0:T(8,128)S(1)}, f32[8,6,128]{2,1,0:T(8,128)S(1)}, u32[]{:S(2)}, u32[]{:S(2)}) %collective-permute-start.6) | collective-permute-done | bytes 24608 | tf_op jit(solution)/shard_map/ppermute | solution.py:41
  38.5 0.0 collective-permute-done.7
  38.5 0.9 %collective-permute-start.8 = (f32[6,52,128]{2,1,0:T(8,128)S(1)}, f32[6,52,128]{2,1,0:T(8,128)S(1)}, u32[]{:S(2)}, u32[]{:S(2)}) collective-permute-start(f32[6,52,128]{2,1,0:T(8,128)S(1)} %get-tuple-element.15), channel_id=1, source_target_pairs={{0,8},{8,0},{16,24},{24,16},{32,40},{40,32},{48,56},{56,48},{64,72... | collective-permute-start | bytes 479240 | tf_op jit(solution)/shard_map/ppermute | solution.py:137
  39.4 2.4 %collective-permute-start.9 = (f32[6,52,128]{2,1,0:T(8,128)S(1)}, f32[6,52,128]{2,1,0:T(8,128)S(1)}, u32[]{:S(2)}, u32[]{:S(2)}) collective-permute-start(f32[6,52,128]{2,1,0:T(8,128)S(1)} %get-tuple-element.14), channel_id=1, source_target_pairs={{0,120},{8,16},{16,8},{24,32},{32,24},{40,48},{48,40},{56,64},{64,... | collective-permute-start | bytes 479240 | tf_op jit(solution)/shard_map/ppermute | solution.py:138
  41.8 1.1 %collective-permute-done.8.inner = f32[6,52,128]{2,1,0:T(8,128)S(1)} collective-permute-done((f32[6,52,128]{2,1,0:T(8,128)S(1)}, f32[6,52,128]{2,1,0:T(8,128)S(1)}, u32[]{:S(2)}, u32[]{:S(2)}) %collective-permute-start.8) | collective-permute-done | bytes 159776 | tf_op jit(solution)/shard_map/ppermute | solution.py:137
  42.9 4.1 %collective-permute-done.9.outer = f32[6,52,128]{2,1,0:T(8,128)S(1)} collective-permute-done((f32[6,52,128]{2,1,0:T(8,128)S(1)}, f32[6,52,128]{2,1,0:T(8,128)S(1)}, u32[]{:S(2)}, u32[]{:S(2)}) %collective-permute-start.9) | collective-permute-done | bytes 159776 | tf_op jit(solution)/shard_map/ppermute | solution.py:138
  47.0 1.7 %krylov.1 = (f32[8,40,128]{2,1,0:T(8,128)S(1)}, f32[8,40,128]{2,1,0:T(8,128)S(1)}, f32[128,128]{1,0:T(8,128)S(1)}) custom-call(f32[8,40,128]{2,1,0:T(8,128)S(1)} %fusion.2.own, f32[8,6,128]{2,1,0:T(8,128)S(1)} %get-tuple-element.19.left, f32[8,6,128]{2,1,0:T(8,128)S(1)} %get-tuple-element.18.right, f32[6,52,128]{2,1,0:T(8,128)S(1)} %collective-permute-done.8.inner, ...), custom_call_target="tpu_custom_call" | custom-call | tf_op jit(solution)/shard_map/krylov/pallas_call | solution.py:237
  48.7 18.1 %all_to_all.5 = f32[128,1,128]{2,1,0:T(1,128)S(1)} all-to-all(f32[128,1,128]{2,1,0:T(1,128)S(1)} %bitcast.19), channel_id=1, replica_groups=mesh['band_0'=4,'band_1'=4,'space_0'=4,'space_1'=2] {'band_0','band_1','..., dimensions={0} | all-to-all | bytes 131072 | tf_op jit(solution)/shard_map/all_to_all | solution.py:295
  66.8 0.9 %combine.1 = f32[8,40,128]{2,1,0:T(8,128)} custom-call(f32[128,128]{1,0:T(8,128)S(1)} %bitcast.18, f32[8,40,128]{2,1,0:T(8,128)S(1)} %fusion.2.own, f32[8,40,128]{2,1,0:T(8,128)S(1)} %get-tuple-element.9.first, f32[8,40,128]{2,1,0:T(8,128)S(1)} %get-tuple-element.10.second), custom_call_target="tpu_custom_call" | custom-call | tf_op jit(solution)/shard_map/combine/pallas_call | solution.py:281
  (6 shorter events, 0.1 us)
Async XLA Ops:
  0.0 0.7 copy-start
  2.7 12.8 %collective-permute-start = (f32[4,8,40,128]{3,2,1,0:T(8,128)S(1)}, f32[4,8,40,128]{3,2,1,0:T(8,128)S(1)}, u32[]{:S(2)}, u32[]{:S(2)}) collective-permute-start(f32[4,8,40,128]{3,2,1,0:T(8,128)S(1)} %density.5), channel_id=1, source_target_pairs={{0,16},{1,65},{2,18},{3,67},{4,20},{5,69},{6,22},{7,71},{8,24},{9,... | collective-permute-start | bytes 1966088 | tf_op jit(solution)/shard_map/ppermute | solution.py:41
  9.2 14.1 %collective-permute-start.1 = (f32[4,8,40,128]{3,2,1,0:T(8,128)S(1)}, f32[4,8,40,128]{3,2,1,0:T(8,128)S(1)}, u32[]{:S(2)}, u32[]{:S(2)}) collective-permute-start(f32[4,8,40,128]{3,2,1,0:T(8,128)S(1)} %density.6), channel_id=1, source_target_pairs={{0,8},{1,33},{2,10},{3,35},{4,12},{5,37},{6,14},{7,39},{8,0},{9,41... | collective-permute-start | bytes 1966088 | tf_op jit(solution)/shard_map/ppermute | solution.py:41
  12.0 11.2 %collective-permute-start.2 = (f32[4,8,40,128]{3,2,1,0:T(8,128)S(1)}, f32[4,8,40,128]{3,2,1,0:T(8,128)S(1)}, u32[]{:S(2)}, u32[]{:S(2)}) collective-permute-start(f32[4,8,40,128]{3,2,1,0:T(8,128)S(1)} %density.7), channel_id=1, source_target_pairs={{0,24},{1,97},{2,26},{3,99},{4,28},{5,101},{6,30},{7,103},{8,16},{... | collective-permute-start | bytes 1966088 | tf_op jit(solution)/shard_map/ppermute | solution.py:41
  23.4 6.0 %collective-permute-start.3 = (f32[8,40,128]{2,1,0:T(8,128)S(1)}, f32[8,40,128]{2,1,0:T(8,128)S(1)}, u32[]{:S(2)}, u32[]{:S(2)}) collective-permute-start(f32[8,40,128]{2,1,0:T(8,128)S(1)} %get-tuple-element.11), channel_id=1, source_target_pairs={{0,64},{1,17},{2,66},{3,19},{4,68},{5,21},{6,70},{7,23},{8,72},{9,... | collective-permute-start | bytes 491528 | tf_op jit(solution)/shard_map/ppermute | solution.py:41
  26.0 4.9 %collective-permute-start.4 = (f32[8,40,128]{2,1,0:T(8,128)S(1)}, f32[8,40,128]{2,1,0:T(8,128)S(1)}, u32[]{:S(2)}, u32[]{:S(2)}) collective-permute-start(f32[8,40,128]{2,1,0:T(8,128)S(1)} %get-tuple-element.13), channel_id=1, source_target_pairs={{0,32},{1,9},{2,34},{3,11},{4,36},{5,13},{6,38},{7,15},{8,40},{9,1... | collective-permute-start | bytes 491528 | tf_op jit(solution)/shard_map/ppermute | solution.py:41
  26.3 5.4 %collective-permute-start.5 = (f32[8,40,128]{2,1,0:T(8,128)S(1)}, f32[8,40,128]{2,1,0:T(8,128)S(1)}, u32[]{:S(2)}, u32[]{:S(2)}) collective-permute-start(f32[8,40,128]{2,1,0:T(8,128)S(1)} %get-tuple-element.12), channel_id=1, source_target_pairs={{0,96},{1,25},{2,98},{3,27},{4,100},{5,29},{6,102},{7,31},{8,104},... | collective-permute-start | bytes 491528 | tf_op jit(solution)/shard_map/ppermute | solution.py:41
  31.7 6.7 %collective-permute-start.6 = (f32[8,6,128]{2,1,0:T(8,128)S(1)}, f32[8,6,128]{2,1,0:T(8,128)S(1)}, u32[]{:S(2)}, u32[]{:S(2)}) collective-permute-start(f32[8,6,128]{2,1,0:T(8,128)S(1)} %get-tuple-element.16), channel_id=1, source_target_pairs={{0,7},{1,2},{2,1},{3,4},{4,3},{5,6},{6,5},{7,0},{8,15},{9,10},{10,... | collective-permute-start | bytes 73736 | tf_op jit(solution)/shard_map/ppermute | solution.py:41
  36.9 1.6 %collective-permute-start.7 = (f32[8,6,128]{2,1,0:T(8,128)S(1)}, f32[8,6,128]{2,1,0:T(8,128)S(1)}, u32[]{:S(2)}, u32[]{:S(2)}) collective-permute-start(f32[8,6,128]{2,1,0:T(8,128)S(1)} %get-tuple-element.17), channel_id=1, source_target_pairs={{0,1},{1,0},{2,3},{3,2},{4,5},{5,4},{6,7},{7,6},{8,9},{9,8},{10,11... | collective-permute-start | bytes 73736 | tf_op jit(solution)/shard_map/ppermute | solution.py:128
  38.5 4.3 %collective-permute-start.8 = (f32[6,52,128]{2,1,0:T(8,128)S(1)}, f32[6,52,128]{2,1,0:T(8,128)S(1)}, u32[]{:S(2)}, u32[]{:S(2)}) collective-permute-start(f32[6,52,128]{2,1,0:T(8,128)S(1)} %get-tuple-element.15), channel_id=1, source_target_pairs={{0,8},{8,0},{16,24},{24,16},{32,40},{40,32},{48,56},{56,48},{64,72... | collective-permute-start | bytes 479240 | tf_op jit(solution)/shard_map/ppermute | solution.py:137
  39.4 7.6 %collective-permute-start.9 = (f32[6,52,128]{2,1,0:T(8,128)S(1)}, f32[6,52,128]{2,1,0:T(8,128)S(1)}, u32[]{:S(2)}, u32[]{:S(2)}) collective-permute-start(f32[6,52,128]{2,1,0:T(8,128)S(1)} %get-tuple-element.14), channel_id=1, source_target_pairs={{0,120},{8,16},{16,8},{24,32},{32,24},{40,48},{48,40},{56,64},{64,... | collective-permute-start | bytes 479240 | tf_op jit(solution)/shard_map/ppermute | solution.py:138

commit v5 on v4

--- a/solution.py
+++ b/solution.py
@@ -41,67 +41,83 @@
     return lax.ppermute(value, EVERY, pairs)
 
 
-def density_body(first, scale, orb, occ, out, held, level, arrive, ready):
+CHUNK = 160
+
+
+def density_body(firsts, scale, orb, occ, *refs):
+    outs, (held, level, arrive, ready) = refs[:-4], refs[-4:]
     z, x, core = lax.axis_index("band_0"), lax.axis_index("band_1"), lax.axis_index("space_1")
-    bands, deep = held.shape[1], held.shape[2]
+    bands, deep = held.shape[1:3]
     weights = pltpu.make_async_copy(occ, level, ready)
-    weights.start()
     copies = []
-    for second in range(SIDE):
+    for slot in range(len(firsts) * SIDE):
+        first, second = firsts[slot // SIDE], slot % SIDE
         to_z = z ^ jnp.where(core == 0, second, first)
         to_x = x ^ jnp.where(core == 0, first, second)
-        row = (to_z * SIDE + to_x) * deep
-        copies.append(pltpu.make_async_copy(orb.at[:, pl.ds(row, deep)], held.at[second], arrive.at[second]))
+        row = pl.multiple_of((to_z * SIDE + to_x) * deep, deep)
+        copies.append(pltpu.make_async_copy(orb.at[:, pl.ds(row, deep)], held.at[slot], arrive.at[slot]))
         copies[-1].start()
+        if slot == 0:
+            weights.start()
     weights.wait()
     factor = [level[b] * scale for b in range(bands)]
-    for second in range(SIDE):
-        copies[second].wait()
-
-        def row(r, carry):
+    for slot, copy in enumerate(copies):
+        copy.wait()
+        out, at = outs[slot // 2], slot % 2
+
+        def part(i, carry):
+            rows = pl.ds(pl.multiple_of(i * CHUNK, CHUNK), CHUNK)
             total = None
             for b in range(bands):
-                wave = held[second, b, r].astype(F32)
+                wave = held[slot, b, rows].astype(F32)
                 term = factor[b] * wave * wave
                 total = term if total is None else total + term
-            out[second, r] = total
+            out[at, rows] = total
             return carry
 
-        lax.fori_loop(0, deep, row, 0)
-
-
-def density_part(orbitals, occupations, scale, first):
+        lax.fori_loop(0, deep // CHUNK, part, 0)
+
+
+def density_part(orbitals, occupations, scale, firsts):
     bands, rows, cols, lanes = orbitals.shape
     deep = rows // 16
-    return pl.pallas_call(
-        functools.partial(density_body, first, scale),
-        out_shape=jax.ShapeDtypeStruct((SIDE, deep, cols, lanes), F32),
-        in_specs=[pl.BlockSpec(memory_space=pl.ANY), pl.BlockSpec(memory_space=pltpu.HBM)],
-        out_specs=pl.BlockSpec(memory_space=pltpu.VMEM),
+    slots = len(firsts) * SIDE
+    half = jax.ShapeDtypeStruct((SIDE // 2, deep * cols, lanes), F32)
+    vmem = pl.BlockSpec(memory_space=pltpu.VMEM)
+    hbm = pl.BlockSpec(memory_space=pl.ANY)
+    parts = pl.pallas_call(
+        functools.partial(density_body, firsts, scale),
+        out_shape=(half,) * (2 * len(firsts)),
+        in_specs=[hbm, hbm],
+        out_specs=(vmem,) * (2 * len(firsts)),
         scratch_shapes=[
-            pltpu.VMEM((SIDE, bands, deep, cols, lanes), orbitals.dtype),
+            pltpu.VMEM((slots, bands, deep * cols, lanes), orbitals.dtype),
             pltpu.SMEM((bands,), F32),
-            pltpu.SemaphoreType.DMA((SIDE,)),
+            pltpu.SemaphoreType.DMA((slots,)),
             pltpu.SemaphoreType.DMA,
         ],
         compiler_params=pltpu.CompilerParams(vmem_limit_bytes=52 * 2**20),
         cost_estimate=pl.CostEstimate(flops=0, bytes_accessed=orbitals.size // 2, transcendentals=0),
         name="density",
-    )(orbitals, occupations)
+    )(orbitals.reshape(bands, rows * cols, lanes), occupations)
+    return [p.reshape(SIDE // 2, deep, cols, lanes) for p in parts]
 
 
 def own_density(orbitals, occupations, scale):
-    part = [None] * SIDE
-    arrived = []
-    for k in (2, 1, 3):
-        part[k] = density_part(orbitals, occupations, scale, k)
-        arrived.append(send(part[k], partner(0, k)))
-    mine = density_part(orbitals, occupations, scale, 0)
-    for other in arrived:
-        mine = mine + other
-    total = mine[0]
-    for other in [send(mine[k], partner(1, k)) for k in (2, 1, 3)]:
-        total = total + other
+    a2, b2 = density_part(orbitals, occupations, scale, (2,))
+    a_near, b_near = send(a2, partner(0, 1)), send(b2, partner(0, 3))
+    a1, b1, a3, b3 = density_part(orbitals, occupations, scale, (1, 3))
+    a_first, b_first = send(a1, partner(0, 1)), send(b3, partner(0, 3))
+    a_near, b_near = lax.optimization_barrier((a_near, b_near))
+    b1, a3 = b1 + b_near, a3 + a_near
+    b1, a3, late = lax.optimization_barrier((b1, a3, occupations))
+    b_last, a_last = send(b1, partner(0, 1)), send(a3, partner(0, 3))
+    a0, b0 = density_part(orbitals, late, scale, (0,))
+    a_first, a_last, b_first, b_last = lax.optimization_barrier((a_first, a_last, b_first, b_last))
+    a0, b0 = a0 + a_first + a_last, b0 + b_first + b_last
+    total = a0[0]
+    for block, k in ((b0[0], 2), (a0[1], 1), (b0[1], 3)):
+        total = total + send(block, partner(1, k))
     return total
 
 

time: 67.9 us -> 67 us (0.987)
  starting transfers between devices: 17.3 us -> 19.6 us
  blocking collectives: 18.1 us -> 16 us
  Pallas kernels: 10.6 us -> 9.07 us
    ppermute x1, starting transfers between devices: 0.01 us -> 5.45 us  [halo(): lax.ppermute(jnp.where(first, right, left), 'space_1', [(0, 1), (1, 0)])]
    ppermute x1, waiting for transfers between devices: 1.1 us -> 4 us  [halo(): inner = lax.ppermute(jnp.where(even, last_rows, first_rows), BAND, inner)]
    ppermute x1, starting transfers between devices: 2.38 us -> 0.24 us  [halo(): outer = lax.ppermute(jnp.where(even, first_rows, last_rows), BAND, outer)]
    all_to_all x1, blocking collectives: 18.1 us -> 16 us  [local(): lax.all_to_all(lines[:, None], EVERY, split_axis=0, concat_axis=0, tiled=...]
    ppermute x7 -> x10, waiting for transfers between devices: 15.5 us -> 13.6 us  [send(): return lax.ppermute(value, EVERY, pairs)]
    pallas_call x4 -> x3, Pallas kernels: 8.05 us -> 6.52 us  [density_part(): pl.pallas_call(functools.partial(density_body, firsts, scale), out_shape=...]
    ppermute x1, starting transfers between devices: 0.85 us -> 0.09 us  [halo(): inner = lax.ppermute(jnp.where(even, last_rows, first_rows), BAND, inner)]
    ppermute x1, waiting for transfers between devices: 4.09 us -> 3.41 us  [halo(): outer = lax.ppermute(jnp.where(even, first_rows, last_rows), BAND, outer)]
  transfers between devices with their start and end apart: 10 -> 13, of which waited for: 8 -> 9; matrix products, arithmetic and copies ran while one was open for 0% -> 0% of each run, Pallas kernels for 9% -> 7%
where the time goes in v5:
time: 67 us; the launch traced here: 66.8 us
  waiting for transfers between devices  21 us (31%)
  starting transfers between devices  19.6 us (29%)
  blocking collectives  16 us (24%)
  Pallas kernels  9.07 us (14%)
  local copies, waits for them, and re-layouts  0.69 us (1%)
    all_to_all x1, blocking collectives, local(): lax.all_to_all(lines[:, None], EVERY, split_axis=0, concat_axis=0, tiled=...  16 us
    ppermute x10, starting transfers between devices, send(): return lax.ppermute(value, EVERY, pairs)  13.8 us
    ppermute x10, waiting for transfers between devices, send(): return lax.ppermute(value, EVERY, pairs)  13.6 us
    pallas_call x3, Pallas kernels, density_part(): pl.pallas_call(functools.partial(density_body, firsts, scale), out_shape=...  6.52 us
    ppermute x1, starting transfers between devices, halo(): lax.ppermute(jnp.where(first, right, left), 'space_1', [(0, 1), (1, 0)])  5.45 us
    ppermute x1, waiting for transfers between devices, halo(): inner = lax.ppermute(jnp.where(even, last_rows, first_rows), BAND, inner)  4 us
    ppermute x1, waiting for transfers between devices, halo(): outer = lax.ppermute(jnp.where(even, first_rows, last_rows), BAND, outer)  3.41 us
    pallas_call x1, Pallas kernels, krylov(): pl.pallas_call(krylov_body, out_shape=(field, field, jax.ShapeDtypeStruct...  1.68 us
  transfers between devices with their start and end apart: 13, of which 9 were waited for; matrix products, arithmetic and copies ran while one was open for 0% of the time, Pallas kernels for 7%

profile of v5, /device:TPU:1, one launch (start us, length us, event | category | flops | bytes accessed | tf_op | source)
XLA Modules:
  0.0 66.8 jit_solution(17591878843139986276)
XLA Ops:
  0.0 0.7 copy-done
  0.7 1.9 %density.4 = (f32[2,320,128]{2,1,0:T(8,128)S(1)}, f32[2,320,128]{2,1,0:T(8,128)S(1)}) custom-call(bf16[8,5120,128]{2,1,0:T(8,128)(2,1)} %bitcast.37, f32[8]{0:T(128)S(1)} %copy-done), custom_call_target="tpu_custom_call" | custom-call | bytes 2621440 | tf_op jit(solution)/shard_map/density/pallas_call | solution.py:88
  2.6 2.5 %collective-permute-start = (f32[2,8,40,128]{3,2,1,0:T(8,128)S(1)}, f32[2,8,40,128]{3,2,1,0:T(8,128)S(1)}, u32[]{:S(2)}, u32[]{:S(2)}) collective-permute-start(f32[2,8,40,128]{3,2,1,0:T(8,128)S(1)} %bitcast.36), channel_id=1, source_target_pairs={{0,8},{1,33},{2,10},{3,35},{4,12},{5,37},{6,14},{7,39},{8,0},{9,41... | collective-permute-start | bytes 983048 | tf_op jit(solution)/shard_map/ppermute | solution.py:41
  5.1 2.2 %collective-permute-start.1 = (f32[2,8,40,128]{3,2,1,0:T(8,128)S(1)}, f32[2,8,40,128]{3,2,1,0:T(8,128)S(1)}, u32[]{:S(2)}, u32[]{:S(2)}) collective-permute-start(f32[2,8,40,128]{3,2,1,0:T(8,128)S(1)} %bitcast.35), channel_id=1, source_target_pairs={{0,24},{1,97},{2,26},{3,99},{4,28},{5,101},{6,30},{7,103},{8,16},{... | collective-permute-start | bytes 983048 | tf_op jit(solution)/shard_map/ppermute | solution.py:41
  7.4 2.7 %density.3 = (f32[2,320,128]{2,1,0:T(8,128)S(1)}, f32[2,320,128]{2,1,0:T(8,128)S(1)}, f32[2,320,128]{2,1,0:T(8,128)S(1)}, f32[2,320,128]{2,1,0:T(8,128)S(1)}) custom-call(bf16[8,5120,128]{2,1,0:T(8,128)(2,1)} %bitcast.38, f32[8]{0:T(128)S(1)} %copy-done), custom_call_target="tpu_custom_call" | custom-call | bytes 2621440 | tf_op jit(solution)/shard_map/density/pallas_call | solution.py:88
  10.1 0.8 %collective-permute-start.2 = (f32[2,8,40,128]{3,2,1,0:T(8,128)S(1)}, f32[2,8,40,128]{3,2,1,0:T(8,128)S(1)}, u32[]{:S(2)}, u32[]{:S(2)}) collective-permute-start(f32[2,8,40,128]{3,2,1,0:T(8,128)S(1)} %bitcast.34), channel_id=1, source_target_pairs={{0,8},{1,33},{2,10},{3,35},{4,12},{5,37},{6,14},{7,39},{8,0},{9,41... | collective-permute-start | bytes 983048 | tf_op jit(solution)/shard_map/ppermute | solution.py:41
  10.9 0.6 collective-permute-start.4
  11.5 0.0 collective-permute-done
  11.5 1.0 %collective-permute-done.1 = f32[2,8,40,128]{3,2,1,0:T(8,128)S(1)} collective-permute-done((f32[2,8,40,128]{3,2,1,0:T(8,128)S(1)}, f32[2,8,40,128]{3,2,1,0:T(8,128)S(1)}, u32[]{:S(2)}, u32[]{:S(2)}) %collective-permute-start.1) | collective-permute-done | bytes 327712 | tf_op jit(solution)/shard_map/ppermute | solution.py:41
  12.6 2.3 %collective-permute-start.3 = (f32[2,8,40,128]{3,2,1,0:T(8,128)S(1)}, f32[2,8,40,128]{3,2,1,0:T(8,128)S(1)}, u32[]{:S(2)}, u32[]{:S(2)}) collective-permute-start(f32[2,8,40,128]{3,2,1,0:T(8,128)S(1)} %add.35), channel_id=1, source_target_pairs={{0,24},{1,97},{2,26},{3,99},{4,28},{5,101},{6,30},{7,103},{8,16},{... | collective-permute-start | bytes 983048 | tf_op jit(solution)/shard_map/ppermute | solution.py:41
  14.9 0.0 collective-permute-start.5
  14.9 1.9 %density.5 = (f32[2,320,128]{2,1,0:T(8,128)S(1)}, f32[2,320,128]{2,1,0:T(8,128)S(1)}) custom-call(bf16[8,5120,128]{2,1,0:T(8,128)(2,1)} %bitcast.39, f32[8]{0:T(128)S(1)} %copy-done), custom_call_target="tpu_custom_call" | custom-call | bytes 2621440 | tf_op jit(solution)/shard_map/density/pallas_call | solution.py:88
  16.9 0.0 collective-permute-done.2
  16.9 1.5 %collective-permute-done.4 = f32[2,8,40,128]{3,2,1,0:T(8,128)S(1)} collective-permute-done((f32[2,8,40,128]{3,2,1,0:T(8,128)S(1)}, f32[2,8,40,128]{3,2,1,0:T(8,128)S(1)}, u32[]{:S(2)}, u32[]{:S(2)}) %collective-permute-start.4) | collective-permute-done | bytes 327712 | tf_op jit(solution)/shard_map/ppermute | solution.py:41
  18.3 3.5 %collective-permute-done.3 = f32[2,8,40,128]{3,2,1,0:T(8,128)S(1)} collective-permute-done((f32[2,8,40,128]{3,2,1,0:T(8,128)S(1)}, f32[2,8,40,128]{3,2,1,0:T(8,128)S(1)}, u32[]{:S(2)}, u32[]{:S(2)}) %collective-permute-start.3) | collective-permute-done | bytes 327712 | tf_op jit(solution)/shard_map/ppermute | solution.py:41
  21.9 1.0 %collective-permute-start.7 = (f32[8,40,128]{2,1,0:T(8,128)S(1)}, f32[8,40,128]{2,1,0:T(8,128)S(1)}, u32[]{:S(2)}, u32[]{:S(2)}) collective-permute-start(f32[8,40,128]{2,1,0:T(8,128)S(1)} %slice_bitcast_fusion.1), channel_id=1, source_target_pairs={{0,32},{1,9},{2,34},{3,11},{4,36},{5,13},{6,38},{7,15},{8,40},{9,1... | collective-permute-start | bytes 491528 | tf_op jit(solution)/shard_map/ppermute | solution.py:41
  23.0 2.5 %collective-permute-start.6 = (f32[8,40,128]{2,1,0:T(8,128)S(1)}, f32[8,40,128]{2,1,0:T(8,128)S(1)}, u32[]{:S(2)}, u32[]{:S(2)}) collective-permute-start(f32[8,40,128]{2,1,0:T(8,128)S(1)} %get-tuple-element.45), channel_id=1, source_target_pairs={{0,64},{1,17},{2,66},{3,19},{4,68},{5,21},{6,70},{7,23},{8,72},{9,... | collective-permute-start | bytes 491528 | tf_op jit(solution)/shard_map/ppermute | solution.py:41
  25.5 0.5 collective-permute-start.8
  26.0 0.1 collective-permute-done.7
  26.2 3.7 %collective-permute-done.6 = f32[8,40,128]{2,1,0:T(8,128)S(1)} collective-permute-done((f32[8,40,128]{2,1,0:T(8,128)S(1)}, f32[8,40,128]{2,1,0:T(8,128)S(1)}, u32[]{:S(2)}, u32[]{:S(2)}) %collective-permute-start.6) | collective-permute-done | bytes 163872 | tf_op jit(solution)/shard_map/ppermute | solution.py:41
  29.9 1.7 %collective-permute-done.8 = f32[8,40,128]{2,1,0:T(8,128)S(1)} collective-permute-done((f32[8,40,128]{2,1,0:T(8,128)S(1)}, f32[8,40,128]{2,1,0:T(8,128)S(1)}, u32[]{:S(2)}, u32[]{:S(2)}) %collective-permute-start.8) | collective-permute-done | bytes 163872 | tf_op jit(solution)/shard_map/ppermute | solution.py:41
  31.6 5.4 %collective-permute-start.10 = (f32[8,6,128]{2,1,0:T(8,128)S(1)}, f32[8,6,128]{2,1,0:T(8,128)S(1)}, u32[]{:S(2)}, u32[]{:S(2)}) collective-permute-start(f32[8,6,128]{2,1,0:T(8,128)S(1)} %get-tuple-element.50), channel_id=1, source_target_pairs={{0,1},{1,0},{2,3},{3,2},{4,5},{5,4},{6,7},{7,6},{8,9},{9,8},{10,11... | collective-permute-start | bytes 73736 | tf_op jit(solution)/shard_map/ppermute | solution.py:144
  37.1 1.3 %collective-permute-start.9 = (f32[8,6,128]{2,1,0:T(8,128)S(1)}, f32[8,6,128]{2,1,0:T(8,128)S(1)}, u32[]{:S(2)}, u32[]{:S(2)}) collective-permute-start(f32[8,6,128]{2,1,0:T(8,128)S(1)} %get-tuple-element.49), channel_id=1, source_target_pairs={{0,7},{1,2},{2,1},{3,4},{4,3},{5,6},{6,5},{7,0},{8,15},{9,10},{10,... | collective-permute-start | bytes 73736 | tf_op jit(solution)/shard_map/ppermute | solution.py:41
  38.4 0.0 collective-permute-done.10
  38.4 2.1 %collective-permute-done.9 = f32[8,6,128]{2,1,0:T(8,128)S(1)} collective-permute-done((f32[8,6,128]{2,1,0:T(8,128)S(1)}, f32[8,6,128]{2,1,0:T(8,128)S(1)}, u32[]{:S(2)}, u32[]{:S(2)}) %collective-permute-start.9) | collective-permute-done | bytes 24608 | tf_op jit(solution)/shard_map/ppermute | solution.py:41
  40.5 0.1 collective-permute-start.11
  40.6 0.2 collective-permute-start.12
  40.8 4.0 %collective-permute-done.11.inner = f32[6,52,128]{2,1,0:T(8,128)S(1)} collective-permute-done((f32[6,52,128]{2,1,0:T(8,128)S(1)}, f32[6,52,128]{2,1,0:T(8,128)S(1)}, u32[]{:S(2)}, u32[]{:S(2)}) %collective-permute-start.11) | collective-permute-done | bytes 159776 | tf_op jit(solution)/shard_map/ppermute | solution.py:153
  44.8 3.4 %collective-permute-done.12.outer = f32[6,52,128]{2,1,0:T(8,128)S(1)} collective-permute-done((f32[6,52,128]{2,1,0:T(8,128)S(1)}, f32[6,52,128]{2,1,0:T(8,128)S(1)}, u32[]{:S(2)}, u32[]{:S(2)}) %collective-permute-start.12) | collective-permute-done | bytes 159776 | tf_op jit(solution)/shard_map/ppermute | solution.py:154
  48.3 1.7 %krylov.1 = (f32[8,40,128]{2,1,0:T(8,128)S(1)}, f32[8,40,128]{2,1,0:T(8,128)S(1)}, f32[128,128]{1,0:T(8,128)S(1)}) custom-call(f32[8,40,128]{2,1,0:T(8,128)S(1)} %fusion.2.own, f32[8,6,128]{2,1,0:T(8,128)S(1)} %get-tuple-element.52.left, f32[8,6,128]{2,1,0:T(8,128)S(1)} %get-tuple-element.51.right, f32[6,52,128]{2,1,0:T(8,128)S(1)} %collective-permute-done.11.inner, ...), custom_call_target="tpu_custom_call" | custom-call | tf_op jit(solution)/shard_map/krylov/pallas_call | solution.py:253
  49.9 16.0 %all_to_all.5 = f32[128,1,128]{2,1,0:T(1,128)S(1)} all-to-all(f32[128,1,128]{2,1,0:T(1,128)S(1)} %bitcast.32), channel_id=1, replica_groups=mesh['band_0'=4,'band_1'=4,'space_0'=4,'space_1'=2] {'band_0','band_1','..., dimensions={0} | all-to-all | bytes 131072 | tf_op jit(solution)/shard_map/all_to_all | solution.py:311
  66.0 0.9 %combine.1 = f32[8,40,128]{2,1,0:T(8,128)} custom-call(f32[128,128]{1,0:T(8,128)S(1)} %bitcast.31, f32[8,40,128]{2,1,0:T(8,128)S(1)} %fusion.2.own, f32[8,40,128]{2,1,0:T(8,128)S(1)} %get-tuple-element.43.first, f32[8,40,128]{2,1,0:T(8,128)S(1)} %get-tuple-element.44.second), custom_call_target="tpu_custom_call" | custom-call | tf_op jit(solution)/shard_map/combine/pallas_call | solution.py:297
  (13 shorter events, 0.3 us)
Async XLA Ops:
  0.0 0.7 copy-start
  2.6 8.9 %collective-permute-start = (f32[2,8,40,128]{3,2,1,0:T(8,128)S(1)}, f32[2,8,40,128]{3,2,1,0:T(8,128)S(1)}, u32[]{:S(2)}, u32[]{:S(2)}) collective-permute-start(f32[2,8,40,128]{3,2,1,0:T(8,128)S(1)} %bitcast.36), channel_id=1, source_target_pairs={{0,8},{1,33},{2,10},{3,35},{4,12},{5,37},{6,14},{7,39},{8,0},{9,41... | collective-permute-start | bytes 983048 | tf_op jit(solution)/shard_map/ppermute | solution.py:41
  5.1 7.4 %collective-permute-start.1 = (f32[2,8,40,128]{3,2,1,0:T(8,128)S(1)}, f32[2,8,40,128]{3,2,1,0:T(8,128)S(1)}, u32[]{:S(2)}, u32[]{:S(2)}) collective-permute-start(f32[2,8,40,128]{3,2,1,0:T(8,128)S(1)} %bitcast.35), channel_id=1, source_target_pairs={{0,24},{1,97},{2,26},{3,99},{4,28},{5,101},{6,30},{7,103},{8,16},{... | collective-permute-start | bytes 983048 | tf_op jit(solution)/shard_map/ppermute | solution.py:41
  10.1 6.8 %collective-permute-start.2 = (f32[2,8,40,128]{3,2,1,0:T(8,128)S(1)}, f32[2,8,40,128]{3,2,1,0:T(8,128)S(1)}, u32[]{:S(2)}, u32[]{:S(2)}) collective-permute-start(f32[2,8,40,128]{3,2,1,0:T(8,128)S(1)} %bitcast.34), channel_id=1, source_target_pairs={{0,8},{1,33},{2,10},{3,35},{4,12},{5,37},{6,14},{7,39},{8,0},{9,41... | collective-permute-start | bytes 983048 | tf_op jit(solution)/shard_map/ppermute | solution.py:41
  10.9 7.4 %collective-permute-start.4 = (f32[2,8,40,128]{3,2,1,0:T(8,128)S(1)}, f32[2,8,40,128]{3,2,1,0:T(8,128)S(1)}, u32[]{:S(2)}, u32[]{:S(2)}) collective-permute-start(f32[2,8,40,128]{3,2,1,0:T(8,128)S(1)} %bitcast.33), channel_id=1, source_target_pairs={{0,24},{1,97},{2,26},{3,99},{4,28},{5,101},{6,30},{7,103},{8,16},{... | collective-permute-start | bytes 983048 | tf_op jit(solution)/shard_map/ppermute | solution.py:41
  12.6 9.2 %collective-permute-start.3 = (f32[2,8,40,128]{3,2,1,0:T(8,128)S(1)}, f32[2,8,40,128]{3,2,1,0:T(8,128)S(1)}, u32[]{:S(2)}, u32[]{:S(2)}) collective-permute-start(f32[2,8,40,128]{3,2,1,0:T(8,128)S(1)} %add.35), channel_id=1, source_target_pairs={{0,24},{1,97},{2,26},{3,99},{4,28},{5,101},{6,30},{7,103},{8,16},{... | collective-permute-start | bytes 983048 | tf_op jit(solution)/shard_map/ppermute | solution.py:41
  14.9 6.9 %collective-permute-start.5 = (f32[2,8,40,128]{3,2,1,0:T(8,128)S(1)}, f32[2,8,40,128]{3,2,1,0:T(8,128)S(1)}, u32[]{:S(2)}, u32[]{:S(2)}) collective-permute-start(f32[2,8,40,128]{3,2,1,0:T(8,128)S(1)} %add.34), channel_id=1, source_target_pairs={{0,8},{1,33},{2,10},{3,35},{4,12},{5,37},{6,14},{7,39},{8,0},{9,41... | collective-permute-start | bytes 983048 | tf_op jit(solution)/shard_map/ppermute | solution.py:41
  21.9 4.2 %collective-permute-start.7 = (f32[8,40,128]{2,1,0:T(8,128)S(1)}, f32[8,40,128]{2,1,0:T(8,128)S(1)}, u32[]{:S(2)}, u32[]{:S(2)}) collective-permute-start(f32[8,40,128]{2,1,0:T(8,128)S(1)} %slice_bitcast_fusion.1), channel_id=1, source_target_pairs={{0,32},{1,9},{2,34},{3,11},{4,36},{5,13},{6,38},{7,15},{8,40},{9,1... | collective-permute-start | bytes 491528 | tf_op jit(solution)/shard_map/ppermute | solution.py:41
  23.0 6.9 %collective-permute-start.6 = (f32[8,40,128]{2,1,0:T(8,128)S(1)}, f32[8,40,128]{2,1,0:T(8,128)S(1)}, u32[]{:S(2)}, u32[]{:S(2)}) collective-permute-start(f32[8,40,128]{2,1,0:T(8,128)S(1)} %get-tuple-element.45), channel_id=1, source_target_pairs={{0,64},{1,17},{2,66},{3,19},{4,68},{5,21},{6,70},{7,23},{8,72},{9,... | collective-permute-start | bytes 491528 | tf_op jit(solution)/shard_map/ppermute | solution.py:41
  25.5 6.1 %collective-permute-start.8 = (f32[8,40,128]{2,1,0:T(8,128)S(1)}, f32[8,40,128]{2,1,0:T(8,128)S(1)}, u32[]{:S(2)}, u32[]{:S(2)}) collective-permute-start(f32[8,40,128]{2,1,0:T(8,128)S(1)} %get-tuple-element.46), channel_id=1, source_target_pairs={{0,96},{1,25},{2,98},{3,27},{4,100},{5,29},{6,102},{7,31},{8,104},... | collective-permute-start | bytes 491528 | tf_op jit(solution)/shard_map/ppermute | solution.py:41
  31.6 6.7 %collective-permute-start.10 = (f32[8,6,128]{2,1,0:T(8,128)S(1)}, f32[8,6,128]{2,1,0:T(8,128)S(1)}, u32[]{:S(2)}, u32[]{:S(2)}) collective-permute-start(f32[8,6,128]{2,1,0:T(8,128)S(1)} %get-tuple-element.50), channel_id=1, source_target_pairs={{0,1},{1,0},{2,3},{3,2},{4,5},{5,4},{6,7},{7,6},{8,9},{9,8},{10,11... | collective-permute-start | bytes 73736 | tf_op jit(solution)/shard_map/ppermute | solution.py:144
  37.1 3.3 %collective-permute-start.9 = (f32[8,6,128]{2,1,0:T(8,128)S(1)}, f32[8,6,128]{2,1,0:T(8,128)S(1)}, u32[]{:S(2)}, u32[]{:S(2)}) collective-permute-start(f32[8,6,128]{2,1,0:T(8,128)S(1)} %get-tuple-element.49), channel_id=1, source_target_pairs={{0,7},{1,2},{2,1},{3,4},{4,3},{5,6},{6,5},{7,0},{8,15},{9,10},{10,... | collective-permute-start | bytes 73736 | tf_op jit(solution)/shard_map/ppermute | solution.py:41
  40.5 4.3 %collective-permute-start.11 = (f32[6,52,128]{2,1,0:T(8,128)S(1)}, f32[6,52,128]{2,1,0:T(8,128)S(1)}, u32[]{:S(2)}, u32[]{:S(2)}) collective-permute-start(f32[6,52,128]{2,1,0:T(8,128)S(1)} %get-tuple-element.48), channel_id=1, source_target_pairs={{0,8},{8,0},{16,24},{24,16},{32,40},{40,32},{48,56},{56,48},{64,72... | collective-permute-start | bytes 479240 | tf_op jit(solution)/shard_map/ppermute | solution.py:153
  40.6 7.7 %collective-permute-start.12 = (f32[6,52,128]{2,1,0:T(8,128)S(1)}, f32[6,52,128]{2,1,0:T(8,128)S(1)}, u32[]{:S(2)}, u32[]{:S(2)}) collective-permute-start(f32[6,52,128]{2,1,0:T(8,128)S(1)} %get-tuple-element.47), channel_id=1, source_target_pairs={{0,120},{8,16},{16,8},{24,32},{32,24},{40,48},{48,40},{56,64},{64,... | collective-permute-start | bytes 479240 | tf_op jit(solution)/shard_map/ppermute | solution.py:154

commit v6 on v5

--- a/solution.py
+++ b/solution.py
@@ -11,7 +11,8 @@
 
 
 ITERS = 3
-REACH = 2 * ITERS
+REACH = 2 * ITERS - 1
+SIDEWAYS = REACH - 1
 BAND = ("band_0", "band_1")
 SPACE = ("space_0", "space_1")
 EVERY = BAND + SPACE
@@ -145,7 +146,7 @@
     space = lax.axis_index(SPACE)
     far = jnp.where((space > 0) & (space < 7), far, 0.0)
     left, right = jnp.where(first, far, near), jnp.where(first, near, far)
-    wide = jnp.concatenate([left, field, right], 1)
+    wide = jnp.concatenate([left[:, -SIDEWAYS:], field, right[:, :SIDEWAYS]], 1)
     even = lax.axis_index("band_1") % 2 == 0
     inner = [(i, i ^ 1) for i in range(16)]
     outer = [(i, (i + 1 if i % 2 else i - 1) % 16) for i in range(16)]
@@ -155,29 +156,35 @@
     return left, right, inner, outer
 
 
-def laplacian(ref, r, start, size, masks):
-    def at(row, shift):
-        return ref[row, start + shift : start + shift + size]
-
-    center = at(r, 0)
+def laplacian(ref, r, start, size, masks, outer=None):
+    outer = ref if outer is None else outer
+
+    def at(down, across):
+        source = outer if abs(down) + abs(across) == 2 else ref
+        return source[r + down, start + across : start + across + size]
+
+    center = at(0, 0)
     lanes = center.shape[1]
 
     def along(k):
         return jnp.where(masks[k], pltpu.roll(center, -k % lanes, 1), 0.0)
 
-    near = at(r + 1, 0) + at(r - 1, 0) + at(r, 1) + at(r, -1) + along(1) + along(-1)
-    distant = at(r + 2, 0) + at(r - 2, 0) + at(r, 2) + at(r, -2) + along(2) + along(-2)
+    near = at(1, 0) + at(-1, 0) + at(0, 1) + at(0, -1) + along(1) + along(-1)
+    distant = at(2, 0) + at(-2, 0) + at(0, 2) + at(0, -2) + along(2) + along(-2)
     return 7.5 * center - 4.0 / 3.0 * near + 1.0 / 12.0 * distant
 
 
 PAD = 8
 
 
-def krylov_body(own, left, right, inner, outer, first_out, second_out, lines, zero, one, two):
+def krylov_body(own, left, right, inner, outer, first_out, second_out, lines, zero, one, two, double):
     rows, cols, lanes = own.shape
     deep = rows + 2 * REACH
     band, space = lax.axis_index(BAND), lax.axis_index(SPACE)
-    wide = slice(PAD - REACH, PAD + cols + REACH)
+    wide = slice(PAD - SIDEWAYS, PAD + cols + SIDEWAYS)
+    for edge in (slice(0, REACH), slice(REACH + rows, deep)):
+        zero[edge, 0:PAD] = jnp.zeros((REACH, PAD, lanes), F32)
+        zero[edge, PAD + cols :] = jnp.zeros((REACH, PAD, lanes), F32)
     zero[REACH : REACH + rows, PAD : PAD + cols] = own[...]
     zero[REACH : REACH + rows, PAD - REACH : PAD] = left[...]
     zero[REACH : REACH + rows, PAD + cols : PAD + cols + REACH] = right[...]
@@ -196,26 +203,35 @@
         lane = lax.broadcasted_iota(jnp.int32, (size, lanes), 1)
         return {1: lane < lanes - 1, -1: lane >= 1, 2: lane < lanes - 2, -2: lane >= 2}
 
-    def advance(source, target, edge):
+    def advance(source, target, edge, unroll, twice=None):
         start = PAD - REACH + edge
         size = cols + 2 * (REACH - edge)
         inside = masks(size)
-        col = lax.broadcasted_iota(jnp.int32, (size, lanes), 0) + (space * cols + start - PAD)
-        col_in = (col >= 0) & (col < 8 * cols)
+        at = lax.broadcasted_iota(jnp.int32, (size, lanes), 0) + (start - PAD)
+        col_in = (at >= -space * cols) & (at < (8 - space) * cols)
+        beside = jnp.where((at < 0) | (at >= cols), 2.0, 1.0)
 
         def step(i, carry):
-            for j in range(4):
-                r = edge + 4 * i + j
-                row = band * rows + (r - REACH)
-                row_in = (row >= 0) & (row < 16 * rows)
-                image = laplacian(source, r, start, size, inside)
-                target[r, start : start + size] = jnp.where(col_in & row_in, image, 0.0)
+            for j in range(unroll):
+                r = edge + unroll * i + j
+                own = r - REACH
+                row_in = (own >= -band * rows) & (own < (16 - band) * rows)
+                image = jnp.where(col_in & row_in, laplacian(source, r, start, size, inside), 0.0)
+                target[r, start : start + size] = image
+                if twice is not None:
+                    twice[r, start : start + size] = image * jnp.where((own < 0) | (own >= rows), 2.0, beside)
             return carry
 
-        lax.fori_loop(0, (deep - 2 * edge) // 4, step, 0)
-
-    advance(zero, one, 2)
-    advance(one, two, 4)
+        lax.fori_loop(0, (deep - 2 * edge) // unroll, step, 0)
+
+    blank = jnp.zeros((cols + 2 * PAD, lanes), F32)
+    for r in (REACH - 2, REACH + rows + 1):
+        double[r] = blank
+    for r in range(REACH - 1, REACH + rows + 1):
+        double[r, 0:PAD] = blank[0:PAD]
+        double[r, PAD + cols :] = blank[0:PAD]
+    advance(zero, one, 2, 7)
+    advance(one, two, 4, 5, double)
     inside = masks(cols)
 
     def fold(p, q):
@@ -229,7 +245,7 @@
             s0 = zero[at, PAD : PAD + cols]
             s1 = one[at, PAD : PAD + cols]
             s2 = two[at, PAD : PAD + cols]
-            s3 = laplacian(two, at, PAD, cols, inside)
+            s3 = laplacian(two, at, PAD, cols, inside, double)
             first_out[r] = s1
             second_out[r] = s2
             pairs = ((s0, s0), (s0, s1), (s1, s1), (s1, s2), (s2, s2), (s2, s3))
@@ -255,7 +271,7 @@
         out_shape=(field, field, jax.ShapeDtypeStruct((128, lanes), F32)),
         in_specs=[vmem] * (1 + len(pieces)),
         out_specs=(vmem, vmem, vmem),
-        scratch_shapes=[scratch, scratch, scratch],
+        scratch_shapes=[scratch] * 4,
         compiler_params=pltpu.CompilerParams(vmem_limit_bytes=8 * 2**20),
         name="krylov",
     )(own, *pieces)

time: 67 us -> 65.7 us (0.981)
  no operation moved by 1% of the time
where the time goes in v6:
time: 65.7 us; the launch traced here: 65.5 us
  waiting for transfers between devices  20.5 us (31%)
  starting transfers between devices  19.6 us (30%)
  blocking collectives  15.5 us (24%)
  Pallas kernels  8.78 us (13%)
  local copies, waits for them, and re-layouts  0.7 us (1%)
    all_to_all x1, blocking collectives, local(): lax.all_to_all(lines[:, None], EVERY, split_axis=0, concat_axis=0, tiled=...  15.5 us
    ppermute x10, starting transfers between devices, send(): return lax.ppermute(value, EVERY, pairs)  13.8 us
    ppermute x10, waiting for transfers between devices, send(): return lax.ppermute(value, EVERY, pairs)  13.6 us
    pallas_call x3, Pallas kernels, density_part(): pl.pallas_call(functools.partial(density_body, firsts, scale), out_shape=...  6.52 us
    ppermute x1, starting transfers between devices, halo(): lax.ppermute(jnp.where(first, right, left), 'space_1', [(0, 1), (1, 0)])  5.45 us
    ppermute x1, waiting for transfers between devices, halo(): inner = lax.ppermute(jnp.where(even, last_rows, first_rows), BAND, inner)  3.47 us
    ppermute x1, waiting for transfers between devices, halo(): outer = lax.ppermute(jnp.where(even, first_rows, last_rows), BAND, outer)  3.41 us
    pallas_call x1, Pallas kernels, krylov(): pl.pallas_call(krylov_body, out_shape=(field, field, jax.ShapeDtypeStruct...  1.39 us
  transfers between devices with their start and end apart: 13, of which 9 were waited for; matrix products, arithmetic and copies ran while one was open for 0% of the time, Pallas kernels for 7%

profile of v6, /device:TPU:1, one launch (start us, length us, event | category | flops | bytes accessed | tf_op | source)
XLA Modules:
  0.0 65.5 jit_solution(15758290405518212315)
XLA Ops:
  0.0 0.7 copy-done
  0.7 1.9 %density.4 = (f32[2,320,128]{2,1,0:T(8,128)S(1)}, f32[2,320,128]{2,1,0:T(8,128)S(1)}) custom-call(bf16[8,5120,128]{2,1,0:T(8,128)(2,1)} %bitcast.37, f32[8]{0:T(128)S(1)} %copy-done), custom_call_target="tpu_custom_call" | custom-call | bytes 2621440 | tf_op jit(solution)/shard_map/density/pallas_call | solution.py:89
  2.6 2.5 %collective-permute-start = (f32[2,8,40,128]{3,2,1,0:T(8,128)S(1)}, f32[2,8,40,128]{3,2,1,0:T(8,128)S(1)}, u32[]{:S(2)}, u32[]{:S(2)}) collective-permute-start(f32[2,8,40,128]{3,2,1,0:T(8,128)S(1)} %bitcast.36), channel_id=1, source_target_pairs={{0,8},{1,33},{2,10},{3,35},{4,12},{5,37},{6,14},{7,39},{8,0},{9,41... | collective-permute-start | bytes 983048 | tf_op jit(solution)/shard_map/ppermute | solution.py:42
  5.1 2.2 %collective-permute-start.1 = (f32[2,8,40,128]{3,2,1,0:T(8,128)S(1)}, f32[2,8,40,128]{3,2,1,0:T(8,128)S(1)}, u32[]{:S(2)}, u32[]{:S(2)}) collective-permute-start(f32[2,8,40,128]{3,2,1,0:T(8,128)S(1)} %bitcast.35), channel_id=1, source_target_pairs={{0,24},{1,97},{2,26},{3,99},{4,28},{5,101},{6,30},{7,103},{8,16},{... | collective-permute-start | bytes 983048 | tf_op jit(solution)/shard_map/ppermute | solution.py:42
  7.4 2.7 %density.3 = (f32[2,320,128]{2,1,0:T(8,128)S(1)}, f32[2,320,128]{2,1,0:T(8,128)S(1)}, f32[2,320,128]{2,1,0:T(8,128)S(1)}, f32[2,320,128]{2,1,0:T(8,128)S(1)}) custom-call(bf16[8,5120,128]{2,1,0:T(8,128)(2,1)} %bitcast.38, f32[8]{0:T(128)S(1)} %copy-done), custom_call_target="tpu_custom_call" | custom-call | bytes 2621440 | tf_op jit(solution)/shard_map/density/pallas_call | solution.py:89
  10.1 0.8 %collective-permute-start.2 = (f32[2,8,40,128]{3,2,1,0:T(8,128)S(1)}, f32[2,8,40,128]{3,2,1,0:T(8,128)S(1)}, u32[]{:S(2)}, u32[]{:S(2)}) collective-permute-start(f32[2,8,40,128]{3,2,1,0:T(8,128)S(1)} %bitcast.34), channel_id=1, source_target_pairs={{0,8},{1,33},{2,10},{3,35},{4,12},{5,37},{6,14},{7,39},{8,0},{9,41... | collective-permute-start | bytes 983048 | tf_op jit(solution)/shard_map/ppermute | solution.py:42
  10.9 0.6 collective-permute-start.4
  11.5 0.0 collective-permute-done
  11.5 1.0 %collective-permute-done.1 = f32[2,8,40,128]{3,2,1,0:T(8,128)S(1)} collective-permute-done((f32[2,8,40,128]{3,2,1,0:T(8,128)S(1)}, f32[2,8,40,128]{3,2,1,0:T(8,128)S(1)}, u32[]{:S(2)}, u32[]{:S(2)}) %collective-permute-start.1) | collective-permute-done | bytes 327712 | tf_op jit(solution)/shard_map/ppermute | solution.py:42
  12.6 2.3 %collective-permute-start.3 = (f32[2,8,40,128]{3,2,1,0:T(8,128)S(1)}, f32[2,8,40,128]{3,2,1,0:T(8,128)S(1)}, u32[]{:S(2)}, u32[]{:S(2)}) collective-permute-start(f32[2,8,40,128]{3,2,1,0:T(8,128)S(1)} %add.35), channel_id=1, source_target_pairs={{0,24},{1,97},{2,26},{3,99},{4,28},{5,101},{6,30},{7,103},{8,16},{... | collective-permute-start | bytes 983048 | tf_op jit(solution)/shard_map/ppermute | solution.py:42
  14.9 0.0 collective-permute-start.5
  14.9 1.9 %density.5 = (f32[2,320,128]{2,1,0:T(8,128)S(1)}, f32[2,320,128]{2,1,0:T(8,128)S(1)}) custom-call(bf16[8,5120,128]{2,1,0:T(8,128)(2,1)} %bitcast.39, f32[8]{0:T(128)S(1)} %copy-done), custom_call_target="tpu_custom_call" | custom-call | bytes 2621440 | tf_op jit(solution)/shard_map/density/pallas_call | solution.py:89
  16.9 0.0 collective-permute-done.2
  16.9 1.5 %collective-permute-done.4 = f32[2,8,40,128]{3,2,1,0:T(8,128)S(1)} collective-permute-done((f32[2,8,40,128]{3,2,1,0:T(8,128)S(1)}, f32[2,8,40,128]{3,2,1,0:T(8,128)S(1)}, u32[]{:S(2)}, u32[]{:S(2)}) %collective-permute-start.4) | collective-permute-done | bytes 327712 | tf_op jit(solution)/shard_map/ppermute | solution.py:42
  18.3 3.5 %collective-permute-done.3 = f32[2,8,40,128]{3,2,1,0:T(8,128)S(1)} collective-permute-done((f32[2,8,40,128]{3,2,1,0:T(8,128)S(1)}, f32[2,8,40,128]{3,2,1,0:T(8,128)S(1)}, u32[]{:S(2)}, u32[]{:S(2)}) %collective-permute-start.3) | collective-permute-done | bytes 327712 | tf_op jit(solution)/shard_map/ppermute | solution.py:42
  21.9 1.0 %collective-permute-start.7 = (f32[8,40,128]{2,1,0:T(8,128)S(1)}, f32[8,40,128]{2,1,0:T(8,128)S(1)}, u32[]{:S(2)}, u32[]{:S(2)}) collective-permute-start(f32[8,40,128]{2,1,0:T(8,128)S(1)} %slice_bitcast_fusion.1), channel_id=1, source_target_pairs={{0,32},{1,9},{2,34},{3,11},{4,36},{5,13},{6,38},{7,15},{8,40},{9,1... | collective-permute-start | bytes 491528 | tf_op jit(solution)/shard_map/ppermute | solution.py:42
  23.0 2.5 %collective-permute-start.6 = (f32[8,40,128]{2,1,0:T(8,128)S(1)}, f32[8,40,128]{2,1,0:T(8,128)S(1)}, u32[]{:S(2)}, u32[]{:S(2)}) collective-permute-start(f32[8,40,128]{2,1,0:T(8,128)S(1)} %get-tuple-element.45), channel_id=1, source_target_pairs={{0,64},{1,17},{2,66},{3,19},{4,68},{5,21},{6,70},{7,23},{8,72},{9,... | collective-permute-start | bytes 491528 | tf_op jit(solution)/shard_map/ppermute | solution.py:42
  25.5 0.5 collective-permute-start.8
  26.0 0.1 collective-permute-done.7
  26.2 3.7 %collective-permute-done.6 = f32[8,40,128]{2,1,0:T(8,128)S(1)} collective-permute-done((f32[8,40,128]{2,1,0:T(8,128)S(1)}, f32[8,40,128]{2,1,0:T(8,128)S(1)}, u32[]{:S(2)}, u32[]{:S(2)}) %collective-permute-start.6) | collective-permute-done | bytes 163872 | tf_op jit(solution)/shard_map/ppermute | solution.py:42
  29.9 1.7 %collective-permute-done.8 = f32[8,40,128]{2,1,0:T(8,128)S(1)} collective-permute-done((f32[8,40,128]{2,1,0:T(8,128)S(1)}, f32[8,40,128]{2,1,0:T(8,128)S(1)}, u32[]{:S(2)}, u32[]{:S(2)}) %collective-permute-start.8) | collective-permute-done | bytes 163872 | tf_op jit(solution)/shard_map/ppermute | solution.py:42
  31.6 5.4 %collective-permute-start.10 = (f32[8,5,128]{2,1,0:T(8,128)S(1)}, f32[8,5,128]{2,1,0:T(8,128)S(1)}, u32[]{:S(2)}, u32[]{:S(2)}) collective-permute-start(f32[8,5,128]{2,1,0:T(8,128)S(1)} %get-tuple-element.50), channel_id=1, source_target_pairs={{0,1},{1,0},{2,3},{3,2},{4,5},{5,4},{6,7},{7,6},{8,9},{9,8},{10,11... | collective-permute-start | bytes 61448 | tf_op jit(solution)/shard_map/ppermute | solution.py:145
  37.1 1.3 %collective-permute-start.9 = (f32[8,5,128]{2,1,0:T(8,128)S(1)}, f32[8,5,128]{2,1,0:T(8,128)S(1)}, u32[]{:S(2)}, u32[]{:S(2)}) collective-permute-start(f32[8,5,128]{2,1,0:T(8,128)S(1)} %get-tuple-element.49), channel_id=1, source_target_pairs={{0,7},{1,2},{2,1},{3,4},{4,3},{5,6},{6,5},{7,0},{8,15},{9,10},{10,... | collective-permute-start | bytes 61448 | tf_op jit(solution)/shard_map/ppermute | solution.py:42
  38.4 0.0 collective-permute-done.10
  38.4 2.1 %collective-permute-done.9 = f32[8,5,128]{2,1,0:T(8,128)S(1)} collective-permute-done((f32[8,5,128]{2,1,0:T(8,128)S(1)}, f32[8,5,128]{2,1,0:T(8,128)S(1)}, u32[]{:S(2)}, u32[]{:S(2)}) %collective-permute-start.9) | collective-permute-done | bytes 20512 | tf_op jit(solution)/shard_map/ppermute | solution.py:42
  40.5 0.1 collective-permute-start.11
  40.6 0.2 collective-permute-start.12
  40.9 3.5 %collective-permute-done.11.inner = f32[5,48,128]{2,1,0:T(8,128)S(1)} collective-permute-done((f32[5,48,128]{2,1,0:T(8,128)S(1)}, f32[5,48,128]{2,1,0:T(8,128)S(1)}, u32[]{:S(2)}, u32[]{:S(2)}) %collective-permute-start.11) | collective-permute-done | bytes 122912 | tf_op jit(solution)/shard_map/ppermute | solution.py:154
  44.3 3.4 %collective-permute-done.12.outer = f32[5,48,128]{2,1,0:T(8,128)S(1)} collective-permute-done((f32[5,48,128]{2,1,0:T(8,128)S(1)}, f32[5,48,128]{2,1,0:T(8,128)S(1)}, u32[]{:S(2)}, u32[]{:S(2)}) %collective-permute-start.12) | collective-permute-done | bytes 122912 | tf_op jit(solution)/shard_map/ppermute | solution.py:155
  47.7 1.4 %krylov.1 = (f32[8,40,128]{2,1,0:T(8,128)S(1)}, f32[8,40,128]{2,1,0:T(8,128)S(1)}, f32[128,128]{1,0:T(8,128)S(1)}) custom-call(f32[8,40,128]{2,1,0:T(8,128)S(1)} %fusion.2.own, f32[8,5,128]{2,1,0:T(8,128)S(1)} %get-tuple-element.52.left, f32[8,5,128]{2,1,0:T(8,128)S(1)} %get-tuple-element.51.right, f32[5,48,128]{2,1,0:T(8,128)S(1)} %collective-permute-done.11.inner, ...), custom_call_target="tpu_custom_call" | custom-call | tf_op jit(solution)/shard_map/krylov/pallas_call | solution.py:269
  49.1 15.5 %all_to_all.5 = f32[128,1,128]{2,1,0:T(1,128)S(1)} all-to-all(f32[128,1,128]{2,1,0:T(1,128)S(1)} %bitcast.32), channel_id=1, replica_groups=mesh['band_0'=4,'band_1'=4,'space_0'=4,'space_1'=2] {'band_0','band_1','..., dimensions={0} | all-to-all | bytes 131072 | tf_op jit(solution)/shard_map/all_to_all | solution.py:327
  64.6 0.9 %combine.1 = f32[8,40,128]{2,1,0:T(8,128)} custom-call(f32[128,128]{1,0:T(8,128)S(1)} %bitcast.31, f32[8,40,128]{2,1,0:T(8,128)S(1)} %fusion.2.own, f32[8,40,128]{2,1,0:T(8,128)S(1)} %get-tuple-element.43.first, f32[8,40,128]{2,1,0:T(8,128)S(1)} %get-tuple-element.44.second), custom_call_target="tpu_custom_call" | custom-call | tf_op jit(solution)/shard_map/combine/pallas_call | solution.py:313
  (15 shorter events, 0.3 us)
Async XLA Ops:
  0.0 0.7 %copy-start = (f32[8]{0:T(128)S(1)}, f32[8]{0:T(128)}, u32[]{:S(2)}) copy-start(f32[8]{0:T(128)} %occ.4) | copy-start | bytes 100
  2.6 8.9 %collective-permute-start = (f32[2,8,40,128]{3,2,1,0:T(8,128)S(1)}, f32[2,8,40,128]{3,2,1,0:T(8,128)S(1)}, u32[]{:S(2)}, u32[]{:S(2)}) collective-permute-start(f32[2,8,40,128]{3,2,1,0:T(8,128)S(1)} %bitcast.36), channel_id=1, source_target_pairs={{0,8},{1,33},{2,10},{3,35},{4,12},{5,37},{6,14},{7,39},{8,0},{9,41... | collective-permute-start | bytes 983048 | tf_op jit(solution)/shard_map/ppermute | solution.py:42
  5.1 7.4 %collective-permute-start.1 = (f32[2,8,40,128]{3,2,1,0:T(8,128)S(1)}, f32[2,8,40,128]{3,2,1,0:T(8,128)S(1)}, u32[]{:S(2)}, u32[]{:S(2)}) collective-permute-start(f32[2,8,40,128]{3,2,1,0:T(8,128)S(1)} %bitcast.35), channel_id=1, source_target_pairs={{0,24},{1,97},{2,26},{3,99},{4,28},{5,101},{6,30},{7,103},{8,16},{... | collective-permute-start | bytes 983048 | tf_op jit(solution)/shard_map/ppermute | solution.py:42
  10.1 6.8 %collective-permute-start.2 = (f32[2,8,40,128]{3,2,1,0:T(8,128)S(1)}, f32[2,8,40,128]{3,2,1,0:T(8,128)S(1)}, u32[]{:S(2)}, u32[]{:S(2)}) collective-permute-start(f32[2,8,40,128]{3,2,1,0:T(8,128)S(1)} %bitcast.34), channel_id=1, source_target_pairs={{0,8},{1,33},{2,10},{3,35},{4,12},{5,37},{6,14},{7,39},{8,0},{9,41... | collective-permute-start | bytes 983048 | tf_op jit(solution)/shard_map/ppermute | solution.py:42
  10.9 7.4 %collective-permute-start.4 = (f32[2,8,40,128]{3,2,1,0:T(8,128)S(1)}, f32[2,8,40,128]{3,2,1,0:T(8,128)S(1)}, u32[]{:S(2)}, u32[]{:S(2)}) collective-permute-start(f32[2,8,40,128]{3,2,1,0:T(8,128)S(1)} %bitcast.33), channel_id=1, source_target_pairs={{0,24},{1,97},{2,26},{3,99},{4,28},{5,101},{6,30},{7,103},{8,16},{... | collective-permute-start | bytes 983048 | tf_op jit(solution)/shard_map/ppermute | solution.py:42
  12.6 9.2 %collective-permute-start.3 = (f32[2,8,40,128]{3,2,1,0:T(8,128)S(1)}, f32[2,8,40,128]{3,2,1,0:T(8,128)S(1)}, u32[]{:S(2)}, u32[]{:S(2)}) collective-permute-start(f32[2,8,40,128]{3,2,1,0:T(8,128)S(1)} %add.35), channel_id=1, source_target_pairs={{0,24},{1,97},{2,26},{3,99},{4,28},{5,101},{6,30},{7,103},{8,16},{... | collective-permute-start | bytes 983048 | tf_op jit(solution)/shard_map/ppermute | solution.py:42
  14.9 6.9 %collective-permute-start.5 = (f32[2,8,40,128]{3,2,1,0:T(8,128)S(1)}, f32[2,8,40,128]{3,2,1,0:T(8,128)S(1)}, u32[]{:S(2)}, u32[]{:S(2)}) collective-permute-start(f32[2,8,40,128]{3,2,1,0:T(8,128)S(1)} %add.34), channel_id=1, source_target_pairs={{0,8},{1,33},{2,10},{3,35},{4,12},{5,37},{6,14},{7,39},{8,0},{9,41... | collective-permute-start | bytes 983048 | tf_op jit(solution)/shard_map/ppermute | solution.py:42
  21.9 4.2 %collective-permute-start.7 = (f32[8,40,128]{2,1,0:T(8,128)S(1)}, f32[8,40,128]{2,1,0:T(8,128)S(1)}, u32[]{:S(2)}, u32[]{:S(2)}) collective-permute-start(f32[8,40,128]{2,1,0:T(8,128)S(1)} %slice_bitcast_fusion.1), channel_id=1, source_target_pairs={{0,32},{1,9},{2,34},{3,11},{4,36},{5,13},{6,38},{7,15},{8,40},{9,1... | collective-permute-start | bytes 491528 | tf_op jit(solution)/shard_map/ppermute | solution.py:42
  23.0 6.9 %collective-permute-start.6 = (f32[8,40,128]{2,1,0:T(8,128)S(1)}, f32[8,40,128]{2,1,0:T(8,128)S(1)}, u32[]{:S(2)}, u32[]{:S(2)}) collective-permute-start(f32[8,40,128]{2,1,0:T(8,128)S(1)} %get-tuple-element.45), channel_id=1, source_target_pairs={{0,64},{1,17},{2,66},{3,19},{4,68},{5,21},{6,70},{7,23},{8,72},{9,... | collective-permute-start | bytes 491528 | tf_op jit(solution)/shard_map/ppermute | solution.py:42
  25.5 6.1 %collective-permute-start.8 = (f32[8,40,128]{2,1,0:T(8,128)S(1)}, f32[8,40,128]{2,1,0:T(8,128)S(1)}, u32[]{:S(2)}, u32[]{:S(2)}) collective-permute-start(f32[8,40,128]{2,1,0:T(8,128)S(1)} %get-tuple-element.46), channel_id=1, source_target_pairs={{0,96},{1,25},{2,98},{3,27},{4,100},{5,29},{6,102},{7,31},{8,104},... | collective-permute-start | bytes 491528 | tf_op jit(solution)/shard_map/ppermute | solution.py:42
  31.6 6.7 %collective-permute-start.10 = (f32[8,5,128]{2,1,0:T(8,128)S(1)}, f32[8,5,128]{2,1,0:T(8,128)S(1)}, u32[]{:S(2)}, u32[]{:S(2)}) collective-permute-start(f32[8,5,128]{2,1,0:T(8,128)S(1)} %get-tuple-element.50), channel_id=1, source_target_pairs={{0,1},{1,0},{2,3},{3,2},{4,5},{5,4},{6,7},{7,6},{8,9},{9,8},{10,11... | collective-permute-start | bytes 61448 | tf_op jit(solution)/shard_map/ppermute | solution.py:145
  37.1 3.3 %collective-permute-start.9 = (f32[8,5,128]{2,1,0:T(8,128)S(1)}, f32[8,5,128]{2,1,0:T(8,128)S(1)}, u32[]{:S(2)}, u32[]{:S(2)}) collective-permute-start(f32[8,5,128]{2,1,0:T(8,128)S(1)} %get-tuple-element.49), channel_id=1, source_target_pairs={{0,7},{1,2},{2,1},{3,4},{4,3},{5,6},{6,5},{7,0},{8,15},{9,10},{10,... | collective-permute-start | bytes 61448 | tf_op jit(solution)/shard_map/ppermute | solution.py:42
  40.5 3.8 %collective-permute-start.11 = (f32[5,48,128]{2,1,0:T(8,128)S(1)}, f32[5,48,128]{2,1,0:T(8,128)S(1)}, u32[]{:S(2)}, u32[]{:S(2)}) collective-permute-start(f32[5,48,128]{2,1,0:T(8,128)S(1)} %get-tuple-element.48), channel_id=1, source_target_pairs={{0,8},{8,0},{16,24},{24,16},{32,40},{40,32},{48,56},{56,48},{64,72... | collective-permute-start | bytes 368648 | tf_op jit(solution)/shard_map/ppermute | solution.py:154
  40.6 7.1 %collective-permute-start.12 = (f32[5,48,128]{2,1,0:T(8,128)S(1)}, f32[5,48,128]{2,1,0:T(8,128)S(1)}, u32[]{:S(2)}, u32[]{:S(2)}) collective-permute-start(f32[5,48,128]{2,1,0:T(8,128)S(1)} %get-tuple-element.47), channel_id=1, source_target_pairs={{0,120},{8,16},{16,8},{24,32},{32,24},{40,48},{48,40},{56,64},{64,... | collective-permute-start | bytes 368648 | tf_op jit(solution)/shard_map/ppermute | solution.py:155

commit v7 on v6

--- a/solution.py
+++ b/solution.py
@@ -117,7 +117,7 @@
     a_first, a_last, b_first, b_last = lax.optimization_barrier((a_first, a_last, b_first, b_last))
     a0, b0 = a0 + a_first + a_last, b0 + b_first + b_last
     total = a0[0]
-    for block, k in ((b0[0], 2), (a0[1], 1), (b0[1], 3)):
+    for block, k in ((a0[1], 1), (b0[1], 3), (b0[0], 2)):
         total = total + send(block, partner(1, k))
     return total
 

time: 65.7 us -> 65.4 us (level)
    ppermute x1, starting transfers between devices: 5.45 us -> 6.19 us  [halo(): lax.ppermute(jnp.where(first, right, left), 'space_1', [(0, 1), (1, 0)])]
where the time goes in v7:
time: 65.4 us; the launch traced here: 65.2 us
  starting transfers between devices  19.9 us (30%)
  waiting for transfers between devices  19.9 us (30%)
  blocking collectives  15.5 us (24%)
  Pallas kernels  8.78 us (13%)
  local copies, waits for them, and re-layouts  0.7 us (1%)
    all_to_all x1, blocking collectives, local(): lax.all_to_all(lines[:, None], EVERY, split_axis=0, concat_axis=0, tiled=...  15.5 us
    ppermute x10, starting transfers between devices, send(): return lax.ppermute(value, EVERY, pairs)  13.4 us
    ppermute x10, waiting for transfers between devices, send(): return lax.ppermute(value, EVERY, pairs)  13 us
    pallas_call x3, Pallas kernels, density_part(): pl.pallas_call(functools.partial(density_body, firsts, scale), out_shape=...  6.52 us
    ppermute x1, starting transfers between devices, halo(): lax.ppermute(jnp.where(first, right, left), 'space_1', [(0, 1), (1, 0)])  6.19 us
    ppermute x1, waiting for transfers between devices, halo(): inner = lax.ppermute(jnp.where(even, last_rows, first_rows), BAND, inner)  3.49 us
    ppermute x1, waiting for transfers between devices, halo(): outer = lax.ppermute(jnp.where(even, first_rows, last_rows), BAND, outer)  3.41 us
    pallas_call x1, Pallas kernels, krylov(): pl.pallas_call(krylov_body, out_shape=(field, field, jax.ShapeDtypeStruct...  1.39 us
  transfers between devices with their start and end apart: 13, of which 9 were waited for; matrix products, arithmetic and copies ran while one was open for 0% of the time, Pallas kernels for 7%

profile of v7, /device:TPU:1, one launch (start us, length us, event | category | flops | bytes accessed | tf_op | source)
XLA Modules:
  0.0 65.2 jit_solution(6443805266780668939)
XLA Ops:
  0.0 0.7 %copy-done = f32[8]{0:T(128)S(1)} copy-done((f32[8]{0:T(128)S(1)}, f32[8]{0:T(128)}, u32[]{:S(2)}) %copy-start) | copy-done | bytes 56
  0.7 1.9 %density.4 = (f32[2,320,128]{2,1,0:T(8,128)S(1)}, f32[2,320,128]{2,1,0:T(8,128)S(1)}) custom-call(bf16[8,5120,128]{2,1,0:T(8,128)(2,1)} %bitcast.37, f32[8]{0:T(128)S(1)} %copy-done), custom_call_target="tpu_custom_call" | custom-call | bytes 2621440 | tf_op jit(solution)/shard_map/density/pallas_call | solution.py:89
  2.6 2.5 %collective-permute-start = (f32[2,8,40,128]{3,2,1,0:T(8,128)S(1)}, f32[2,8,40,128]{3,2,1,0:T(8,128)S(1)}, u32[]{:S(2)}, u32[]{:S(2)}) collective-permute-start(f32[2,8,40,128]{3,2,1,0:T(8,128)S(1)} %bitcast.36), channel_id=1, source_target_pairs={{0,8},{1,33},{2,10},{3,35},{4,12},{5,37},{6,14},{7,39},{8,0},{9,41... | collective-permute-start | bytes 983048 | tf_op jit(solution)/shard_map/ppermute | solution.py:42
  5.1 2.2 %collective-permute-start.1 = (f32[2,8,40,128]{3,2,1,0:T(8,128)S(1)}, f32[2,8,40,128]{3,2,1,0:T(8,128)S(1)}, u32[]{:S(2)}, u32[]{:S(2)}) collective-permute-start(f32[2,8,40,128]{3,2,1,0:T(8,128)S(1)} %bitcast.35), channel_id=1, source_target_pairs={{0,24},{1,97},{2,26},{3,99},{4,28},{5,101},{6,30},{7,103},{8,16},{... | collective-permute-start | bytes 983048 | tf_op jit(solution)/shard_map/ppermute | solution.py:42
  7.4 2.7 %density.3 = (f32[2,320,128]{2,1,0:T(8,128)S(1)}, f32[2,320,128]{2,1,0:T(8,128)S(1)}, f32[2,320,128]{2,1,0:T(8,128)S(1)}, f32[2,320,128]{2,1,0:T(8,128)S(1)}) custom-call(bf16[8,5120,128]{2,1,0:T(8,128)(2,1)} %bitcast.38, f32[8]{0:T(128)S(1)} %copy-done), custom_call_target="tpu_custom_call" | custom-call | bytes 2621440 | tf_op jit(solution)/shard_map/density/pallas_call | solution.py:89
  10.1 0.8 %collective-permute-start.2 = (f32[2,8,40,128]{3,2,1,0:T(8,128)S(1)}, f32[2,8,40,128]{3,2,1,0:T(8,128)S(1)}, u32[]{:S(2)}, u32[]{:S(2)}) collective-permute-start(f32[2,8,40,128]{3,2,1,0:T(8,128)S(1)} %bitcast.34), channel_id=1, source_target_pairs={{0,8},{1,33},{2,10},{3,35},{4,12},{5,37},{6,14},{7,39},{8,0},{9,41... | collective-permute-start | bytes 983048 | tf_op jit(solution)/shard_map/ppermute | solution.py:42
  10.9 0.6 collective-permute-start.4
  11.5 0.0 collective-permute-done
  11.5 1.0 %collective-permute-done.1 = f32[2,8,40,128]{3,2,1,0:T(8,128)S(1)} collective-permute-done((f32[2,8,40,128]{3,2,1,0:T(8,128)S(1)}, f32[2,8,40,128]{3,2,1,0:T(8,128)S(1)}, u32[]{:S(2)}, u32[]{:S(2)}) %collective-permute-start.1) | collective-permute-done | bytes 327712 | tf_op jit(solution)/shard_map/ppermute | solution.py:42
  12.6 2.3 %collective-permute-start.3 = (f32[2,8,40,128]{3,2,1,0:T(8,128)S(1)}, f32[2,8,40,128]{3,2,1,0:T(8,128)S(1)}, u32[]{:S(2)}, u32[]{:S(2)}) collective-permute-start(f32[2,8,40,128]{3,2,1,0:T(8,128)S(1)} %add.35), channel_id=1, source_target_pairs={{0,24},{1,97},{2,26},{3,99},{4,28},{5,101},{6,30},{7,103},{8,16},{... | collective-permute-start | bytes 983048 | tf_op jit(solution)/shard_map/ppermute | solution.py:42
  14.9 0.0 collective-permute-start.5
  14.9 1.9 %density.5 = (f32[2,320,128]{2,1,0:T(8,128)S(1)}, f32[2,320,128]{2,1,0:T(8,128)S(1)}) custom-call(bf16[8,5120,128]{2,1,0:T(8,128)(2,1)} %bitcast.39, f32[8]{0:T(128)S(1)} %copy-done), custom_call_target="tpu_custom_call" | custom-call | bytes 2621440 | tf_op jit(solution)/shard_map/density/pallas_call | solution.py:89
  16.9 0.0 collective-permute-done.2
  16.9 1.5 %collective-permute-done.4 = f32[2,8,40,128]{3,2,1,0:T(8,128)S(1)} collective-permute-done((f32[2,8,40,128]{3,2,1,0:T(8,128)S(1)}, f32[2,8,40,128]{3,2,1,0:T(8,128)S(1)}, u32[]{:S(2)}, u32[]{:S(2)}) %collective-permute-start.4) | collective-permute-done | bytes 327712 | tf_op jit(solution)/shard_map/ppermute | solution.py:42
  18.3 3.5 %collective-permute-done.3 = f32[2,8,40,128]{3,2,1,0:T(8,128)S(1)} collective-permute-done((f32[2,8,40,128]{3,2,1,0:T(8,128)S(1)}, f32[2,8,40,128]{3,2,1,0:T(8,128)S(1)}, u32[]{:S(2)}, u32[]{:S(2)}) %collective-permute-start.3) | collective-permute-done | bytes 327712 | tf_op jit(solution)/shard_map/ppermute | solution.py:42
  21.8 0.0 collective-permute-done.5
  21.9 1.0 %collective-permute-start.6 = (f32[8,40,128]{2,1,0:T(8,128)S(1)}, f32[8,40,128]{2,1,0:T(8,128)S(1)}, u32[]{:S(2)}, u32[]{:S(2)}) collective-permute-start(f32[8,40,128]{2,1,0:T(8,128)S(1)} %slice_bitcast_fusion.2), channel_id=1, source_target_pairs={{0,32},{1,9},{2,34},{3,11},{4,36},{5,13},{6,38},{7,15},{8,40},{9,1... | collective-permute-start | bytes 491528 | tf_op jit(solution)/shard_map/ppermute | solution.py:42
  23.0 1.9 %collective-permute-start.7 = (f32[8,40,128]{2,1,0:T(8,128)S(1)}, f32[8,40,128]{2,1,0:T(8,128)S(1)}, u32[]{:S(2)}, u32[]{:S(2)}) collective-permute-start(f32[8,40,128]{2,1,0:T(8,128)S(1)} %get-tuple-element.45), channel_id=1, source_target_pairs={{0,96},{1,25},{2,98},{3,27},{4,100},{5,29},{6,102},{7,31},{8,104},... | collective-permute-start | bytes 491528 | tf_op jit(solution)/shard_map/ppermute | solution.py:42
  24.9 0.7 %collective-permute-start.8 = (f32[8,40,128]{2,1,0:T(8,128)S(1)}, f32[8,40,128]{2,1,0:T(8,128)S(1)}, u32[]{:S(2)}, u32[]{:S(2)}) collective-permute-start(f32[8,40,128]{2,1,0:T(8,128)S(1)} %get-tuple-element.46), channel_id=1, source_target_pairs={{0,64},{1,17},{2,66},{3,19},{4,68},{5,21},{6,70},{7,23},{8,72},{9,... | collective-permute-start | bytes 491528 | tf_op jit(solution)/shard_map/ppermute | solution.py:42
  25.6 0.5 collective-permute-done.6
  26.2 2.7 %collective-permute-done.7 = f32[8,40,128]{2,1,0:T(8,128)S(1)} collective-permute-done((f32[8,40,128]{2,1,0:T(8,128)S(1)}, f32[8,40,128]{2,1,0:T(8,128)S(1)}, u32[]{:S(2)}, u32[]{:S(2)}) %collective-permute-start.7) | collective-permute-done | bytes 163872 | tf_op jit(solution)/shard_map/ppermute | solution.py:42
  28.9 1.7 %collective-permute-done.8 = f32[8,40,128]{2,1,0:T(8,128)S(1)} collective-permute-done((f32[8,40,128]{2,1,0:T(8,128)S(1)}, f32[8,40,128]{2,1,0:T(8,128)S(1)}, u32[]{:S(2)}, u32[]{:S(2)}) %collective-permute-start.8) | collective-permute-done | bytes 163872 | tf_op jit(solution)/shard_map/ppermute | solution.py:42
  30.6 6.2 %collective-permute-start.10 = (f32[8,5,128]{2,1,0:T(8,128)S(1)}, f32[8,5,128]{2,1,0:T(8,128)S(1)}, u32[]{:S(2)}, u32[]{:S(2)}) collective-permute-start(f32[8,5,128]{2,1,0:T(8,128)S(1)} %get-tuple-element.50), channel_id=1, source_target_pairs={{0,1},{1,0},{2,3},{3,2},{4,5},{5,4},{6,7},{7,6},{8,9},{9,8},{10,11... | collective-permute-start | bytes 61448 | tf_op jit(solution)/shard_map/ppermute | solution.py:145
  36.8 1.3 %collective-permute-start.9 = (f32[8,5,128]{2,1,0:T(8,128)S(1)}, f32[8,5,128]{2,1,0:T(8,128)S(1)}, u32[]{:S(2)}, u32[]{:S(2)}) collective-permute-start(f32[8,5,128]{2,1,0:T(8,128)S(1)} %get-tuple-element.49), channel_id=1, source_target_pairs={{0,7},{1,2},{2,1},{3,4},{4,3},{5,6},{6,5},{7,0},{8,15},{9,10},{10,... | collective-permute-start | bytes 61448 | tf_op jit(solution)/shard_map/ppermute | solution.py:42
  38.1 2.1 %collective-permute-done.9 = f32[8,5,128]{2,1,0:T(8,128)S(1)} collective-permute-done((f32[8,5,128]{2,1,0:T(8,128)S(1)}, f32[8,5,128]{2,1,0:T(8,128)S(1)}, u32[]{:S(2)}, u32[]{:S(2)}) %collective-permute-start.9) | collective-permute-done | bytes 20512 | tf_op jit(solution)/shard_map/ppermute | solution.py:42
  40.3 0.1 collective-permute-start.11
  40.3 0.2 collective-permute-start.12
  40.6 3.5 %collective-permute-done.11.inner = f32[5,48,128]{2,1,0:T(8,128)S(1)} collective-permute-done((f32[5,48,128]{2,1,0:T(8,128)S(1)}, f32[5,48,128]{2,1,0:T(8,128)S(1)}, u32[]{:S(2)}, u32[]{:S(2)}) %collective-permute-start.11) | collective-permute-done | bytes 122912 | tf_op jit(solution)/shard_map/ppermute | solution.py:154
  44.1 3.4 %collective-permute-done.12.outer = f32[5,48,128]{2,1,0:T(8,128)S(1)} collective-permute-done((f32[5,48,128]{2,1,0:T(8,128)S(1)}, f32[5,48,128]{2,1,0:T(8,128)S(1)}, u32[]{:S(2)}, u32[]{:S(2)}) %collective-permute-start.12) | collective-permute-done | bytes 122912 | tf_op jit(solution)/shard_map/ppermute | solution.py:155
  47.5 1.4 %krylov.1 = (f32[8,40,128]{2,1,0:T(8,128)S(1)}, f32[8,40,128]{2,1,0:T(8,128)S(1)}, f32[128,128]{1,0:T(8,128)S(1)}) custom-call(f32[8,40,128]{2,1,0:T(8,128)S(1)} %fusion.2.own, f32[8,5,128]{2,1,0:T(8,128)S(1)} %get-tuple-element.52.left, f32[8,5,128]{2,1,0:T(8,128)S(1)} %get-tuple-element.51.right, f32[5,48,128]{2,1,0:T(8,128)S(1)} %collective-permute-done.11.inner, ...), custom_call_target="tpu_custom_call" | custom-call | tf_op jit(solution)/shard_map/krylov/pallas_call | solution.py:269
  48.9 15.5 %all_to_all.5 = f32[128,1,128]{2,1,0:T(1,128)S(1)} all-to-all(f32[128,1,128]{2,1,0:T(1,128)S(1)} %bitcast.32), channel_id=1, replica_groups=mesh['band_0'=4,'band_1'=4,'space_0'=4,'space_1'=2] {'band_0','band_1','..., dimensions={0} | all-to-all | bytes 131072 | tf_op jit(solution)/shard_map/all_to_all | solution.py:327
  64.4 0.9 %combine.1 = f32[8,40,128]{2,1,0:T(8,128)} custom-call(f32[128,128]{1,0:T(8,128)S(1)} %bitcast.31, f32[8,40,128]{2,1,0:T(8,128)S(1)} %fusion.2.own, f32[8,40,128]{2,1,0:T(8,128)S(1)} %get-tuple-element.43.first, f32[8,40,128]{2,1,0:T(8,128)S(1)} %get-tuple-element.44.second), custom_call_target="tpu_custom_call" | custom-call | tf_op jit(solution)/shard_map/combine/pallas_call | solution.py:313
  (15 shorter events, 0.3 us)
Async XLA Ops:
  0.0 0.7 %copy-start = (f32[8]{0:T(128)S(1)}, f32[8]{0:T(128)}, u32[]{:S(2)}) copy-start(f32[8]{0:T(128)} %occ.4) | copy-start | bytes 100
  2.6 8.9 %collective-permute-start = (f32[2,8,40,128]{3,2,1,0:T(8,128)S(1)}, f32[2,8,40,128]{3,2,1,0:T(8,128)S(1)}, u32[]{:S(2)}, u32[]{:S(2)}) collective-permute-start(f32[2,8,40,128]{3,2,1,0:T(8,128)S(1)} %bitcast.36), channel_id=1, source_target_pairs={{0,8},{1,33},{2,10},{3,35},{4,12},{5,37},{6,14},{7,39},{8,0},{9,41... | collective-permute-start | bytes 983048 | tf_op jit(solution)/shard_map/ppermute | solution.py:42
  5.1 7.4 %collective-permute-start.1 = (f32[2,8,40,128]{3,2,1,0:T(8,128)S(1)}, f32[2,8,40,128]{3,2,1,0:T(8,128)S(1)}, u32[]{:S(2)}, u32[]{:S(2)}) collective-permute-start(f32[2,8,40,128]{3,2,1,0:T(8,128)S(1)} %bitcast.35), channel_id=1, source_target_pairs={{0,24},{1,97},{2,26},{3,99},{4,28},{5,101},{6,30},{7,103},{8,16},{... | collective-permute-start | bytes 983048 | tf_op jit(solution)/shard_map/ppermute | solution.py:42
  10.1 6.8 %collective-permute-start.2 = (f32[2,8,40,128]{3,2,1,0:T(8,128)S(1)}, f32[2,8,40,128]{3,2,1,0:T(8,128)S(1)}, u32[]{:S(2)}, u32[]{:S(2)}) collective-permute-start(f32[2,8,40,128]{3,2,1,0:T(8,128)S(1)} %bitcast.34), channel_id=1, source_target_pairs={{0,8},{1,33},{2,10},{3,35},{4,12},{5,37},{6,14},{7,39},{8,0},{9,41... | collective-permute-start | bytes 983048 | tf_op jit(solution)/shard_map/ppermute | solution.py:42
  10.9 7.4 %collective-permute-start.4 = (f32[2,8,40,128]{3,2,1,0:T(8,128)S(1)}, f32[2,8,40,128]{3,2,1,0:T(8,128)S(1)}, u32[]{:S(2)}, u32[]{:S(2)}) collective-permute-start(f32[2,8,40,128]{3,2,1,0:T(8,128)S(1)} %bitcast.33), channel_id=1, source_target_pairs={{0,24},{1,97},{2,26},{3,99},{4,28},{5,101},{6,30},{7,103},{8,16},{... | collective-permute-start | bytes 983048 | tf_op jit(solution)/shard_map/ppermute | solution.py:42
  12.6 9.2 %collective-permute-start.3 = (f32[2,8,40,128]{3,2,1,0:T(8,128)S(1)}, f32[2,8,40,128]{3,2,1,0:T(8,128)S(1)}, u32[]{:S(2)}, u32[]{:S(2)}) collective-permute-start(f32[2,8,40,128]{3,2,1,0:T(8,128)S(1)} %add.35), channel_id=1, source_target_pairs={{0,24},{1,97},{2,26},{3,99},{4,28},{5,101},{6,30},{7,103},{8,16},{... | collective-permute-start | bytes 983048 | tf_op jit(solution)/shard_map/ppermute | solution.py:42
  14.9 6.9 %collective-permute-start.5 = (f32[2,8,40,128]{3,2,1,0:T(8,128)S(1)}, f32[2,8,40,128]{3,2,1,0:T(8,128)S(1)}, u32[]{:S(2)}, u32[]{:S(2)}) collective-permute-start(f32[2,8,40,128]{3,2,1,0:T(8,128)S(1)} %add.34), channel_id=1, source_target_pairs={{0,8},{1,33},{2,10},{3,35},{4,12},{5,37},{6,14},{7,39},{8,0},{9,41... | collective-permute-start | bytes 983048 | tf_op jit(solution)/shard_map/ppermute | solution.py:42
  21.9 4.2 %collective-permute-start.6 = (f32[8,40,128]{2,1,0:T(8,128)S(1)}, f32[8,40,128]{2,1,0:T(8,128)S(1)}, u32[]{:S(2)}, u32[]{:S(2)}) collective-permute-start(f32[8,40,128]{2,1,0:T(8,128)S(1)} %slice_bitcast_fusion.2), channel_id=1, source_target_pairs={{0,32},{1,9},{2,34},{3,11},{4,36},{5,13},{6,38},{7,15},{8,40},{9,1... | collective-permute-start | bytes 491528 | tf_op jit(solution)/shard_map/ppermute | solution.py:42
  23.0 5.9 %collective-permute-start.7 = (f32[8,40,128]{2,1,0:T(8,128)S(1)}, f32[8,40,128]{2,1,0:T(8,128)S(1)}, u32[]{:S(2)}, u32[]{:S(2)}) collective-permute-start(f32[8,40,128]{2,1,0:T(8,128)S(1)} %get-tuple-element.45), channel_id=1, source_target_pairs={{0,96},{1,25},{2,98},{3,27},{4,100},{5,29},{6,102},{7,31},{8,104},... | collective-permute-start | bytes 491528 | tf_op jit(solution)/shard_map/ppermute | solution.py:42
  24.9 5.7 %collective-permute-start.8 = (f32[8,40,128]{2,1,0:T(8,128)S(1)}, f32[8,40,128]{2,1,0:T(8,128)S(1)}, u32[]{:S(2)}, u32[]{:S(2)}) collective-permute-start(f32[8,40,128]{2,1,0:T(8,128)S(1)} %get-tuple-element.46), channel_id=1, source_target_pairs={{0,64},{1,17},{2,66},{3,19},{4,68},{5,21},{6,70},{7,23},{8,72},{9,... | collective-permute-start | bytes 491528 | tf_op jit(solution)/shard_map/ppermute | solution.py:42
  30.6 7.5 %collective-permute-start.10 = (f32[8,5,128]{2,1,0:T(8,128)S(1)}, f32[8,5,128]{2,1,0:T(8,128)S(1)}, u32[]{:S(2)}, u32[]{:S(2)}) collective-permute-start(f32[8,5,128]{2,1,0:T(8,128)S(1)} %get-tuple-element.50), channel_id=1, source_target_pairs={{0,1},{1,0},{2,3},{3,2},{4,5},{5,4},{6,7},{7,6},{8,9},{9,8},{10,11... | collective-permute-start | bytes 61448 | tf_op jit(solution)/shard_map/ppermute | solution.py:145
  36.8 3.3 %collective-permute-start.9 = (f32[8,5,128]{2,1,0:T(8,128)S(1)}, f32[8,5,128]{2,1,0:T(8,128)S(1)}, u32[]{:S(2)}, u32[]{:S(2)}) collective-permute-start(f32[8,5,128]{2,1,0:T(8,128)S(1)} %get-tuple-element.49), channel_id=1, source_target_pairs={{0,7},{1,2},{2,1},{3,4},{4,3},{5,6},{6,5},{7,0},{8,15},{9,10},{10,... | collective-permute-start | bytes 61448 | tf_op jit(solution)/shard_map/ppermute | solution.py:42
  40.3 3.8 %collective-permute-start.11 = (f32[5,48,128]{2,1,0:T(8,128)S(1)}, f32[5,48,128]{2,1,0:T(8,128)S(1)}, u32[]{:S(2)}, u32[]{:S(2)}) collective-permute-start(f32[5,48,128]{2,1,0:T(8,128)S(1)} %get-tuple-element.48), channel_id=1, source_target_pairs={{0,8},{8,0},{16,24},{24,16},{32,40},{40,32},{48,56},{56,48},{64,72... | collective-permute-start | bytes 368648 | tf_op jit(solution)/shard_map/ppermute | solution.py:154
  40.3 7.1 %collective-permute-start.12 = (f32[5,48,128]{2,1,0:T(8,128)S(1)}, f32[5,48,128]{2,1,0:T(8,128)S(1)}, u32[]{:S(2)}, u32[]{:S(2)}) collective-permute-start(f32[5,48,128]{2,1,0:T(8,128)S(1)} %get-tuple-element.47), channel_id=1, source_target_pairs={{0,120},{8,16},{16,8},{24,32},{32,24},{40,48},{48,40},{56,64},{64,... | collective-permute-start | bytes 368648 | tf_op jit(solution)/shard_map/ppermute | solution.py:155

commit v8 on v7

--- a/solution.py
+++ b/solution.py
@@ -141,10 +141,10 @@
 def halo(field):
     first = lax.axis_index("space_1") == 0
     left, right = field[:, :REACH], field[:, -REACH:]
-    far = send(jnp.where(first, left, right), beside())
+    space = lax.axis_index(SPACE)
+    border = jnp.where(first, left, right)
+    far = send(jnp.where((space > 0) & (space < 7), border, 0.0), beside())
     near = lax.ppermute(jnp.where(first, right, left), "space_1", [(0, 1), (1, 0)])
-    space = lax.axis_index(SPACE)
-    far = jnp.where((space > 0) & (space < 7), far, 0.0)
     left, right = jnp.where(first, far, near), jnp.where(first, near, far)
     wide = jnp.concatenate([left[:, -SIDEWAYS:], field, right[:, :SIDEWAYS]], 1)
     even = lax.axis_index("band_1") % 2 == 0

time: 65.4 us -> 65.4 us (level)
  no operation moved by 1% of the time
where the time goes in v8:
time: 65.4 us; the launch traced here: 65.2 us
  starting transfers between devices  19.9 us (30%)
  waiting for transfers between devices  19.9 us (30%)
  blocking collectives  15.5 us (24%)
  Pallas kernels  8.78 us (13%)
  local copies, waits for them, and re-layouts  0.7 us (1%)
    all_to_all x1, blocking collectives, local(): lax.all_to_all(lines[:, None], EVERY, split_axis=0, concat_axis=0, tiled=...  15.5 us
    ppermute x10, starting transfers between devices, send(): return lax.ppermute(value, EVERY, pairs)  13.4 us
    ppermute x10, waiting for transfers between devices, send(): return lax.ppermute(value, EVERY, pairs)  13 us
    pallas_call x3, Pallas kernels, density_part(): pl.pallas_call(functools.partial(density_body, firsts, scale), out_shape=...  6.52 us
    ppermute x1, starting transfers between devices, halo(): lax.ppermute(jnp.where(first, right, left), 'space_1', [(0, 1), (1, 0)])  6.19 us
    ppermute x1, waiting for transfers between devices, halo(): inner = lax.ppermute(jnp.where(even, last_rows, first_rows), BAND, inner)  3.49 us
    ppermute x1, waiting for transfers between devices, halo(): outer = lax.ppermute(jnp.where(even, first_rows, last_rows), BAND, outer)  3.41 us
    pallas_call x1, Pallas kernels, krylov(): pl.pallas_call(krylov_body, out_shape=(field, field, jax.ShapeDtypeStruct...  1.39 us
  transfers between devices with their start and end apart: 13, of which 9 were waited for; matrix products, arithmetic and copies ran while one was open for 0% of the time, Pallas kernels for 7%

profile of v8, /device:TPU:1, one launch (start us, length us, event | category | flops | bytes accessed | tf_op | source)
XLA Modules:
  0.0 65.2 jit_solution(3641219401547528286)
XLA Ops:
  0.0 0.7 %copy-done = f32[8]{0:T(128)S(1)} copy-done((f32[8]{0:T(128)S(1)}, f32[8]{0:T(128)}, u32[]{:S(2)}) %copy-start) | copy-done | bytes 56
  0.7 1.9 %density.4 = (f32[2,320,128]{2,1,0:T(8,128)S(1)}, f32[2,320,128]{2,1,0:T(8,128)S(1)}) custom-call(bf16[8,5120,128]{2,1,0:T(8,128)(2,1)} %bitcast.37, f32[8]{0:T(128)S(1)} %copy-done), custom_call_target="tpu_custom_call" | custom-call | bytes 2621440 | tf_op jit(solution)/shard_map/density/pallas_call | solution.py:89
  2.6 2.5 %collective-permute-start = (f32[2,8,40,128]{3,2,1,0:T(8,128)S(1)}, f32[2,8,40,128]{3,2,1,0:T(8,128)S(1)}, u32[]{:S(2)}, u32[]{:S(2)}) collective-permute-start(f32[2,8,40,128]{3,2,1,0:T(8,128)S(1)} %bitcast.36), channel_id=1, source_target_pairs={{0,8},{1,33},{2,10},{3,35},{4,12},{5,37},{6,14},{7,39},{8,0},{9,41... | collective-permute-start | bytes 983048 | tf_op jit(solution)/shard_map/ppermute | solution.py:42
  5.1 2.2 %collective-permute-start.1 = (f32[2,8,40,128]{3,2,1,0:T(8,128)S(1)}, f32[2,8,40,128]{3,2,1,0:T(8,128)S(1)}, u32[]{:S(2)}, u32[]{:S(2)}) collective-permute-start(f32[2,8,40,128]{3,2,1,0:T(8,128)S(1)} %bitcast.35), channel_id=1, source_target_pairs={{0,24},{1,97},{2,26},{3,99},{4,28},{5,101},{6,30},{7,103},{8,16},{... | collective-permute-start | bytes 983048 | tf_op jit(solution)/shard_map/ppermute | solution.py:42
  7.4 2.7 %density.3 = (f32[2,320,128]{2,1,0:T(8,128)S(1)}, f32[2,320,128]{2,1,0:T(8,128)S(1)}, f32[2,320,128]{2,1,0:T(8,128)S(1)}, f32[2,320,128]{2,1,0:T(8,128)S(1)}) custom-call(bf16[8,5120,128]{2,1,0:T(8,128)(2,1)} %bitcast.38, f32[8]{0:T(128)S(1)} %copy-done), custom_call_target="tpu_custom_call" | custom-call | bytes 2621440 | tf_op jit(solution)/shard_map/density/pallas_call | solution.py:89
  10.1 0.8 %collective-permute-start.2 = (f32[2,8,40,128]{3,2,1,0:T(8,128)S(1)}, f32[2,8,40,128]{3,2,1,0:T(8,128)S(1)}, u32[]{:S(2)}, u32[]{:S(2)}) collective-permute-start(f32[2,8,40,128]{3,2,1,0:T(8,128)S(1)} %bitcast.34), channel_id=1, source_target_pairs={{0,8},{1,33},{2,10},{3,35},{4,12},{5,37},{6,14},{7,39},{8,0},{9,41... | collective-permute-start | bytes 983048 | tf_op jit(solution)/shard_map/ppermute | solution.py:42
  10.9 0.6 collective-permute-start.4
  11.5 0.0 collective-permute-done
  11.5 1.0 %collective-permute-done.1 = f32[2,8,40,128]{3,2,1,0:T(8,128)S(1)} collective-permute-done((f32[2,8,40,128]{3,2,1,0:T(8,128)S(1)}, f32[2,8,40,128]{3,2,1,0:T(8,128)S(1)}, u32[]{:S(2)}, u32[]{:S(2)}) %collective-permute-start.1) | collective-permute-done | bytes 327712 | tf_op jit(solution)/shard_map/ppermute | solution.py:42
  12.6 2.3 %collective-permute-start.3 = (f32[2,8,40,128]{3,2,1,0:T(8,128)S(1)}, f32[2,8,40,128]{3,2,1,0:T(8,128)S(1)}, u32[]{:S(2)}, u32[]{:S(2)}) collective-permute-start(f32[2,8,40,128]{3,2,1,0:T(8,128)S(1)} %add.35), channel_id=1, source_target_pairs={{0,24},{1,97},{2,26},{3,99},{4,28},{5,101},{6,30},{7,103},{8,16},{... | collective-permute-start | bytes 983048 | tf_op jit(solution)/shard_map/ppermute | solution.py:42
  14.9 0.0 collective-permute-start.5
  14.9 1.9 %density.5 = (f32[2,320,128]{2,1,0:T(8,128)S(1)}, f32[2,320,128]{2,1,0:T(8,128)S(1)}) custom-call(bf16[8,5120,128]{2,1,0:T(8,128)(2,1)} %bitcast.39, f32[8]{0:T(128)S(1)} %copy-done), custom_call_target="tpu_custom_call" | custom-call | bytes 2621440 | tf_op jit(solution)/shard_map/density/pallas_call | solution.py:89
  16.9 0.0 collective-permute-done.2
  16.9 1.5 %collective-permute-done.4 = f32[2,8,40,128]{3,2,1,0:T(8,128)S(1)} collective-permute-done((f32[2,8,40,128]{3,2,1,0:T(8,128)S(1)}, f32[2,8,40,128]{3,2,1,0:T(8,128)S(1)}, u32[]{:S(2)}, u32[]{:S(2)}) %collective-permute-start.4) | collective-permute-done | bytes 327712 | tf_op jit(solution)/shard_map/ppermute | solution.py:42
  18.3 3.5 %collective-permute-done.3 = f32[2,8,40,128]{3,2,1,0:T(8,128)S(1)} collective-permute-done((f32[2,8,40,128]{3,2,1,0:T(8,128)S(1)}, f32[2,8,40,128]{3,2,1,0:T(8,128)S(1)}, u32[]{:S(2)}, u32[]{:S(2)}) %collective-permute-start.3) | collective-permute-done | bytes 327712 | tf_op jit(solution)/shard_map/ppermute | solution.py:42
  21.9 1.0 %collective-permute-start.6 = (f32[8,40,128]{2,1,0:T(8,128)S(1)}, f32[8,40,128]{2,1,0:T(8,128)S(1)}, u32[]{:S(2)}, u32[]{:S(2)}) collective-permute-start(f32[8,40,128]{2,1,0:T(8,128)S(1)} %slice_bitcast_fusion.2), channel_id=1, source_target_pairs={{0,32},{1,9},{2,34},{3,11},{4,36},{5,13},{6,38},{7,15},{8,40},{9,1... | collective-permute-start | bytes 491528 | tf_op jit(solution)/shard_map/ppermute | solution.py:42
  23.0 1.9 %collective-permute-start.7 = (f32[8,40,128]{2,1,0:T(8,128)S(1)}, f32[8,40,128]{2,1,0:T(8,128)S(1)}, u32[]{:S(2)}, u32[]{:S(2)}) collective-permute-start(f32[8,40,128]{2,1,0:T(8,128)S(1)} %get-tuple-element.45), channel_id=1, source_target_pairs={{0,96},{1,25},{2,98},{3,27},{4,100},{5,29},{6,102},{7,31},{8,104},... | collective-permute-start | bytes 491528 | tf_op jit(solution)/shard_map/ppermute | solution.py:42
  24.9 0.7 %collective-permute-start.8 = (f32[8,40,128]{2,1,0:T(8,128)S(1)}, f32[8,40,128]{2,1,0:T(8,128)S(1)}, u32[]{:S(2)}, u32[]{:S(2)}) collective-permute-start(f32[8,40,128]{2,1,0:T(8,128)S(1)} %get-tuple-element.46), channel_id=1, source_target_pairs={{0,64},{1,17},{2,66},{3,19},{4,68},{5,21},{6,70},{7,23},{8,72},{9,... | collective-permute-start | bytes 491528 | tf_op jit(solution)/shard_map/ppermute | solution.py:42
  25.6 0.5 collective-permute-done.6
  26.2 2.7 %collective-permute-done.7 = f32[8,40,128]{2,1,0:T(8,128)S(1)} collective-permute-done((f32[8,40,128]{2,1,0:T(8,128)S(1)}, f32[8,40,128]{2,1,0:T(8,128)S(1)}, u32[]{:S(2)}, u32[]{:S(2)}) %collective-permute-start.7) | collective-permute-done | bytes 163872 | tf_op jit(solution)/shard_map/ppermute | solution.py:42
  28.9 1.7 %collective-permute-done.8 = f32[8,40,128]{2,1,0:T(8,128)S(1)} collective-permute-done((f32[8,40,128]{2,1,0:T(8,128)S(1)}, f32[8,40,128]{2,1,0:T(8,128)S(1)}, u32[]{:S(2)}, u32[]{:S(2)}) %collective-permute-start.8) | collective-permute-done | bytes 163872 | tf_op jit(solution)/shard_map/ppermute | solution.py:42
  30.6 6.2 %collective-permute-start.10 = (f32[8,5,128]{2,1,0:T(8,128)S(1)}, f32[8,5,128]{2,1,0:T(8,128)S(1)}, u32[]{:S(2)}, u32[]{:S(2)}) collective-permute-start(f32[8,5,128]{2,1,0:T(8,128)S(1)} %get-tuple-element.49), channel_id=1, source_target_pairs={{0,1},{1,0},{2,3},{3,2},{4,5},{5,4},{6,7},{7,6},{8,9},{9,8},{10,11... | collective-permute-start | bytes 61448 | tf_op jit(solution)/shard_map/ppermute | solution.py:147
  36.8 1.3 %collective-permute-start.9 = (f32[8,5,128]{2,1,0:T(8,128)S(1)}, f32[8,5,128]{2,1,0:T(8,128)S(1)}, u32[]{:S(2)}, u32[]{:S(2)}) collective-permute-start(f32[8,5,128]{2,1,0:T(8,128)S(1)} %get-tuple-element.50), channel_id=1, source_target_pairs={{0,7},{1,2},{2,1},{3,4},{4,3},{5,6},{6,5},{7,0},{8,15},{9,10},{10,... | collective-permute-start | bytes 61448 | tf_op jit(solution)/shard_map/ppermute | solution.py:42
  38.1 0.0 collective-permute-done.10
  38.1 2.1 %collective-permute-done.9 = f32[8,5,128]{2,1,0:T(8,128)S(1)} collective-permute-done((f32[8,5,128]{2,1,0:T(8,128)S(1)}, f32[8,5,128]{2,1,0:T(8,128)S(1)}, u32[]{:S(2)}, u32[]{:S(2)}) %collective-permute-start.9) | collective-permute-done | bytes 20512 | tf_op jit(solution)/shard_map/ppermute | solution.py:42
  40.3 0.1 collective-permute-start.11
  40.3 0.2 collective-permute-start.12
  40.6 3.5 %collective-permute-done.11.inner = f32[5,48,128]{2,1,0:T(8,128)S(1)} collective-permute-done((f32[5,48,128]{2,1,0:T(8,128)S(1)}, f32[5,48,128]{2,1,0:T(8,128)S(1)}, u32[]{:S(2)}, u32[]{:S(2)}) %collective-permute-start.11) | collective-permute-done | bytes 122912 | tf_op jit(solution)/shard_map/ppermute | solution.py:154
  44.1 3.4 %collective-permute-done.12.outer = f32[5,48,128]{2,1,0:T(8,128)S(1)} collective-permute-done((f32[5,48,128]{2,1,0:T(8,128)S(1)}, f32[5,48,128]{2,1,0:T(8,128)S(1)}, u32[]{:S(2)}, u32[]{:S(2)}) %collective-permute-start.12) | collective-permute-done | bytes 122912 | tf_op jit(solution)/shard_map/ppermute | solution.py:155
  47.5 1.4 %krylov.1 = (f32[8,40,128]{2,1,0:T(8,128)S(1)}, f32[8,40,128]{2,1,0:T(8,128)S(1)}, f32[128,128]{1,0:T(8,128)S(1)}) custom-call(f32[8,40,128]{2,1,0:T(8,128)S(1)} %fusion.2.own, f32[8,5,128]{2,1,0:T(8,128)S(1)} %get-tuple-element.52.left, f32[8,5,128]{2,1,0:T(8,128)S(1)} %get-tuple-element.51.right, f32[5,48,128]{2,1,0:T(8,128)S(1)} %collective-permute-done.11.inner, ...), custom_call_target="tpu_custom_call" | custom-call | tf_op jit(solution)/shard_map/krylov/pallas_call | solution.py:269
  48.9 15.5 %all_to_all.5 = f32[128,1,128]{2,1,0:T(1,128)S(1)} all-to-all(f32[128,1,128]{2,1,0:T(1,128)S(1)} %bitcast.32), channel_id=1, replica_groups=mesh['band_0'=4,'band_1'=4,'space_0'=4,'space_1'=2] {'band_0','band_1','..., dimensions={0} | all-to-all | bytes 131072 | tf_op jit(solution)/shard_map/all_to_all | solution.py:327
  64.4 0.9 %combine.1 = f32[8,40,128]{2,1,0:T(8,128)} custom-call(f32[128,128]{1,0:T(8,128)S(1)} %bitcast.31, f32[8,40,128]{2,1,0:T(8,128)S(1)} %fusion.2.own, f32[8,40,128]{2,1,0:T(8,128)S(1)} %get-tuple-element.43.first, f32[8,40,128]{2,1,0:T(8,128)S(1)} %get-tuple-element.44.second), custom_call_target="tpu_custom_call" | custom-call | tf_op jit(solution)/shard_map/combine/pallas_call | solution.py:313
  (15 shorter events, 0.3 us)
Async XLA Ops:
  0.0 0.7 %copy-start = (f32[8]{0:T(128)S(1)}, f32[8]{0:T(128)}, u32[]{:S(2)}) copy-start(f32[8]{0:T(128)} %occ.4) | copy-start | bytes 100
  2.6 8.9 %collective-permute-start = (f32[2,8,40,128]{3,2,1,0:T(8,128)S(1)}, f32[2,8,40,128]{3,2,1,0:T(8,128)S(1)}, u32[]{:S(2)}, u32[]{:S(2)}) collective-permute-start(f32[2,8,40,128]{3,2,1,0:T(8,128)S(1)} %bitcast.36), channel_id=1, source_target_pairs={{0,8},{1,33},{2,10},{3,35},{4,12},{5,37},{6,14},{7,39},{8,0},{9,41... | collective-permute-start | bytes 983048 | tf_op jit(solution)/shard_map/ppermute | solution.py:42
  5.1 7.4 %collective-permute-start.1 = (f32[2,8,40,128]{3,2,1,0:T(8,128)S(1)}, f32[2,8,40,128]{3,2,1,0:T(8,128)S(1)}, u32[]{:S(2)}, u32[]{:S(2)}) collective-permute-start(f32[2,8,40,128]{3,2,1,0:T(8,128)S(1)} %bitcast.35), channel_id=1, source_target_pairs={{0,24},{1,97},{2,26},{3,99},{4,28},{5,101},{6,30},{7,103},{8,16},{... | collective-permute-start | bytes 983048 | tf_op jit(solution)/shard_map/ppermute | solution.py:42
  10.1 6.8 %collective-permute-start.2 = (f32[2,8,40,128]{3,2,1,0:T(8,128)S(1)}, f32[2,8,40,128]{3,2,1,0:T(8,128)S(1)}, u32[]{:S(2)}, u32[]{:S(2)}) collective-permute-start(f32[2,8,40,128]{3,2,1,0:T(8,128)S(1)} %bitcast.34), channel_id=1, source_target_pairs={{0,8},{1,33},{2,10},{3,35},{4,12},{5,37},{6,14},{7,39},{8,0},{9,41... | collective-permute-start | bytes 983048 | tf_op jit(solution)/shard_map/ppermute | solution.py:42
  10.9 7.4 %collective-permute-start.4 = (f32[2,8,40,128]{3,2,1,0:T(8,128)S(1)}, f32[2,8,40,128]{3,2,1,0:T(8,128)S(1)}, u32[]{:S(2)}, u32[]{:S(2)}) collective-permute-start(f32[2,8,40,128]{3,2,1,0:T(8,128)S(1)} %bitcast.33), channel_id=1, source_target_pairs={{0,24},{1,97},{2,26},{3,99},{4,28},{5,101},{6,30},{7,103},{8,16},{... | collective-permute-start | bytes 983048 | tf_op jit(solution)/shard_map/ppermute | solution.py:42
  12.6 9.2 %collective-permute-start.3 = (f32[2,8,40,128]{3,2,1,0:T(8,128)S(1)}, f32[2,8,40,128]{3,2,1,0:T(8,128)S(1)}, u32[]{:S(2)}, u32[]{:S(2)}) collective-permute-start(f32[2,8,40,128]{3,2,1,0:T(8,128)S(1)} %add.35), channel_id=1, source_target_pairs={{0,24},{1,97},{2,26},{3,99},{4,28},{5,101},{6,30},{7,103},{8,16},{... | collective-permute-start | bytes 983048 | tf_op jit(solution)/shard_map/ppermute | solution.py:42
  14.9 6.9 %collective-permute-start.5 = (f32[2,8,40,128]{3,2,1,0:T(8,128)S(1)}, f32[2,8,40,128]{3,2,1,0:T(8,128)S(1)}, u32[]{:S(2)}, u32[]{:S(2)}) collective-permute-start(f32[2,8,40,128]{3,2,1,0:T(8,128)S(1)} %add.34), channel_id=1, source_target_pairs={{0,8},{1,33},{2,10},{3,35},{4,12},{5,37},{6,14},{7,39},{8,0},{9,41... | collective-permute-start | bytes 983048 | tf_op jit(solution)/shard_map/ppermute | solution.py:42
  21.9 4.2 %collective-permute-start.6 = (f32[8,40,128]{2,1,0:T(8,128)S(1)}, f32[8,40,128]{2,1,0:T(8,128)S(1)}, u32[]{:S(2)}, u32[]{:S(2)}) collective-permute-start(f32[8,40,128]{2,1,0:T(8,128)S(1)} %slice_bitcast_fusion.2), channel_id=1, source_target_pairs={{0,32},{1,9},{2,34},{3,11},{4,36},{5,13},{6,38},{7,15},{8,40},{9,1... | collective-permute-start | bytes 491528 | tf_op jit(solution)/shard_map/ppermute | solution.py:42
  23.0 5.9 %collective-permute-start.7 = (f32[8,40,128]{2,1,0:T(8,128)S(1)}, f32[8,40,128]{2,1,0:T(8,128)S(1)}, u32[]{:S(2)}, u32[]{:S(2)}) collective-permute-start(f32[8,40,128]{2,1,0:T(8,128)S(1)} %get-tuple-element.45), channel_id=1, source_target_pairs={{0,96},{1,25},{2,98},{3,27},{4,100},{5,29},{6,102},{7,31},{8,104},... | collective-permute-start | bytes 491528 | tf_op jit(solution)/shard_map/ppermute | solution.py:42
  24.9 5.7 %collective-permute-start.8 = (f32[8,40,128]{2,1,0:T(8,128)S(1)}, f32[8,40,128]{2,1,0:T(8,128)S(1)}, u32[]{:S(2)}, u32[]{:S(2)}) collective-permute-start(f32[8,40,128]{2,1,0:T(8,128)S(1)} %get-tuple-element.46), channel_id=1, source_target_pairs={{0,64},{1,17},{2,66},{3,19},{4,68},{5,21},{6,70},{7,23},{8,72},{9,... | collective-permute-start | bytes 491528 | tf_op jit(solution)/shard_map/ppermute | solution.py:42
  30.6 7.5 %collective-permute-start.10 = (f32[8,5,128]{2,1,0:T(8,128)S(1)}, f32[8,5,128]{2,1,0:T(8,128)S(1)}, u32[]{:S(2)}, u32[]{:S(2)}) collective-permute-start(f32[8,5,128]{2,1,0:T(8,128)S(1)} %get-tuple-element.49), channel_id=1, source_target_pairs={{0,1},{1,0},{2,3},{3,2},{4,5},{5,4},{6,7},{7,6},{8,9},{9,8},{10,11... | collective-permute-start | bytes 61448 | tf_op jit(solution)/shard_map/ppermute | solution.py:147
  36.8 3.3 %collective-permute-start.9 = (f32[8,5,128]{2,1,0:T(8,128)S(1)}, f32[8,5,128]{2,1,0:T(8,128)S(1)}, u32[]{:S(2)}, u32[]{:S(2)}) collective-permute-start(f32[8,5,128]{2,1,0:T(8,128)S(1)} %get-tuple-element.50), channel_id=1, source_target_pairs={{0,7},{1,2},{2,1},{3,4},{4,3},{5,6},{6,5},{7,0},{8,15},{9,10},{10,... | collective-permute-start | bytes 61448 | tf_op jit(solution)/shard_map/ppermute | solution.py:42
  40.3 3.8 %collective-permute-start.11 = (f32[5,48,128]{2,1,0:T(8,128)S(1)}, f32[5,48,128]{2,1,0:T(8,128)S(1)}, u32[]{:S(2)}, u32[]{:S(2)}) collective-permute-start(f32[5,48,128]{2,1,0:T(8,128)S(1)} %get-tuple-element.48), channel_id=1, source_target_pairs={{0,8},{8,0},{16,24},{24,16},{32,40},{40,32},{48,56},{56,48},{64,72... | collective-permute-start | bytes 368648 | tf_op jit(solution)/shard_map/ppermute | solution.py:154
  40.3 7.1 %collective-permute-start.12 = (f32[5,48,128]{2,1,0:T(8,128)S(1)}, f32[5,48,128]{2,1,0:T(8,128)S(1)}, u32[]{:S(2)}, u32[]{:S(2)}) collective-permute-start(f32[5,48,128]{2,1,0:T(8,128)S(1)} %get-tuple-element.47), channel_id=1, source_target_pairs={{0,120},{8,16},{16,8},{24,32},{32,24},{40,48},{48,40},{56,64},{64,... | collective-permute-start | bytes 368648 | tf_op jit(solution)/shard_map/ppermute | solution.py:155

commit v9 on v7

--- a/solution.py
+++ b/solution.py
@@ -109,7 +109,8 @@
     a_near, b_near = send(a2, partner(0, 1)), send(b2, partner(0, 3))
     a1, b1, a3, b3 = density_part(orbitals, occupations, scale, (1, 3))
     a_first, b_first = send(a1, partner(0, 1)), send(b3, partner(0, 3))
-    a_near, b_near = lax.optimization_barrier((a_near, b_near))
+    token = lax.ppermute(a1[1, :1, :8], "space_1", [(0, 1), (1, 0)])
+    a_near, b_near, token = lax.optimization_barrier((a_near, b_near, token))
     b1, a3 = b1 + b_near, a3 + a_near
     b1, a3, late = lax.optimization_barrier((b1, a3, occupations))
     b_last, a_last = send(b1, partner(0, 1)), send(a3, partner(0, 3))

time: 65.4 us -> 65.4 us (level)
  no operation moved by 1% of the time
where the time goes in v9:
time: 65.4 us; the launch traced here: 65.2 us
  starting transfers between devices  19.9 us (30%)
  waiting for transfers between devices  19.9 us (30%)
  blocking collectives  15.5 us (24%)
  Pallas kernels  8.78 us (13%)
  local copies, waits for them, and re-layouts  0.7 us (1%)
    all_to_all x1, blocking collectives, local(): lax.all_to_all(lines[:, None], EVERY, split_axis=0, concat_axis=0, tiled=...  15.5 us
    ppermute x10, starting transfers between devices, send(): return lax.ppermute(value, EVERY, pairs)  13.4 us
    ppermute x10, waiting for transfers between devices, send(): return lax.ppermute(value, EVERY, pairs)  13 us
    pallas_call x3, Pallas kernels, density_part(): pl.pallas_call(functools.partial(density_body, firsts, scale), out_shape=...  6.52 us
    ppermute x1, starting transfers between devices, halo(): lax.ppermute(jnp.where(first, right, left), 'space_1', [(0, 1), (1, 0)])  6.19 us
    ppermute x1, waiting for transfers between devices, halo(): inner = lax.ppermute(jnp.where(even, last_rows, first_rows), BAND, inner)  3.49 us
    ppermute x1, waiting for transfers between devices, halo(): outer = lax.ppermute(jnp.where(even, first_rows, last_rows), BAND, outer)  3.41 us
    pallas_call x1, Pallas kernels, krylov(): pl.pallas_call(krylov_body, out_shape=(field, field, jax.ShapeDtypeStruct...  1.39 us
  transfers between devices with their start and end apart: 13, of which 9 were waited for; matrix products, arithmetic and copies ran while one was open for 0% of the time, Pallas kernels for 7%

profile of v9, /device:TPU:1, one launch (start us, length us, event | category | flops | bytes accessed | tf_op | source)
XLA Modules:
  0.0 65.2 jit_solution(6443805266780668939)
XLA Ops:
  0.0 0.7 %copy-done = f32[8]{0:T(128)S(1)} copy-done((f32[8]{0:T(128)S(1)}, f32[8]{0:T(128)}, u32[]{:S(2)}) %copy-start) | copy-done | bytes 56
  0.7 1.9 %density.4 = (f32[2,320,128]{2,1,0:T(8,128)S(1)}, f32[2,320,128]{2,1,0:T(8,128)S(1)}) custom-call(bf16[8,5120,128]{2,1,0:T(8,128)(2,1)} %bitcast.37, f32[8]{0:T(128)S(1)} %copy-done), custom_call_target="tpu_custom_call" | custom-call | bytes 2621440 | tf_op jit(solution)/shard_map/density/pallas_call | solution.py:89
  2.6 2.5 %collective-permute-start = (f32[2,8,40,128]{3,2,1,0:T(8,128)S(1)}, f32[2,8,40,128]{3,2,1,0:T(8,128)S(1)}, u32[]{:S(2)}, u32[]{:S(2)}) collective-permute-start(f32[2,8,40,128]{3,2,1,0:T(8,128)S(1)} %bitcast.36), channel_id=1, source_target_pairs={{0,8},{1,33},{2,10},{3,35},{4,12},{5,37},{6,14},{7,39},{8,0},{9,41... | collective-permute-start | bytes 983048 | tf_op jit(solution)/shard_map/ppermute | solution.py:42
  5.1 2.2 %collective-permute-start.1 = (f32[2,8,40,128]{3,2,1,0:T(8,128)S(1)}, f32[2,8,40,128]{3,2,1,0:T(8,128)S(1)}, u32[]{:S(2)}, u32[]{:S(2)}) collective-permute-start(f32[2,8,40,128]{3,2,1,0:T(8,128)S(1)} %bitcast.35), channel_id=1, source_target_pairs={{0,24},{1,97},{2,26},{3,99},{4,28},{5,101},{6,30},{7,103},{8,16},{... | collective-permute-start | bytes 983048 | tf_op jit(solution)/shard_map/ppermute | solution.py:42
  7.4 2.7 %density.3 = (f32[2,320,128]{2,1,0:T(8,128)S(1)}, f32[2,320,128]{2,1,0:T(8,128)S(1)}, f32[2,320,128]{2,1,0:T(8,128)S(1)}, f32[2,320,128]{2,1,0:T(8,128)S(1)}) custom-call(bf16[8,5120,128]{2,1,0:T(8,128)(2,1)} %bitcast.38, f32[8]{0:T(128)S(1)} %copy-done), custom_call_target="tpu_custom_call" | custom-call | bytes 2621440 | tf_op jit(solution)/shard_map/density/pallas_call | solution.py:89
  10.1 0.8 %collective-permute-start.2 = (f32[2,8,40,128]{3,2,1,0:T(8,128)S(1)}, f32[2,8,40,128]{3,2,1,0:T(8,128)S(1)}, u32[]{:S(2)}, u32[]{:S(2)}) collective-permute-start(f32[2,8,40,128]{3,2,1,0:T(8,128)S(1)} %bitcast.34), channel_id=1, source_target_pairs={{0,8},{1,33},{2,10},{3,35},{4,12},{5,37},{6,14},{7,39},{8,0},{9,41... | collective-permute-start | bytes 983048 | tf_op jit(solution)/shard_map/ppermute | solution.py:42
  10.9 0.6 collective-permute-start.4
  11.5 0.0 collective-permute-done
  11.5 1.0 %collective-permute-done.1 = f32[2,8,40,128]{3,2,1,0:T(8,128)S(1)} collective-permute-done((f32[2,8,40,128]{3,2,1,0:T(8,128)S(1)}, f32[2,8,40,128]{3,2,1,0:T(8,128)S(1)}, u32[]{:S(2)}, u32[]{:S(2)}) %collective-permute-start.1) | collective-permute-done | bytes 327712 | tf_op jit(solution)/shard_map/ppermute | solution.py:42
  12.6 2.3 %collective-permute-start.3 = (f32[2,8,40,128]{3,2,1,0:T(8,128)S(1)}, f32[2,8,40,128]{3,2,1,0:T(8,128)S(1)}, u32[]{:S(2)}, u32[]{:S(2)}) collective-permute-start(f32[2,8,40,128]{3,2,1,0:T(8,128)S(1)} %add.35), channel_id=1, source_target_pairs={{0,24},{1,97},{2,26},{3,99},{4,28},{5,101},{6,30},{7,103},{8,16},{... | collective-permute-start | bytes 983048 | tf_op jit(solution)/shard_map/ppermute | solution.py:42
  14.9 0.0 collective-permute-start.5
  14.9 1.9 %density.5 = (f32[2,320,128]{2,1,0:T(8,128)S(1)}, f32[2,320,128]{2,1,0:T(8,128)S(1)}) custom-call(bf16[8,5120,128]{2,1,0:T(8,128)(2,1)} %bitcast.39, f32[8]{0:T(128)S(1)} %copy-done), custom_call_target="tpu_custom_call" | custom-call | bytes 2621440 | tf_op jit(solution)/shard_map/density/pallas_call | solution.py:89
  16.9 0.0 collective-permute-done.2
  16.9 1.5 %collective-permute-done.4 = f32[2,8,40,128]{3,2,1,0:T(8,128)S(1)} collective-permute-done((f32[2,8,40,128]{3,2,1,0:T(8,128)S(1)}, f32[2,8,40,128]{3,2,1,0:T(8,128)S(1)}, u32[]{:S(2)}, u32[]{:S(2)}) %collective-permute-start.4) | collective-permute-done | bytes 327712 | tf_op jit(solution)/shard_map/ppermute | solution.py:42
  18.3 3.5 %collective-permute-done.3 = f32[2,8,40,128]{3,2,1,0:T(8,128)S(1)} collective-permute-done((f32[2,8,40,128]{3,2,1,0:T(8,128)S(1)}, f32[2,8,40,128]{3,2,1,0:T(8,128)S(1)}, u32[]{:S(2)}, u32[]{:S(2)}) %collective-permute-start.3) | collective-permute-done | bytes 327712 | tf_op jit(solution)/shard_map/ppermute | solution.py:42
  21.8 0.0 collective-permute-done.5
  21.9 1.0 %collective-permute-start.6 = (f32[8,40,128]{2,1,0:T(8,128)S(1)}, f32[8,40,128]{2,1,0:T(8,128)S(1)}, u32[]{:S(2)}, u32[]{:S(2)}) collective-permute-start(f32[8,40,128]{2,1,0:T(8,128)S(1)} %slice_bitcast_fusion.2), channel_id=1, source_target_pairs={{0,32},{1,9},{2,34},{3,11},{4,36},{5,13},{6,38},{7,15},{8,40},{9,1... | collective-permute-start | bytes 491528 | tf_op jit(solution)/shard_map/ppermute | solution.py:42
  23.0 1.9 %collective-permute-start.7 = (f32[8,40,128]{2,1,0:T(8,128)S(1)}, f32[8,40,128]{2,1,0:T(8,128)S(1)}, u32[]{:S(2)}, u32[]{:S(2)}) collective-permute-start(f32[8,40,128]{2,1,0:T(8,128)S(1)} %get-tuple-element.45), channel_id=1, source_target_pairs={{0,96},{1,25},{2,98},{3,27},{4,100},{5,29},{6,102},{7,31},{8,104},... | collective-permute-start | bytes 491528 | tf_op jit(solution)/shard_map/ppermute | solution.py:42
  24.9 0.7 %collective-permute-start.8 = (f32[8,40,128]{2,1,0:T(8,128)S(1)}, f32[8,40,128]{2,1,0:T(8,128)S(1)}, u32[]{:S(2)}, u32[]{:S(2)}) collective-permute-start(f32[8,40,128]{2,1,0:T(8,128)S(1)} %get-tuple-element.46), channel_id=1, source_target_pairs={{0,64},{1,17},{2,66},{3,19},{4,68},{5,21},{6,70},{7,23},{8,72},{9,... | collective-permute-start | bytes 491528 | tf_op jit(solution)/shard_map/ppermute | solution.py:42
  25.6 0.5 collective-permute-done.6
  26.2 2.7 %collective-permute-done.7 = f32[8,40,128]{2,1,0:T(8,128)S(1)} collective-permute-done((f32[8,40,128]{2,1,0:T(8,128)S(1)}, f32[8,40,128]{2,1,0:T(8,128)S(1)}, u32[]{:S(2)}, u32[]{:S(2)}) %collective-permute-start.7) | collective-permute-done | bytes 163872 | tf_op jit(solution)/shard_map/ppermute | solution.py:42
  28.9 1.7 %collective-permute-done.8 = f32[8,40,128]{2,1,0:T(8,128)S(1)} collective-permute-done((f32[8,40,128]{2,1,0:T(8,128)S(1)}, f32[8,40,128]{2,1,0:T(8,128)S(1)}, u32[]{:S(2)}, u32[]{:S(2)}) %collective-permute-start.8) | collective-permute-done | bytes 163872 | tf_op jit(solution)/shard_map/ppermute | solution.py:42
  30.6 6.2 %collective-permute-start.10 = (f32[8,5,128]{2,1,0:T(8,128)S(1)}, f32[8,5,128]{2,1,0:T(8,128)S(1)}, u32[]{:S(2)}, u32[]{:S(2)}) collective-permute-start(f32[8,5,128]{2,1,0:T(8,128)S(1)} %get-tuple-element.50), channel_id=1, source_target_pairs={{0,1},{1,0},{2,3},{3,2},{4,5},{5,4},{6,7},{7,6},{8,9},{9,8},{10,11... | collective-permute-start | bytes 61448 | tf_op jit(solution)/shard_map/ppermute | solution.py:146
  36.8 1.3 %collective-permute-start.9 = (f32[8,5,128]{2,1,0:T(8,128)S(1)}, f32[8,5,128]{2,1,0:T(8,128)S(1)}, u32[]{:S(2)}, u32[]{:S(2)}) collective-permute-start(f32[8,5,128]{2,1,0:T(8,128)S(1)} %get-tuple-element.49), channel_id=1, source_target_pairs={{0,7},{1,2},{2,1},{3,4},{4,3},{5,6},{6,5},{7,0},{8,15},{9,10},{10,... | collective-permute-start | bytes 61448 | tf_op jit(solution)/shard_map/ppermute | solution.py:42
  38.1 2.1 %collective-permute-done.9 = f32[8,5,128]{2,1,0:T(8,128)S(1)} collective-permute-done((f32[8,5,128]{2,1,0:T(8,128)S(1)}, f32[8,5,128]{2,1,0:T(8,128)S(1)}, u32[]{:S(2)}, u32[]{:S(2)}) %collective-permute-start.9) | collective-permute-done | bytes 20512 | tf_op jit(solution)/shard_map/ppermute | solution.py:42
  40.3 0.1 collective-permute-start.11
  40.3 0.2 collective-permute-start.12
  40.6 3.5 %collective-permute-done.11.inner = f32[5,48,128]{2,1,0:T(8,128)S(1)} collective-permute-done((f32[5,48,128]{2,1,0:T(8,128)S(1)}, f32[5,48,128]{2,1,0:T(8,128)S(1)}, u32[]{:S(2)}, u32[]{:S(2)}) %collective-permute-start.11) | collective-permute-done | bytes 122912 | tf_op jit(solution)/shard_map/ppermute | solution.py:155
  44.1 3.4 %collective-permute-done.12.outer = f32[5,48,128]{2,1,0:T(8,128)S(1)} collective-permute-done((f32[5,48,128]{2,1,0:T(8,128)S(1)}, f32[5,48,128]{2,1,0:T(8,128)S(1)}, u32[]{:S(2)}, u32[]{:S(2)}) %collective-permute-start.12) | collective-permute-done | bytes 122912 | tf_op jit(solution)/shard_map/ppermute | solution.py:156
  47.5 1.4 %krylov.1 = (f32[8,40,128]{2,1,0:T(8,128)S(1)}, f32[8,40,128]{2,1,0:T(8,128)S(1)}, f32[128,128]{1,0:T(8,128)S(1)}) custom-call(f32[8,40,128]{2,1,0:T(8,128)S(1)} %fusion.2.own, f32[8,5,128]{2,1,0:T(8,128)S(1)} %get-tuple-element.52.left, f32[8,5,128]{2,1,0:T(8,128)S(1)} %get-tuple-element.51.right, f32[5,48,128]{2,1,0:T(8,128)S(1)} %collective-permute-done.11.inner, ...), custom_call_target="tpu_custom_call" | custom-call | tf_op jit(solution)/shard_map/krylov/pallas_call | solution.py:270
  48.9 15.5 %all_to_all.5 = f32[128,1,128]{2,1,0:T(1,128)S(1)} all-to-all(f32[128,1,128]{2,1,0:T(1,128)S(1)} %bitcast.32), channel_id=1, replica_groups=mesh['band_0'=4,'band_1'=4,'space_0'=4,'space_1'=2] {'band_0','band_1','..., dimensions={0} | all-to-all | bytes 131072 | tf_op jit(solution)/shard_map/all_to_all | solution.py:328
  64.4 0.9 %combine.1 = f32[8,40,128]{2,1,0:T(8,128)} custom-call(f32[128,128]{1,0:T(8,128)S(1)} %bitcast.31, f32[8,40,128]{2,1,0:T(8,128)S(1)} %fusion.2.own, f32[8,40,128]{2,1,0:T(8,128)S(1)} %get-tuple-element.43.first, f32[8,40,128]{2,1,0:T(8,128)S(1)} %get-tuple-element.44.second), custom_call_target="tpu_custom_call" | custom-call | tf_op jit(solution)/shard_map/combine/pallas_call | solution.py:314
  (15 shorter events, 0.3 us)
Async XLA Ops:
  0.0 0.7 %copy-start = (f32[8]{0:T(128)S(1)}, f32[8]{0:T(128)}, u32[]{:S(2)}) copy-start(f32[8]{0:T(128)} %occ.4) | copy-start | bytes 100
  2.6 8.9 %collective-permute-start = (f32[2,8,40,128]{3,2,1,0:T(8,128)S(1)}, f32[2,8,40,128]{3,2,1,0:T(8,128)S(1)}, u32[]{:S(2)}, u32[]{:S(2)}) collective-permute-start(f32[2,8,40,128]{3,2,1,0:T(8,128)S(1)} %bitcast.36), channel_id=1, source_target_pairs={{0,8},{1,33},{2,10},{3,35},{4,12},{5,37},{6,14},{7,39},{8,0},{9,41... | collective-permute-start | bytes 983048 | tf_op jit(solution)/shard_map/ppermute | solution.py:42
  5.1 7.4 %collective-permute-start.1 = (f32[2,8,40,128]{3,2,1,0:T(8,128)S(1)}, f32[2,8,40,128]{3,2,1,0:T(8,128)S(1)}, u32[]{:S(2)}, u32[]{:S(2)}) collective-permute-start(f32[2,8,40,128]{3,2,1,0:T(8,128)S(1)} %bitcast.35), channel_id=1, source_target_pairs={{0,24},{1,97},{2,26},{3,99},{4,28},{5,101},{6,30},{7,103},{8,16},{... | collective-permute-start | bytes 983048 | tf_op jit(solution)/shard_map/ppermute | solution.py:42
  10.1 6.8 %collective-permute-start.2 = (f32[2,8,40,128]{3,2,1,0:T(8,128)S(1)}, f32[2,8,40,128]{3,2,1,0:T(8,128)S(1)}, u32[]{:S(2)}, u32[]{:S(2)}) collective-permute-start(f32[2,8,40,128]{3,2,1,0:T(8,128)S(1)} %bitcast.34), channel_id=1, source_target_pairs={{0,8},{1,33},{2,10},{3,35},{4,12},{5,37},{6,14},{7,39},{8,0},{9,41... | collective-permute-start | bytes 983048 | tf_op jit(solution)/shard_map/ppermute | solution.py:42
  10.9 7.4 %collective-permute-start.4 = (f32[2,8,40,128]{3,2,1,0:T(8,128)S(1)}, f32[2,8,40,128]{3,2,1,0:T(8,128)S(1)}, u32[]{:S(2)}, u32[]{:S(2)}) collective-permute-start(f32[2,8,40,128]{3,2,1,0:T(8,128)S(1)} %bitcast.33), channel_id=1, source_target_pairs={{0,24},{1,97},{2,26},{3,99},{4,28},{5,101},{6,30},{7,103},{8,16},{... | collective-permute-start | bytes 983048 | tf_op jit(solution)/shard_map/ppermute | solution.py:42
  12.6 9.2 %collective-permute-start.3 = (f32[2,8,40,128]{3,2,1,0:T(8,128)S(1)}, f32[2,8,40,128]{3,2,1,0:T(8,128)S(1)}, u32[]{:S(2)}, u32[]{:S(2)}) collective-permute-start(f32[2,8,40,128]{3,2,1,0:T(8,128)S(1)} %add.35), channel_id=1, source_target_pairs={{0,24},{1,97},{2,26},{3,99},{4,28},{5,101},{6,30},{7,103},{8,16},{... | collective-permute-start | bytes 983048 | tf_op jit(solution)/shard_map/ppermute | solution.py:42
  14.9 6.9 %collective-permute-start.5 = (f32[2,8,40,128]{3,2,1,0:T(8,128)S(1)}, f32[2,8,40,128]{3,2,1,0:T(8,128)S(1)}, u32[]{:S(2)}, u32[]{:S(2)}) collective-permute-start(f32[2,8,40,128]{3,2,1,0:T(8,128)S(1)} %add.34), channel_id=1, source_target_pairs={{0,8},{1,33},{2,10},{3,35},{4,12},{5,37},{6,14},{7,39},{8,0},{9,41... | collective-permute-start | bytes 983048 | tf_op jit(solution)/shard_map/ppermute | solution.py:42
  21.9 4.2 %collective-permute-start.6 = (f32[8,40,128]{2,1,0:T(8,128)S(1)}, f32[8,40,128]{2,1,0:T(8,128)S(1)}, u32[]{:S(2)}, u32[]{:S(2)}) collective-permute-start(f32[8,40,128]{2,1,0:T(8,128)S(1)} %slice_bitcast_fusion.2), channel_id=1, source_target_pairs={{0,32},{1,9},{2,34},{3,11},{4,36},{5,13},{6,38},{7,15},{8,40},{9,1... | collective-permute-start | bytes 491528 | tf_op jit(solution)/shard_map/ppermute | solution.py:42
  23.0 5.9 %collective-permute-start.7 = (f32[8,40,128]{2,1,0:T(8,128)S(1)}, f32[8,40,128]{2,1,0:T(8,128)S(1)}, u32[]{:S(2)}, u32[]{:S(2)}) collective-permute-start(f32[8,40,128]{2,1,0:T(8,128)S(1)} %get-tuple-element.45), channel_id=1, source_target_pairs={{0,96},{1,25},{2,98},{3,27},{4,100},{5,29},{6,102},{7,31},{8,104},... | collective-permute-start | bytes 491528 | tf_op jit(solution)/shard_map/ppermute | solution.py:42
  24.9 5.7 %collective-permute-start.8 = (f32[8,40,128]{2,1,0:T(8,128)S(1)}, f32[8,40,128]{2,1,0:T(8,128)S(1)}, u32[]{:S(2)}, u32[]{:S(2)}) collective-permute-start(f32[8,40,128]{2,1,0:T(8,128)S(1)} %get-tuple-element.46), channel_id=1, source_target_pairs={{0,64},{1,17},{2,66},{3,19},{4,68},{5,21},{6,70},{7,23},{8,72},{9,... | collective-permute-start | bytes 491528 | tf_op jit(solution)/shard_map/ppermute | solution.py:42
  30.6 7.5 %collective-permute-start.10 = (f32[8,5,128]{2,1,0:T(8,128)S(1)}, f32[8,5,128]{2,1,0:T(8,128)S(1)}, u32[]{:S(2)}, u32[]{:S(2)}) collective-permute-start(f32[8,5,128]{2,1,0:T(8,128)S(1)} %get-tuple-element.50), channel_id=1, source_target_pairs={{0,1},{1,0},{2,3},{3,2},{4,5},{5,4},{6,7},{7,6},{8,9},{9,8},{10,11... | collective-permute-start | bytes 61448 | tf_op jit(solution)/shard_map/ppermute | solution.py:146
  36.8 3.3 %collective-permute-start.9 = (f32[8,5,128]{2,1,0:T(8,128)S(1)}, f32[8,5,128]{2,1,0:T(8,128)S(1)}, u32[]{:S(2)}, u32[]{:S(2)}) collective-permute-start(f32[8,5,128]{2,1,0:T(8,128)S(1)} %get-tuple-element.49), channel_id=1, source_target_pairs={{0,7},{1,2},{2,1},{3,4},{4,3},{5,6},{6,5},{7,0},{8,15},{9,10},{10,... | collective-permute-start | bytes 61448 | tf_op jit(solution)/shard_map/ppermute | solution.py:42
  40.3 3.8 %collective-permute-start.11 = (f32[5,48,128]{2,1,0:T(8,128)S(1)}, f32[5,48,128]{2,1,0:T(8,128)S(1)}, u32[]{:S(2)}, u32[]{:S(2)}) collective-permute-start(f32[5,48,128]{2,1,0:T(8,128)S(1)} %get-tuple-element.48), channel_id=1, source_target_pairs={{0,8},{8,0},{16,24},{24,16},{32,40},{40,32},{48,56},{56,48},{64,72... | collective-permute-start | bytes 368648 | tf_op jit(solution)/shard_map/ppermute | solution.py:155
  40.3 7.1 %collective-permute-start.12 = (f32[5,48,128]{2,1,0:T(8,128)S(1)}, f32[5,48,128]{2,1,0:T(8,128)S(1)}, u32[]{:S(2)}, u32[]{:S(2)}) collective-permute-start(f32[5,48,128]{2,1,0:T(8,128)S(1)} %get-tuple-element.47), channel_id=1, source_target_pairs={{0,120},{8,16},{16,8},{24,32},{32,24},{40,48},{48,40},{56,64},{64,... | collective-permute-start | bytes 368648 | tf_op jit(solution)/shard_map/ppermute | solution.py:156
